TPU v7x, 32 devices: a whole 2x2x4 slice. The times are simulated.
32 devices in a mesh: row: 2 (over y), col: 4 (over z), batch: 4 (over x, core).
Axes of the slice: x: 2, y: 2, z: 4, core: 2. Of those that a mesh axis runs over, the one named last changes fastest.
Arguments:
- features: bfloat16 [4096, 8192], P(('col', 'batch'), 'row'), may hold values from -6 to 6
- cross_weight: bfloat16 [8192, 8192], P('row', ('col', 'batch')), may hold values from -0.09375 to 0.09375
- cross_bias: float32 [8192], P('col'), may hold values from -3 to 3
- pattern: int32 [16, 16], replicated, may hold values from 0 to 1, as said below
- linear_weight: bfloat16 [8192, 8192], P('col', ('row', 'batch')), may hold values from -0.0625 to 0.0625
- linear_bias: float32 [8192], P('row'), may hold values from -3 to 3
Outputs:
- mixed_out: bfloat16 [4096, 8192], P(('col', 'batch'), 'row')
Inputs may be any that keep to these rules, and one draw needn't show every extreme that they name: `pattern`: entries are 0 or 1; exactly half of the 16 x 16 blocks are 1.
All inputs are finite; a program needn't handle non-finite values.
Results may differ from a plain program's by a relative error of at most 0.019.
Values may be sent and summed in bfloat16 or wider, within the bound.
No kernel may reach another device: no remote copies, remote signals or barrier semaphores. Data moves between devices by JAX's collectives and lax.ppermute only.
A program may use at most 128 MiB of HBM per device.

v0:
```python
import jax
import jax.numpy as jnp
from jax import lax
from jax.sharding import PartitionSpec as P

D = 8192
NB = 16


def on_device(features, cross_weight, cross_bias, pattern, linear_weight, linear_bias):
    cross_full, linear_full = (
        lax.all_gather(cross_weight, "batch", axis=1, tiled=True),
        lax.all_gather(linear_weight, "batch", axis=1, tiled=True),
    )
    samples = lax.all_gather(features, "col", axis=0, tiled=True)
    input_width = samples.shape[1]
    output_width = cross_full.shape[1]
    block_size = D // NB
    in_blocks = input_width // block_size
    out_blocks = output_width // block_size
    row_index = lax.axis_index("row")
    column_index = lax.axis_index("col")
    kept_blocks = lax.dynamic_slice(
        pattern, (column_index * out_blocks, row_index * in_blocks), (out_blocks, in_blocks)
    )
    block_mask = kept_blocks.T.astype(jnp.bfloat16)
    pruned = (
        cross_full.reshape(in_blocks, block_size, out_blocks, block_size)
        * block_mask[:, None, :, None]
    ).reshape(input_width, output_width)
    partial_sum = jnp.dot(samples, pruned, preferred_element_type=jnp.float32)
    first_feature = column_index * output_width - row_index * input_width
    is_owner = (first_feature >= 0) & (first_feature < input_width)
    safe_first = jnp.clip(first_feature, 0, input_width - output_width)
    own_piece = lax.dynamic_slice_in_dim(samples, safe_first, output_width, 1)
    carried_in = jnp.where(
        is_owner, own_piece.astype(jnp.float32), jnp.zeros_like(own_piece, dtype=jnp.float32)
    )
    hidden, base = (
        lax.psum_scatter(
            partial_sum.astype(jnp.bfloat16), "row", scatter_dimension=0, tiled=True
        ).astype(jnp.float32),
        lax.psum_scatter(
            carried_in.astype(jnp.bfloat16), "row", scatter_dimension=0, tiled=True
        ).astype(jnp.float32),
    )
    own_crossed = (base * (hidden + cross_bias) + base).astype(jnp.bfloat16)
    crossed = lax.all_gather(own_crossed, "row", axis=0, tiled=True)
    summed = lax.psum_scatter(
        jnp.dot(crossed, linear_full, preferred_element_type=jnp.float32).astype(jnp.bfloat16),
        "col",
        scatter_dimension=0,
        tiled=True,
    ).astype(jnp.float32)
    return (summed + linear_bias).astype(jnp.bfloat16)


def solution(mesh):
    return jax.shard_map(
        on_device,
        mesh=mesh,
        in_specs=(
            P(("col", "batch"), "row"),
            P("row", ("col", "batch")),
            P("col"),
            P(),
            P("col", ("row", "batch")),
            P("row"),
        ),
        out_specs=P(("col", "batch"), "row"),
        check_vma=False,
    )
```

profile of v0, /device:TPU:0, one launch (start us, length us, event | category | flops | bytes accessed | tf_op | source)
XLA Modules:
  0.0 723.6 jit_solution(14940952886365916482)
XLA Ops:
  6.5 0.7 all-gather.5.cloned.1.call-update
  7.3 0.7 all-gather.7.cloned.1.call-update
  8.0 0.0 reduce-scatter.4.cloned.1.call-start
  8.1 153.2 %all-gather.5.cloned.1.call-done = bf16[1024,4096]{1,0:T(8,128)(2,1)} async-done(((bf16[256,4096]{1,0:T(8,128)(2,1)}), bf16[1024,4096]{1,0:T(8,128)(2,1)}) %all-gather.5.cloned.1.call-update) | async-done | bytes 8388624 | tf_op jit(solution)/shard_map/all_gather | solution.py:15
  161.3 6.9 select_convert_fusion
  168.2 0.0 reduce-scatter.6.cloned.1.call-start
  168.3 0.8 fusion.5
  169.1 0.1 copy.7
  169.2 5.7 mul.30
  174.9 9.5 %copy.8 = bf16[512,8,4,512]{3,1,2,0:T(8,128)(2,1)} copy(bf16[512,8,4,512]{3,2,1,0:T(4,128)(2,1)S(1)} %bitcast.10) | data formatting | bytes 33554432
  184.4 82.6 %all-gather.7.cloned.1.call-done = bf16[4096,2048]{1,0:T(8,128)(2,1)} async-done(((bf16[4096,512]{1,0:T(8,128)(2,1)}), bf16[4096,2048]{1,0:T(8,128)(2,1)}) %all-gather.7.cloned.1.call-update) | async-done | bytes 16777232 | tf_op jit(solution)/shard_map/all_gather | solution.py:12
  267.0 24.9 %convert_bitcast_fusion = bf16[1024,2048]{1,0:T(8,128)(2,1)} fusion(bf16[1024,4096]{1,0:T(8,128)(2,1)} %all-gather.5.cloned.1.call-done, bf16[4096,2048]{1,0:T(8,128)(2,1)} %all-gather.7.cloned.1.call-done, bf16[4096,2048]{1,0:T(8,128)(2,1)} %bitcast.11), kind=kOutput, calls=%fused_computation.7 | convolution fusion | flops 17190354944 | bytes 46137344 | tf_op jit(solution)/shard_map/dot_general | solution.py:31
  292.0 0.0 all-gather.11.cloned.1.call-start
  292.0 0.5 all-gather.11.cloned.1.call-update
  292.6 0.0 all-gather.9.cloned.1.call-start
  292.6 31.1 %reduce-scatter.4.cloned.1.call-done = bf16[512,2048]{1,0:T(8,128)(2,1)} async-done(((bf16[1024,2048]{1,0:T(8,128)(2,1)}), bf16[512,2048]{1,0:T(8,128)(2,1)}) %reduce-scatter.4.cloned.1.call-update) | async-done | bytes 2097168 | tf_op jit(solution)/shard_map/reduce_scatter | solution.py:43
  323.7 56.6 %reduce-scatter.6.cloned.1.call-done = bf16[512,2048]{1,0:T(8,128)(2,1)} async-done(((bf16[1024,2048]{1,0:T(8,128)(2,1)}), bf16[512,2048]{1,0:T(8,128)(2,1)}) %reduce-scatter.6.cloned.1.call-update) | async-done | bytes 2097168 | tf_op jit(solution)/shard_map/reduce_scatter | solution.py:40
  380.3 4.6 fusion.2
  384.9 0.2 reduce-scatter.8.cloned.1.call-start
  385.1 102.5 %all-gather.11.cloned.1.call-done = bf16[2048,4096]{1,0:T(8,128)(2,1)} async-done(((bf16[2048,1024]{1,0:T(8,128)(2,1)}), bf16[2048,4096]{1,0:T(8,128)(2,1)}) %all-gather.11.cloned.1.call-update) | async-done | bytes 16777232 | tf_op jit(solution)/shard_map/all_gather | solution.py:13
  487.6 58.2 %all-gather.9.cloned.1.call-done = bf16[1024,2048]{1,0:T(8,128)(2,1)} async-done(((bf16[512,2048]{1,0:T(8,128)(2,1)}), bf16[1024,2048]{1,0:T(8,128)(2,1)}) %all-gather.9.cloned.1.call-update) | async-done | bytes 4194320 | tf_op jit(solution)/shard_map/all_gather | solution.py:48
  545.8 22.9 %convolution_convert_fusion = bf16[1024,4096]{1,0:T(8,128)(2,1)} fusion(bf16[1024,2048]{1,0:T(8,128)(2,1)} %all-gather.9.cloned.1.call-done, bf16[2048,4096]{1,0:T(8,128)(2,1)} %all-gather.11.cloned.1.call-done), kind=kOutput, calls=%fused_computation.3 | convolution fusion | flops 17184063488 | bytes 29360128 | tf_op jit(solution)/shard_map/dot_general | solution.py:50
  568.7 144.6 %reduce-scatter.8.cloned.1.call-done = bf16[256,4096]{1,0:T(8,128)(2,1)} async-done(((bf16[1024,4096]{1,0:T(8,128)(2,1)}), bf16[256,4096]{1,0:T(8,128)(2,1)}) %reduce-scatter.8.cloned.1.call-update) | async-done | bytes 2097168 | tf_op jit(solution)/shard_map/reduce_scatter | solution.py:49
  713.3 3.4 add_convert_fusion
  (10 shorter events, 0.1 us)
Async XLA Ops:
  6.5 154.8 %all-gather.5.cloned.1.call-start = ((), (), s32[]{:S(2)}) async-start(), calls=%async_computation.3 | async-start | bytes 10485760 | tf_op jit(solution)/shard_map/all_gather | solution.py:15
  7.3 259.8 %all-gather.7.cloned.1.call-start = ((), (), s32[]{:S(2)}) async-start(), calls=%async_computation.5 | async-start | bytes 20971520 | tf_op jit(solution)/shard_map/all_gather | solution.py:12
  8.0 315.7 %reduce-scatter.4.cloned.1.call-start = ((), (), s32[]{:S(2)}) async-start(), calls=%async_computation.4 | async-start | bytes 6291456 | tf_op jit(solution)/shard_map/reduce_scatter | solution.py:43
  168.2 212.0 %reduce-scatter.6.cloned.1.call-start = ((), (), s32[]{:S(2)}) async-start(), calls=%async_computation.6 | async-start | bytes 6291456 | tf_op jit(solution)/shard_map/reduce_scatter | solution.py:40
  292.0 88.3 %copy-start.1 = (f32[2048]{0:T(1024)S(1)}, f32[2048]{0:T(1024)}, u32[]{:S(2)}) copy-start(f32[2048]{0:T(1024)} %param.8) | copy-start | bytes 24580
  292.0 195.7 %all-gather.11.cloned.1.call-start = ((), (), s32[]{:S(2)}) async-start(), calls=%async_computation.8 | async-start | bytes 20971520 | tf_op jit(solution)/shard_map/all_gather | solution.py:13
  292.6 253.3 %all-gather.9.cloned.1.call-start = ((), (), s32[]{:S(2)}) async-start(), calls=%async_computation.7 | async-start | bytes 6291456 | tf_op jit(solution)/shard_map/all_gather | solution.py:48
  384.9 328.5 %reduce-scatter.8.cloned.1.call-start = ((), (), s32[]{:S(2)}) async-start(), calls=%async_computation.9 | async-start | bytes 10485760 | tf_op jit(solution)/shard_map/reduce_scatter | solution.py:49
  568.7 144.7 %copy-start = (f32[4096]{0:T(1024)S(1)}, f32[4096]{0:T(1024)}, u32[]{:S(2)}) copy-start(f32[4096]{0:T(1024)} %param.11) | copy-start | bytes 49156
Sparse Core Ops, SparseCore 0:
  8.9 152.3 all-gather.4
  162.9 104.1 all-gather.6
  269.3 54.3 reduce-scatter.3
  325.9 54.2 reduce-scatter.5
  381.7 105.9 all-gather.10
  489.0 56.7 all-gather.8
  568.8 144.4 reduce-scatter.7
where the time goes:
time: 724 us
  waiting for transfers between devices  631 us (87%)
  matrix products  47.8 us (7%)
  other arithmetic  15.7 us (2%)
  local copies, waits for them, and re-layouts  15.3 us (2%)
  between operations  13.5 us (2%)
    all_gather x1, waiting for transfers between devices, on_device(): samples = lax.all_gather(features, 'col', axis=0, tiled=True)  153 us
    reduce_scatter x1, waiting for transfers between devices, on_device(): lax.psum_scatter(jnp.dot(crossed, linear_full, preferred_element_type=jnp...  145 us
    all_gather x1, waiting for transfers between devices, on_device(): lax.all_gather(linear_weight, 'batch', axis=1, tiled=True)  103 us
    all_gather x1, waiting for transfers between devices, on_device(): lax.all_gather(cross_weight, 'batch', axis=1, tiled=True)  82.6 us
    all_gather x1, waiting for transfers between devices, on_device(): crossed = lax.all_gather(own_crossed, 'row', axis=0, tiled=True)  58.2 us
    reduce_scatter x1, waiting for transfers between devices, on_device(): lax.psum_scatter(partial_sum.astype(jnp.bfloat16), 'row', scatter_dimensi...  56.6 us
    reduce_scatter x1, waiting for transfers between devices, on_device(): lax.psum_scatter(carried_in.astype(jnp.bfloat16), 'row', scatter_dimensio...  31.1 us
    dot_general x1, matrix products, on_device(): partial_sum = jnp.dot(samples, pruned, preferred_element_type=jnp.float32)  24.9 us
  transfers between devices with their start and end apart: 7, of which 7 were waited for; matrix products, arithmetic and copies ran while one was open for 7% of the time, Pallas kernels for 0%

commit v1 on v0

v1 whole, which is shorter than its diff:
```python
import jax
import jax.numpy as jnp
from jax import lax
from jax.sharding import PartitionSpec as P

CHUNKS = 2


def axis_pairs(size, bit):
    return [(place, place ^ bit) for place in range(size)]


def gather_pieces(shard, size):
    pieces = {0: shard}
    bit = size // 2
    while bit:
        for apart in list(pieces):
            pieces[apart | bit] = lax.ppermute(pieces[apart], "batch", axis_pairs(size, bit))
        bit //= 2
    return pieces


def build(mesh):
    n_row, n_col, n_batch = (mesh.shape[name] for name in ("row", "col", "batch"))

    def on_device(features, cross_weight, cross_bias, pattern, linear_weight, linear_bias):
        grid_side = pattern.shape[0]
        input_width = cross_weight.shape[0]
        width = input_width * n_row
        piece_width = cross_weight.shape[1]
        output_width = piece_width * n_batch
        mixed_width = linear_weight.shape[1]
        block_size = width // grid_side
        row, col, batch = (lax.axis_index(name) for name in ("row", "col", "batch"))

        out_of = (col * n_batch + batch) * piece_width + jnp.arange(piece_width)
        in_of = row * input_width + jnp.arange(input_width)
        kept_columns = jnp.take(pattern, out_of // block_size, axis=0)
        kept = jnp.take(kept_columns, in_of // block_size, axis=1).T
        pruned = cross_weight * kept.astype(cross_weight.dtype)

        cross_pieces = gather_pieces(pruned, n_batch)
        linear_shard, cross_pieces[n_batch // 2] = lax.optimization_barrier(
            (linear_weight, cross_pieces[n_batch // 2])
        )
        linear_pieces = {}
        near = range(n_batch // 2)
        far = range(n_batch // 2, n_batch)
        linear_pieces = gather_pieces(linear_shard, n_batch)
        linear_groups = [
            (group, jnp.concatenate([linear_pieces[apart] for apart in group], axis=1))
            for group in (near, far)
        ]

        rows_per = features.shape[0] // CHUNKS
        gathered = [
            lax.all_gather(
                features[step * rows_per : (step + 1) * rows_per], "col", axis=0, tiled=True
            )
            for step in range(CHUNKS)
        ]

        def owner_of(column):
            return column * output_width // input_width

        is_owner = row == col * output_width // input_width
        turns = []
        for turn in range(1, n_row):
            turns.append(
                [
                    (((owner_of(c) + turn) % n_row) * n_col + c, owner_of(c) * n_col + c)
                    for c in range(n_col)
                ]
            )
        first_base = jnp.where(is_owner, col * output_width - row * input_width, 0)

        crossed = []
        for samples in gathered:
            whole = jnp.zeros((samples.shape[0], output_width), jnp.bfloat16)
            for apart in range(n_batch):
                first = (batch ^ apart) * piece_width
                own = jnp.dot(samples, cross_pieces[apart], preferred_element_type=jnp.float32)
                own = own.astype(jnp.bfloat16)
                hidden = own.astype(jnp.float32)
                for pairs in turns:
                    hidden = hidden + lax.ppermute(own, ("row", "col"), pairs).astype(jnp.float32)
                base = lax.dynamic_slice_in_dim(
                    samples, first_base + first, piece_width, 1
                ).astype(jnp.float32)
                bias = lax.dynamic_slice_in_dim(cross_bias, first, piece_width)
                mine = (base * (hidden + bias) + base).astype(jnp.bfloat16)
                theirs = jnp.zeros_like(mine)
                for pairs in turns:
                    theirs = theirs + lax.ppermute(
                        mine, ("row", "col"), [(to, came) for came, to in pairs]
                    )
                whole = lax.dynamic_update_slice_in_dim(
                    whole, jnp.where(is_owner, mine, theirs), first, 1
                )
            crossed.append(whole)

        out = jnp.zeros((features.shape[0], mixed_width * n_batch), jnp.bfloat16)
        for group, weight in linear_groups:
            for step, whole in enumerate(crossed):
                partial = jnp.dot(whole, weight, preferred_element_type=jnp.float32)
                summed = lax.psum_scatter(
                    partial.astype(jnp.bfloat16), "col", scatter_dimension=0, tiled=True
                ).astype(jnp.float32)
                for place, apart in enumerate(group):
                    first = (batch ^ apart) * mixed_width
                    bias = lax.dynamic_slice_in_dim(linear_bias, first, mixed_width)
                    part = summed[:, place * mixed_width : (place + 1) * mixed_width] + bias
                    out = lax.dynamic_update_slice(
                        out, part.astype(jnp.bfloat16), (step * rows_per, first)
                    )
        return out

    return on_device


def solution(mesh):
    return jax.shard_map(
        build(mesh),
        mesh=mesh,
        in_specs=(
            P(("col", "batch"), "row"),
            P("row", ("col", "batch")),
            P("col"),
            P(),
            P("col", ("row", "batch")),
            P("row"),
        ),
        out_specs=P(("col", "batch"), "row"),
        check_vma=False,
    )
```

time: 724 us -> 471 us (0.65)
  waiting for transfers between devices: 631 us -> 291 us
  starting transfers between devices: 0.42 us -> 37 us
  local copies, waits for them, and re-layouts: 15.3 us -> 41.6 us
  matrix products: 47.8 us -> 69.6 us
    all_gather x4 -> x2, waiting for transfers between devices: 397 us -> 19.4 us  [on_device(): lax.all_gather(features[step * rows_per:(step + 1) * rows_per], 'col', ax...]
    ppermute x0 -> x22, waiting for transfers between devices: none -> 165 us  [the longest x6 93 us: gather_pieces(): lax.ppermute(pieces[apart], 'batch', axis_pairs(size, bit))]
    reduce_scatter x3 -> x4, waiting for transfers between devices: 232 us -> 106 us  [on_device(): lax.psum_scatter(partial.astype(jnp.bfloat16), 'col', scatter_dimension=0...]
    ppermute x0 -> x22, starting transfers between devices: none -> 36.7 us  [the longest x8 21.1 us: on_device(): lax.ppermute(mine, ('row', 'col'), [(to, came) for came, to in pairs])]
    dot_general x2 -> x12, matrix products: 47.8 us -> 69.6 us  [the longest x8 42 us: on_device(): jnp.dot(samples, cross_pieces[apart], preferred_element_type=jnp.float32)]
    gather x0 -> x2, local copies, waits for them, and re-layouts: none -> 17.9 us  [the longest x1 16.8 us: on_device(): kept = jnp.take(kept_columns, in_of // block_size, axis=1).T]
    convert_element_type x4 -> x6, other arithmetic: 15.7 us -> 8.09 us  [the longest x4 4.54 us: on_device(): summed = lax.psum_scatter(partial.astype(jnp.bfloat16), 'col', scatter_di...]
    unnamed x5 -> x42, local copies, waits for them, and re-layouts: 9.55 us -> 16.1 us
  transfers between devices with their start and end apart: 7 -> 28, of which waited for: 7 -> 16; matrix products, arithmetic and copies ran while one was open for 7% -> 25% of each run, Pallas kernels for 0% -> 0%
where the time goes in v1:
time: 471 us; the launch traced here: 470 us
  waiting for transfers between devices  291 us (62%)
  matrix products  69.6 us (15%)
  local copies, waits for them, and re-layouts  41.6 us (9%)
  starting transfers between devices  37 us (8%)
  other arithmetic  17.4 us (4%)
  between operations  14.2 us (3%)
    reduce_scatter x4, waiting for transfers between devices, on_device(): lax.psum_scatter(partial.astype(jnp.bfloat16), 'col', scatter_dimension=0...  106 us
    ppermute x6, waiting for transfers between devices, gather_pieces(): lax.ppermute(pieces[apart], 'batch', axis_pairs(size, bit))  93 us
    ppermute x8, waiting for transfers between devices, on_device(): lax.ppermute(mine, ('row', 'col'), [(to, came) for came, to in pairs])  53.7 us
    dot_general x8, matrix products, on_device(): jnp.dot(samples, cross_pieces[apart], preferred_element_type=jnp.float32)  42 us
    dot_general x4, matrix products, on_device(): partial = jnp.dot(whole, weight, preferred_element_type=jnp.float32)  27.5 us
    ppermute x8, starting transfers between devices, on_device(): lax.ppermute(mine, ('row', 'col'), [(to, came) for came, to in pairs])  21.1 us
    all_gather x2, waiting for transfers between devices, on_device(): lax.all_gather(features[step * rows_per:(step + 1) * rows_per], 'col', ax...  19.4 us
    ppermute x8, waiting for transfers between devices, on_device(): lax.ppermute(own, ('row', 'col'), pairs).astype(jnp.float32)  18.4 us
  transfers between devices with their start and end apart: 28, of which 16 were waited for; matrix products, arithmetic and copies ran while one was open for 25% of the time, Pallas kernels for 0%

profile of v1, /device:TPU:0, one launch (start us, length us, event | category | flops | bytes accessed | tf_op | source)
XLA Modules:
  0.0 470.5 jit_solution(6166128900949458396)
XLA Ops:
  11.1 16.8 %gather_fusion.1 = s32[4096,512]{1,0:T(8,128)} fusion(s32[512,16]{0,1:T(8,128)S(1)} %copy.11, s32[4096]{0:T(1024)S(1)} %broadcast_clamp_fusion), kind=kCustom, calls=%fused_computation.1 | custom fusion | bytes 16793600 | tf_op jit(solution)/shard_map/jit(_take)/gather | solution.py:39
  28.0 6.9 %fusion = bf16[4096,512]{1,0:T(8,128)(2,1)} fusion(bf16[4096,512]{1,0:T(8,128)(2,1)} %param.7, s32[4096,512]{1,0:T(8,128)} %gather_fusion.1, pred[4096]{0:T(1024)(128)(4,1)S(1)} %compare_and_fusion), kind=kLoop, calls=%fused_computation.3 | loop fusion | flops 6291456 | bytes 16781312 | tf_op jit(solution)/shard_map/mul | solution.py:40
  39.3 89.4 %collective-permute-done.5 = bf16[4096,512]{1,0:T(8,128)(2,1)} collective-permute-done((bf16[4096,512]{1,0:T(8,128)(2,1)}, bf16[4096,512]{1,0:T(8,128)(2,1)}, u32[]{:S(2)}, u32[]{:S(2)}) %collective-permute-start.5) | collective-permute-done | bytes 4194336 | tf_op jit(solution)/shard_map/ppermute | solution.py:18
  134.1 5.9 %fusion.7 = bf16[512,512]{0,1:T(8,128)(2,1)S(1)} fusion(bf16[4096,512]{1,0:T(8,128)(2,1)} %collective-permute-done.5, bf16[512,4096]{0,1:T(8,128)(2,1)} %all-gather.5.cloned.1.call-done), kind=kOutput, calls=%fused_computation.30 | convolution fusion | flops 2147745792 | bytes 8912896 | tf_op jit(solution)/shard_map/dot_general | solution.py:82
  147.3 5.3 %fusion.5 = bf16[512,512]{0,1:T(8,128)(2,1)} fusion(bf16[4096,512]{1,0:T(8,128)(2,1)} %fusion, bf16[512,4096]{0,1:T(8,128)(2,1)S(1)} %copy-done.8), kind=kOutput, calls=%fused_computation.28 | convolution fusion | flops 2147745792 | bytes 8912896 | tf_op jit(solution)/shard_map/dot_general | solution.py:82
  153.9 19.4 %all-gather.3.cloned.1.call-done = bf16[512,4096]{0,1:T(8,128)(2,1)} async-done(((bf16[128,4096]{0,1:T(8,128)(2,1)}), bf16[512,4096]{0,1:T(8,128)(2,1)}) %all-gather.3.cloned.1.call-update) | async-done | bytes 4194320 | tf_op jit(solution)/shard_map/all_gather | solution.py:57
  173.3 5.9 %fusion.3 = bf16[512,512]{0,1:T(8,128)(2,1)S(1)} fusion(bf16[4096,512]{1,0:T(8,128)(2,1)} %collective-permute-done.5, bf16[512,4096]{0,1:T(8,128)(2,1)} %all-gather.3.cloned.1.call-done), kind=kOutput, calls=%fused_computation.26 | convolution fusion | flops 2147745792 | bytes 8912896 | tf_op jit(solution)/shard_map/dot_general | solution.py:82
  194.3 6.5 %collective-permute-done.18 = bf16[512,512]{0,1:T(8,128)(2,1)S(1)} collective-permute-done((bf16[512,512]{0,1:T(8,128)(2,1)S(1)}, bf16[512,512]{0,1:T(8,128)(2,1)S(1)}, u32[]{:S(2)}, u32[]{:S(2)}) %collective-permute-start.18) | collective-permute-done | bytes 524320 | tf_op jit(solution)/shard_map/ppermute | solution.py:86
  205.2 5.1 %fusion.1 = bf16[512,512]{0,1:T(8,128)(2,1)S(1)} fusion(bf16[4096,512]{1,0:T(8,128)(2,1)} %fusion, bf16[512,4096]{0,1:T(8,128)(2,1)S(1)} %copy-done.6), kind=kOutput, calls=%fused_computation.24 | convolution fusion | flops 2147745792 | bytes 8912896 | tf_op jit(solution)/shard_map/dot_general | solution.py:82
  222.3 6.5 %collective-permute-done.15 = bf16[512,512]{0,1:T(8,128)(2,1)S(1)} collective-permute-done((bf16[512,512]{0,1:T(8,128)(2,1)S(1)}, bf16[512,512]{0,1:T(8,128)(2,1)S(1)}, u32[]{:S(2)}, u32[]{:S(2)}) %collective-permute-start.15) | collective-permute-done | bytes 524320 | tf_op jit(solution)/shard_map/ppermute | solution.py:94
  233.3 6.7 %collective-permute-done.17 = bf16[512,512]{0,1:T(8,128)(2,1)S(1)} collective-permute-done((bf16[512,512]{0,1:T(8,128)(2,1)S(1)}, bf16[512,512]{0,1:T(8,128)(2,1)S(1)}, u32[]{:S(2)}, u32[]{:S(2)}) %collective-permute-start.17) | collective-permute-done | bytes 524320 | tf_op jit(solution)/shard_map/ppermute | solution.py:94
  241.5 7.0 %collective-permute-done.19 = bf16[512,512]{0,1:T(8,128)(2,1)S(1)} collective-permute-done((bf16[512,512]{0,1:T(8,128)(2,1)S(1)}, bf16[512,512]{0,1:T(8,128)(2,1)S(1)}, u32[]{:S(2)}, u32[]{:S(2)}) %collective-permute-start.19) | collective-permute-done | bytes 524320 | tf_op jit(solution)/shard_map/ppermute | solution.py:94
  249.9 5.9 %convolution_convert_fusion.2 = bf16[512,2048]{1,0:T(8,128)(2,1)} fusion(bf16[512,2048]{0,1:T(8,128)(2,1)S(1)} %select_dynamic-update-slice_fusion, bf16[2048,2048]{1,0:T(8,128)(2,1)S(1)} %constant_dynamic-update-slice_fusion), kind=kOutput, calls=%fused_computation.6 | convolution fusion | flops 4296015872 | bytes 12582912 | tf_op jit(solution)/shard_map/dot_general | solution.py:105
  255.9 5.9 %fusion.4 = bf16[512,512]{0,1:T(8,128)(2,1)S(1)} fusion(bf16[4096,512]{1,0:T(8,128)(2,1)} %collective-permute-done.8, bf16[512,4096]{0,1:T(8,128)(2,1)} %all-gather.3.cloned.1.call-done), kind=kOutput, calls=%fused_computation.27 | convolution fusion | flops 2147745792 | bytes 8912896 | tf_op jit(solution)/shard_map/dot_general | solution.py:82
  263.2 11.9 %collective-permute-done.9 = bf16[512,512]{0,1:T(8,128)(2,1)S(1)} collective-permute-done((bf16[512,512]{0,1:T(8,128)(2,1)S(1)}, bf16[512,512]{0,1:T(8,128)(2,1)S(1)}, u32[]{:S(2)}, u32[]{:S(2)}) %collective-permute-start.9) | collective-permute-done | bytes 524320 | tf_op jit(solution)/shard_map/ppermute | solution.py:86
  290.7 10.9 %collective-permute-done.4 = bf16[512,512]{0,1:T(8,128)(2,1)S(1)} collective-permute-done((bf16[512,512]{0,1:T(8,128)(2,1)S(1)}, bf16[512,512]{0,1:T(8,128)(2,1)S(1)}, u32[]{:S(2)}, u32[]{:S(2)}) %collective-permute-start.4) | collective-permute-done | bytes 524320 | tf_op jit(solution)/shard_map/ppermute | solution.py:94
  301.8 11.1 %collective-permute-done.7 = bf16[512,512]{0,1:T(8,128)(2,1)S(1)} collective-permute-done((bf16[512,512]{0,1:T(8,128)(2,1)S(1)}, bf16[512,512]{0,1:T(8,128)(2,1)S(1)}, u32[]{:S(2)}, u32[]{:S(2)}) %collective-permute-start.7) | collective-permute-done | bytes 524320 | tf_op jit(solution)/shard_map/ppermute | solution.py:94
  313.0 6.7 %collective-permute-done.10 = bf16[512,512]{0,1:T(8,128)(2,1)S(1)} collective-permute-done((bf16[512,512]{0,1:T(8,128)(2,1)S(1)}, bf16[512,512]{0,1:T(8,128)(2,1)S(1)}, u32[]{:S(2)}, u32[]{:S(2)}) %collective-permute-start.10) | collective-permute-done | bytes 524320 | tf_op jit(solution)/shard_map/ppermute | solution.py:94
  319.9 5.9 %convolution_convert_fusion.3 = bf16[512,2048]{1,0:T(8,128)(2,1)} fusion(bf16[512,2048]{0,1:T(8,128)(2,1)S(1)} %select_dynamic-update-slice_fusion.4, bf16[2048,2048]{1,0:T(8,128)(2,1)S(1)} %bitcast.45), kind=kOutput, calls=%fused_computation.7 | convolution fusion | flops 4296015872 | bytes 12582912 | tf_op jit(solution)/shard_map/dot_general | solution.py:105
  334.4 5.7 %convolution_convert_fusion.1 = bf16[512,2048]{1,0:T(8,128)(2,1)} fusion(bf16[512,2048]{0,1:T(8,128)(2,1)S(1)} %select_dynamic-update-slice_fusion.4, bf16[2048,2048]{1,0:T(8,128)(2,1)S(1)} %constant_dynamic-update-slice_fusion.2), kind=kOutput, calls=%fused_computation.5 | convolution fusion | flops 4296015872 | bytes 12582912 | tf_op jit(solution)/shard_map/dot_general | solution.py:105
  340.3 10.1 %convolution_convert_fusion = bf16[512,2048]{1,0:T(8,128)(2,1)} fusion(bf16[512,2048]{0,1:T(8,128)(2,1)} %copy-done.2, bf16[2048,2048]{1,0:T(8,128)(2,1)} %copy-done.5), kind=kOutput, calls=%fused_computation.4 | convolution fusion | flops 4296015872 | bytes 12582912 | tf_op jit(solution)/shard_map/dot_general | solution.py:105
  351.6 18.0 %reduce-scatter.5.cloned.1.call-done = bf16[128,2048]{1,0:T(8,128)(2,1)} async-done(((bf16[512,2048]{1,0:T(8,128)(2,1)}), bf16[128,2048]{1,0:T(8,128)(2,1)}) %reduce-scatter.5.cloned.1.call-update) | async-done | bytes 524304 | tf_op jit(solution)/shard_map/reduce_scatter | solution.py:106
  371.1 43.8 %reduce-scatter.9.cloned.1.call-done = bf16[128,2048]{1,0:T(8,128)(2,1)} async-done(((bf16[512,2048]{1,0:T(8,128)(2,1)}), bf16[128,2048]{1,0:T(8,128)(2,1)}) %reduce-scatter.9.cloned.1.call-update) | async-done | bytes 524304 | tf_op jit(solution)/shard_map/reduce_scatter | solution.py:106
  416.2 44.2 %reduce-scatter.11.cloned.1.call-done = bf16[128,2048]{1,0:T(8,128)(2,1)} async-done(((bf16[512,2048]{1,0:T(8,128)(2,1)}), bf16[128,2048]{1,0:T(8,128)(2,1)}) %reduce-scatter.11.cloned.1.call-update) | async-done | bytes 524304 | tf_op jit(solution)/shard_map/reduce_scatter | solution.py:106
  (135 shorter events, 94.5 us)
Async XLA Ops:
  6.5 127.6 %all-gather.5.cloned.1.call-start = ((), (), s32[]{:S(2)}) async-start(), calls=%async_computation.6 | async-start | bytes 5242880 | tf_op jit(solution)/shard_map/all_gather | solution.py:57
  9.6 163.8 %all-gather.3.cloned.1.call-start = ((), (), s32[]{:S(2)}) async-start(), calls=%async_computation.4 | async-start | bytes 5242880 | tf_op jit(solution)/shard_map/all_gather | solution.py:57
  34.9 93.8 %collective-permute-start.5 = (bf16[4096,512]{1,0:T(8,128)(2,1)}, bf16[4096,512]{1,0:T(8,128)(2,1)}, u32[]{:S(2)}, u32[]{:S(2)}) collective-permute-start(bf16[4096,512]{1,0:T(8,128)(2,1)} %fusion), channel_id=1, source_target_pairs={{0,2},{1,3},{2,0},{3,1},{4,6},{5,7},{6,4},{7,5},{8,10},{9,11},{10,... | collective-permute-start | bytes 12582920 | tf_op jit(solution)/shard_map/ppermute | solution.py:18
  39.1 311.3 %reduce-scatter.7.cloned.1.call-start = ((), (), s32[]{:S(2)}) async-start(), calls=%async_computation.7 | async-start | bytes 2621440 | tf_op jit(solution)/shard_map/reduce_scatter | solution.py:106
  39.2 102.2 %collective-permute-start.2 = (bf16[4096,512]{1,0:T(8,128)(2,1)}, bf16[4096,512]{1,0:T(8,128)(2,1)}, u32[]{:S(2)}, u32[]{:S(2)}) collective-permute-start(bf16[4096,512]{1,0:T(8,128)(2,1)} %fusion), channel_id=1, source_target_pairs={{0,1},{1,0},{2,3},{3,2},{4,5},{5,4},{6,7},{7,6},{8,9},{9,8},{10,11... | collective-permute-start | bytes 12582920 | tf_op jit(solution)/shard_map/ppermute | solution.py:18
  128.7 50.6 %collective-permute-start.8 = (bf16[4096,512]{1,0:T(8,128)(2,1)}, bf16[4096,512]{1,0:T(8,128)(2,1)}, u32[]{:S(2)}, u32[]{:S(2)}) collective-permute-start(bf16[4096,512]{1,0:T(8,128)(2,1)} %collective-permute-done.5), channel_id=1, source_target_pairs={{0,1},{1,0},{2,3},{3,2},{4,5},{5,4},{6,7},{7,6},{8,9},{9,8},{10,11... | collective-permute-start | bytes 12582920 | tf_op jit(solution)/shard_map/ppermute | solution.py:18
  128.8 81.5 %collective-permute-start.11 = (bf16[2048,1024]{1,0:T(8,128)(2,1)}, bf16[2048,1024]{1,0:T(8,128)(2,1)}, u32[]{:S(2)}, u32[]{:S(2)}) collective-permute-start(bf16[2048,1024]{1,0:T(8,128)(2,1)} %param.10), channel_id=1, source_target_pairs={{0,1},{1,0},{2,3},{3,2},{4,5},{5,4},{6,7},{7,6},{8,9},{9,8},{10,11... | collective-permute-start | bytes 12582920 | tf_op jit(solution)/shard_map/ppermute | solution.py:18
  140.1 50.1 %collective-permute-start.16 = (bf16[512,512]{0,1:T(8,128)(2,1)S(1)}, bf16[512,512]{0,1:T(8,128)(2,1)S(1)}, u32[]{:S(2)}, u32[]{:S(2)}) collective-permute-start(bf16[512,512]{0,1:T(8,128)(2,1)S(1)} %fusion.7), channel_id=1, source_target_pairs={{16,0},{20,4},{8,24},{12,28},{17,1},{21,5},{9,25},{13,29},{18,2},{... | collective-permute-start | bytes 1572872 | tf_op jit(solution)/shard_map/ppermute | solution.py:86
  146.0 45.7 %collective-permute-start.14 = (bf16[512,512]{0,1:T(8,128)(2,1)S(1)}, bf16[512,512]{0,1:T(8,128)(2,1)S(1)}, u32[]{:S(2)}, u32[]{:S(2)}) collective-permute-start(bf16[512,512]{0,1:T(8,128)(2,1)S(1)} %fusion.6), channel_id=1, source_target_pairs={{16,0},{20,4},{8,24},{12,28},{17,1},{21,5},{9,25},{13,29},{18,2},{... | collective-permute-start | bytes 1572872 | tf_op jit(solution)/shard_map/ppermute | solution.py:86
  152.6 40.4 %collective-permute-start.12 = (bf16[512,512]{0,1:T(8,128)(2,1)}, bf16[512,512]{0,1:T(8,128)(2,1)}, u32[]{:S(2)}, u32[]{:S(2)}) collective-permute-start(bf16[512,512]{0,1:T(8,128)(2,1)} %fusion.5), channel_id=1, source_target_pairs={{16,0},{20,4},{8,24},{12,28},{17,1},{21,5},{9,25},{13,29},{18,2},{... | collective-permute-start | bytes 1572872 | tf_op jit(solution)/shard_map/ppermute | solution.py:86
  190.2 92.8 %collective-permute-start.20 = (bf16[2048,1024]{1,0:T(8,128)(2,1)}, bf16[2048,1024]{1,0:T(8,128)(2,1)}, u32[]{:S(2)}, u32[]{:S(2)}) collective-permute-start(bf16[2048,1024]{1,0:T(8,128)(2,1)} %param.10), channel_id=1, source_target_pairs={{0,2},{1,3},{2,0},{3,1},{4,6},{5,7},{6,4},{7,5},{8,10},{9,11},{10,... | collective-permute-start | bytes 12582920 | tf_op jit(solution)/shard_map/ppermute | solution.py:18
  191.7 71.4 %collective-permute-start.6 = (bf16[512,512]{0,1:T(8,128)(2,1)S(1)}, bf16[512,512]{0,1:T(8,128)(2,1)S(1)}, u32[]{:S(2)}, u32[]{:S(2)}) collective-permute-start(bf16[512,512]{0,1:T(8,128)(2,1)S(1)} %fusion.3), channel_id=1, source_target_pairs={{16,0},{20,4},{8,24},{12,28},{17,1},{21,5},{9,25},{13,29},{18,2},{... | collective-permute-start | bytes 1572872 | tf_op jit(solution)/shard_map/ppermute | solution.py:86
  193.0 70.1 %collective-permute-start.3 = (bf16[512,512]{0,1:T(8,128)(2,1)S(1)}, bf16[512,512]{0,1:T(8,128)(2,1)S(1)}, u32[]{:S(2)}, u32[]{:S(2)}) collective-permute-start(bf16[512,512]{0,1:T(8,128)(2,1)S(1)} %fusion.2), channel_id=1, source_target_pairs={{16,0},{20,4},{8,24},{12,28},{17,1},{21,5},{9,25},{13,29},{18,2},{... | collective-permute-start | bytes 1572872 | tf_op jit(solution)/shard_map/ppermute | solution.py:86
  210.3 18.5 %collective-permute-start.15 = (bf16[512,512]{0,1:T(8,128)(2,1)S(1)}, bf16[512,512]{0,1:T(8,128)(2,1)S(1)}, u32[]{:S(2)}, u32[]{:S(2)}) collective-permute-start(bf16[512,512]{0,1:T(8,128)(2,1)S(1)} %get-tuple-element.11), channel_id=1, source_target_pairs={{0,16},{4,20},{24,8},{28,12},{1,17},{5,21},{25,9},{29,13},{2,18},{... | collective-permute-start | bytes 1572872 | tf_op jit(solution)/shard_map/ppermute | solution.py:94
  217.5 22.5 %collective-permute-start.17 = (bf16[512,512]{0,1:T(8,128)(2,1)S(1)}, bf16[512,512]{0,1:T(8,128)(2,1)S(1)}, u32[]{:S(2)}, u32[]{:S(2)}) collective-permute-start(bf16[512,512]{0,1:T(8,128)(2,1)S(1)} %get-tuple-element.10), channel_id=1, source_target_pairs={{0,16},{4,20},{24,8},{28,12},{1,17},{5,21},{25,9},{29,13},{2,18},{... | collective-permute-start | bytes 1572872 | tf_op jit(solution)/shard_map/ppermute | solution.py:94
  228.8 19.6 %collective-permute-start.19 = (bf16[512,512]{0,1:T(8,128)(2,1)S(1)}, bf16[512,512]{0,1:T(8,128)(2,1)S(1)}, u32[]{:S(2)}, u32[]{:S(2)}) collective-permute-start(bf16[512,512]{0,1:T(8,128)(2,1)S(1)} %get-tuple-element.9), channel_id=1, source_target_pairs={{0,16},{4,20},{24,8},{28,12},{1,17},{5,21},{25,9},{29,13},{2,18},{... | collective-permute-start | bytes 1572872 | tf_op jit(solution)/shard_map/ppermute | solution.py:94
  240.0 23.2 %collective-permute-start = (bf16[512,512]{0,1:T(8,128)(2,1)S(1)}, bf16[512,512]{0,1:T(8,128)(2,1)S(1)}, u32[]{:S(2)}, u32[]{:S(2)}) collective-permute-start(bf16[512,512]{0,1:T(8,128)(2,1)S(1)} %fusion.1), channel_id=1, source_target_pairs={{16,0},{20,4},{8,24},{12,28},{17,1},{21,5},{9,25},{13,29},{18,2},{... | collective-permute-start | bytes 1572872 | tf_op jit(solution)/shard_map/ppermute | solution.py:86
  255.8 113.7 %reduce-scatter.5.cloned.1.call-start = ((), (), s32[]{:S(2)}) async-start(), calls=%async_computation.5 | async-start | bytes 2621440 | tf_op jit(solution)/shard_map/reduce_scatter | solution.py:106
  278.1 23.6 %collective-permute-start.4 = (bf16[512,512]{0,1:T(8,128)(2,1)S(1)}, bf16[512,512]{0,1:T(8,128)(2,1)S(1)}, u32[]{:S(2)}, u32[]{:S(2)}) collective-permute-start(bf16[512,512]{0,1:T(8,128)(2,1)S(1)} %get-tuple-element.15), channel_id=1, source_target_pairs={{0,16},{4,20},{24,8},{28,12},{1,17},{5,21},{25,9},{29,13},{2,18},{... | collective-permute-start | bytes 1572872 | tf_op jit(solution)/shard_map/ppermute | solution.py:94
  283.0 45.5 %collective-permute-start.21 = (bf16[2048,1024]{1,0:T(8,128)(2,1)}, bf16[2048,1024]{1,0:T(8,128)(2,1)}, u32[]{:S(2)}, u32[]{:S(2)}) collective-permute-start(bf16[2048,1024]{1,0:T(8,128)(2,1)} %collective-permute-done.20), channel_id=1, source_target_pairs={{0,1},{1,0},{2,3},{3,2},{4,5},{5,4},{6,7},{7,6},{8,9},{9,8},{10,11... | collective-permute-start | bytes 12582920 | tf_op jit(solution)/shard_map/ppermute | solution.py:18
  283.0 29.9 %collective-permute-start.7 = (bf16[512,512]{0,1:T(8,128)(2,1)S(1)}, bf16[512,512]{0,1:T(8,128)(2,1)S(1)}, u32[]{:S(2)}, u32[]{:S(2)}) collective-permute-start(bf16[512,512]{0,1:T(8,128)(2,1)S(1)} %get-tuple-element.14), channel_id=1, source_target_pairs={{0,16},{4,20},{24,8},{28,12},{1,17},{5,21},{25,9},{29,13},{2,18},{... | collective-permute-start | bytes 1572872 | tf_op jit(solution)/shard_map/ppermute | solution.py:94
  287.3 32.4 %collective-permute-start.10 = (bf16[512,512]{0,1:T(8,128)(2,1)S(1)}, bf16[512,512]{0,1:T(8,128)(2,1)S(1)}, u32[]{:S(2)}, u32[]{:S(2)}) collective-permute-start(bf16[512,512]{0,1:T(8,128)(2,1)S(1)} %get-tuple-element.13), channel_id=1, source_target_pairs={{0,16},{4,20},{24,8},{28,12},{1,17},{5,21},{25,9},{29,13},{2,18},{... | collective-permute-start | bytes 1572872 | tf_op jit(solution)/shard_map/ppermute | solution.py:94
  325.8 89.1 %reduce-scatter.9.cloned.1.call-start = ((), (), s32[]{:S(2)}) async-start(), calls=%async_computation.8 | async-start | bytes 2621440 | tf_op jit(solution)/shard_map/reduce_scatter | solution.py:106
  340.2 120.2 %reduce-scatter.11.cloned.1.call-start = ((), (), s32[]{:S(2)}) async-start(), calls=%async_computation.9 | async-start | bytes 2621440 | tf_op jit(solution)/shard_map/reduce_scatter | solution.py:106
  (23 other events, 474.2 us)
Sparse Core Ops, SparseCore 0:
  9.7 83.2 all-gather.4
  94.5 78.7 all-gather.2
  256.0 43.1 reduce-scatter.6
  325.9 43.5 reduce-scatter.4
  371.7 43.1 reduce-scatter.8
  417.2 43.1 reduce-scatter.10

commit v2 on v0

v2 whole, which is shorter than its diff:
```python
import functools

import jax
import jax.numpy as jnp
from jax import lax
from jax.experimental import pallas as pl
from jax.experimental.pallas import tpu as pltpu
from jax.sharding import PartitionSpec as P

SHARES = (4, 4)
VMEM_BYTES = 48 * 2**20


def far_and_near(size, bit):
    return [(place, place ^ bit) for place in range(size)]


def cross_kernel(meta, samples, weight, out, total):
    step = pl.program_id(0)

    @pl.when(step == 0)
    def _():
        total[...] = jnp.zeros_like(total)

    @pl.when(step < meta[0])
    def _():
        total[...] += jnp.dot(samples[...], weight[...], preferred_element_type=jnp.float32)

    @pl.when(step == pl.num_programs(0) - 1)
    def _():
        out[...] = total[...].astype(out.dtype)


def cross_product(meta, samples, weight, block):
    rows, depth = samples.shape
    columns = weight.shape[1]
    steps = depth // block
    return pl.pallas_call(
        cross_kernel,
        out_shape=jax.ShapeDtypeStruct((rows, columns), jnp.bfloat16),
        grid_spec=pltpu.PrefetchScalarGridSpec(
            num_scalar_prefetch=1,
            grid=(steps,),
            in_specs=[
                pl.BlockSpec((rows, block), lambda i, meta: (0, meta[1 + i])),
                pl.BlockSpec((block, columns), lambda i, meta: (meta[1 + i], 0)),
            ],
            out_specs=pl.BlockSpec((rows, columns), lambda i, meta: (0, 0)),
            scratch_shapes=[pltpu.VMEM((rows, columns), jnp.float32)],
        ),
        compiler_params=pltpu.CompilerParams(vmem_limit_bytes=VMEM_BYTES),
        cost_estimate=pl.CostEstimate(
            flops=rows * depth * columns,
            bytes_accessed=(rows * depth + depth * columns + 2 * rows * columns),
            transcendentals=0,
        ),
    )(meta, samples, weight)


def linear_kernel(count, per_piece, meta, *refs):
    mine, theirs = refs[:count], refs[count : 2 * count]
    weights, out, joined = refs[2 * count : -2], refs[-2], refs[-1]
    step = pl.program_id(0)

    @pl.when(step == 0)
    def _():
        for apart in range(count):
            width = mine[apart].shape[1]
            columns = pl.ds(pl.multiple_of(meta[1 + apart] * width, width), width)

            @pl.when(meta[0] == 1)
            def _():
                joined[:, columns] = mine[apart][...]

            @pl.when(meta[0] == 0)
            def _():
                joined[:, columns] = theirs[apart][...]

    for place, weight in enumerate(weights):

        @pl.when(step // per_piece == place)
        def _():
            out[...] = jnp.dot(
                joined[...], weight[...], preferred_element_type=jnp.float32
            ).astype(out.dtype)


def linear_product(meta, mine, theirs, weights):
    count = len(mine)
    rows, width = mine[0].shape
    depth, columns = weights[0].shape
    tile = min(columns, 512)
    per_piece = columns // tile
    part = pl.BlockSpec((rows, width), lambda i, meta: (0, 0))

    def weight_spec(place):
        return pl.BlockSpec(
            (depth, tile),
            lambda i, meta: (0, jnp.clip(i - place * per_piece, 0, per_piece - 1)),
        )

    def out_index(i, meta):
        return 0, meta[1 + count + i // per_piece] * per_piece + i % per_piece

    return pl.pallas_call(
        functools.partial(linear_kernel, count, per_piece),
        out_shape=jax.ShapeDtypeStruct((rows, columns * len(weights)), jnp.bfloat16),
        grid_spec=pltpu.PrefetchScalarGridSpec(
            num_scalar_prefetch=1,
            grid=(per_piece * len(weights),),
            in_specs=[part] * (2 * count) + [weight_spec(p) for p in range(len(weights))],
            out_specs=pl.BlockSpec((rows, tile), out_index),
            scratch_shapes=[pltpu.VMEM((rows, depth), jnp.bfloat16)],
        ),
        compiler_params=pltpu.CompilerParams(vmem_limit_bytes=VMEM_BYTES),
        cost_estimate=pl.CostEstimate(
            flops=2 * rows * depth * columns * len(weights),
            bytes_accessed=4 * rows * depth
            + 2 * (depth + rows) * columns * len(weights),
            transcendentals=0,
        ),
    )(meta, *mine, *theirs, *weights)


def after(value, *others):
    return lax.optimization_barrier((value, *others))[0]


def added(*terms):
    return sum(term.astype(jnp.float32) for term in terms)


def finish_kernel(meta, own, came, samples, bias, out):
    base = samples[...].astype(jnp.float32)
    hidden = own[...].astype(jnp.float32) + came[...].astype(jnp.float32)
    out[...] = (base * (hidden + bias[...]) + base).astype(out.dtype)


def finish_cross(meta, own, came, samples, bias):
    rows, columns = own.shape
    tile = rows // 2
    part = pl.BlockSpec((tile, columns), lambda i, meta: (i, 0))
    return pl.pallas_call(
        finish_kernel,
        out_shape=jax.ShapeDtypeStruct((rows, columns), jnp.bfloat16),
        grid_spec=pltpu.PrefetchScalarGridSpec(
            num_scalar_prefetch=1,
            grid=(2,),
            in_specs=[
                part,
                part,
                pl.BlockSpec((tile, columns), lambda i, meta: (i, meta[0])),
                pl.BlockSpec((1, columns), lambda i, meta: (0, meta[1])),
            ],
            out_specs=part,
        ),
        cost_estimate=pl.CostEstimate(
            flops=4 * rows * columns, bytes_accessed=8 * rows * columns, transcendentals=0
        ),
    )(meta, own, came, samples, bias)


class LineSum:
    def __init__(self, partial, place, size):
        self.partial, self.place, self.size = partial, place, size
        self.rows = partial.shape[0] // size
        self.begun = []
        if size == 4:
            inward = [(0, 1), (3, 2)]
            self.begun = [lax.ppermute(self.part(i), "col", inward) for i in (3, 2, 1)]

    def part(self, if_lower):
        upper = self.place >= self.size // 2
        first = jnp.where(upper, self.size - 1 - if_lower, if_lower) * self.rows
        return lax.dynamic_slice_in_dim(self.partial, first, self.rows, 0)

    def end(self):
        if self.size != 4:
            summed = lax.psum_scatter(self.partial, "col", scatter_dimension=0, tiled=True)
            return summed.astype(jnp.float32)
        across, outward = [(1, 2), (2, 1)], [(1, 0), (2, 3)]
        from_3, from_2, from_1 = self.begun
        over_3 = lax.ppermute(added(self.part(3), from_3).astype(jnp.bfloat16), "col", across)
        over_2 = lax.ppermute(added(self.part(2), from_2).astype(jnp.bfloat16), "col", across)
        out_0 = lax.ppermute(added(self.part(0), over_3).astype(jnp.bfloat16), "col", outward)
        own = lax.dynamic_slice_in_dim(self.partial, self.place * self.rows, self.rows, 0)
        is_end = (self.place == 0) | (self.place == self.size - 1)
        return added(own) + jnp.where(is_end, added(out_0), added(from_1, over_2))


def build(mesh):
    n_row, n_col, n_batch = (mesh.shape[name] for name in ("row", "col", "batch"))

    def on_device(features, cross_weight, cross_bias, pattern, linear_weight, linear_bias):
        input_width, piece_width = cross_weight.shape
        width = input_width * n_row
        output_width = piece_width * n_batch
        mixed_width = linear_weight.shape[1]
        block = width // pattern.shape[0]
        in_blocks = input_width // block
        row, col, batch = (lax.axis_index(name) for name in ("row", "col", "batch"))
        half = n_batch // 2

        def to_batch(shard, bit):
            return lax.ppermute(shard, "batch", far_and_near(n_batch, bit))

        def spread_near(pieces):
            bit = half // 2
            while bit:
                for apart in list(pieces):
                    pieces[apart | bit] = to_batch(pieces[apart], bit)
                bit //= 2
            return pieces

        cross_across = to_batch(cross_weight, half)
        linear_across = to_batch(linear_weight, half)
        cross_pieces = spread_near({0: cross_weight})
        linear_pieces = spread_near({0: linear_weight})

        shard_rows = features.shape[0]
        starts = [shard_rows * sum(SHARES[:i]) // sum(SHARES) for i in range(len(SHARES) + 1)]
        gathered = [
            lax.all_gather(features[first:last], "col", axis=0, tiled=True)
            for first, last in zip(starts, starts[1:])
        ]

        def kept_list(apart):
            out_block = (col * n_batch + (batch ^ apart)) * piece_width // block
            kept = lax.dynamic_slice(pattern, (out_block, row * in_blocks), (1, in_blocks))[0]
            number = jnp.sum(kept)
            rank = jnp.cumsum(kept) - 1
            slots = jnp.minimum(jnp.arange(in_blocks), jnp.maximum(number - 1, 0))
            match = (rank[None, :] == slots[:, None]) & (kept[None, :] == 1)
            listed = jnp.sum(jnp.where(match, jnp.arange(in_blocks)[None, :], 0), axis=1)
            return jnp.concatenate([number[None], listed]).astype(jnp.int32)

        kept_lists = [kept_list(apart) for apart in range(n_batch)]

        def owner_of(column):
            return column * output_width // input_width

        is_owner = row == col * output_width // input_width
        turns = [
            [
                ((owner_of(c) + turn) % n_row * n_col + c, owner_of(c) * n_col + c)
                for c in range(n_col)
            ]
            for turn in range(1, n_row)
        ]
        first_base = jnp.where(is_owner, col * output_width - row * input_width, 0)

        chunks = range(len(SHARES))
        bias_row = cross_bias[None, :]
        near = [place for place in range(half)]
        far = [half + place for place in range(half)]
        products, mine, theirs = {}, {}, {}

        def multiply(step, group):
            for apart in group:
                products[step, apart] = cross_product(
                    kept_lists[apart], gathered[step], cross_pieces[apart], block
                )
            return [products[step, apart] for apart in group]

        def finish(step, group):
            for apart in group:
                first = (batch ^ apart) * piece_width
                own = products[step, apart]
                came = [lax.ppermute(own, ("row", "col"), pairs) for pairs in turns]
                place = jnp.stack([(first_base + first) // piece_width, batch ^ apart])
                crossed = finish_cross(
                    place.astype(jnp.int32), own, sum(came[1:], came[0]), gathered[step], bias_row
                )
                back = [
                    lax.ppermute(crossed, ("row", "col"), [(to, source) for source, to in pairs])
                    for pairs in turns
                ]
                mine[step, apart] = crossed
                theirs[step, apart] = sum(back[1:], back[0])

        meta = jnp.stack(
            [is_owner.astype(jnp.int32)]
            + [batch ^ place for place in range(n_batch)]
            + [(batch ^ place) % half for place in range(half)]
        ).astype(jnp.int32)

        def linear(step, group):
            return linear_product(
                meta,
                [mine[step, apart] for apart in range(n_batch)],
                [theirs[step, apart] for apart in range(n_batch)],
                [linear_pieces[apart] for apart in group],
            )

        sums = {}
        for step in chunks:
            last = step == chunks[-1]
            if step:
                gathered[step] = after(gathered[step], *sums[step - 1, 0].begun)
            sent = multiply(step, near)
            if not step:
                cross_across = after(cross_across, *sent)
                arrived = spread_near({0: cross_across})
                cross_pieces.update({half + place: arrived[place] for place in near})
            sent = multiply(step, far)
            if last:
                linear_across = after(linear_across, *sent)
                arrived = spread_near({0: linear_across})
                linear_pieces.update({half + place: arrived[place] for place in near})
                for past in range(step):
                    sums[past, 1] = LineSum(linear(past, far), col, n_col)
            finish(step, near + far)
            if last and step:
                mine[step, 0] = after(mine[step, 0], *sums[step - 1, 1].begun[:2])
            sums[step, 0] = LineSum(linear(step, near), col, n_col)
            if last:
                sums[step, 1] = LineSum(linear(step, far), col, n_col)

        out = jnp.zeros((shard_rows, mixed_width * n_batch), jnp.bfloat16)
        for step in chunks:
            for group in range(2):
                first = ((batch // half) ^ group) * half * mixed_width
                bias = lax.dynamic_slice_in_dim(linear_bias, first, half * mixed_width)
                out = lax.dynamic_update_slice(
                    out,
                    (sums[step, group].end() + bias).astype(jnp.bfloat16),
                    (starts[step], first),
                )
        return out

    return on_device


def solution(mesh):
    return jax.shard_map(
        build(mesh),
        mesh=mesh,
        in_specs=(
            P(("col", "batch"), "row"),
            P("row", ("col", "batch")),
            P("col"),
            P(),
            P("col", ("row", "batch")),
            P("row"),
        ),
        out_specs=P(("col", "batch"), "row"),
        check_vma=False,
    )
```

time: 724 us -> 481 us (0.66)
  waiting for transfers between devices: 631 us -> 213 us
  starting transfers between devices: 0.42 us -> 105 us
  Pallas kernels: 0 us -> 96.1 us
  matrix products: 47.8 us -> 0 us
  local copies, waits for them, and re-layouts: 15.3 us -> 23.2 us
    all_gather x4 -> x2, waiting for transfers between devices: 397 us -> 74.8 us  [on_device(): lax.all_gather(features[first:last], 'col', axis=0, tiled=True)]
    reduce_scatter x3 -> x0, waiting for transfers between devices: 232 us -> none  [the longest x1 145 us: on_device(): lax.psum_scatter(jnp.dot(crossed, linear_full, preferred_element_type=jnp...]
    ppermute x0 -> x46, waiting for transfers between devices: none -> 138 us  [the longest x12 65.2 us: __init__(): self.begun = [lax.ppermute(self.part(i), 'col', inward) for i in (3, 2, 1)]]
    ppermute x0 -> x46, starting transfers between devices: none -> 105 us  [the longest x12 61.5 us: __init__(): self.begun = [lax.ppermute(self.part(i), 'col', inward) for i in (3, 2, 1)]]
    pallas_call x0 -> x20, Pallas kernels: none -> 96.1 us  [the longest x4 38.5 us: linear_product(): pl.pallas_call(functools.partial(linear_kernel, count, per_piece), out_sh...]
    dot_general x2 -> x0, matrix products: 47.8 us -> none  [the longest x1 24.9 us: on_device(): partial_sum = jnp.dot(samples, pruned, preferred_element_type=jnp.float32)]
    dynamic_slice x0 -> x5, local copies, waits for them, and re-layouts: none -> 8.16 us  [the longest x4 8.15 us: part(): return lax.dynamic_slice_in_dim(self.partial, first, self.rows, 0)]
    convert_element_type x4 -> x12, other arithmetic: 15.7 us -> 8.71 us  [the longest x4 3.56 us: end(): added(self.part(2), from_2).astype(jnp.bfloat16)]
  transfers between devices with their start and end apart: 7 -> 48, of which waited for: 7 -> 20; matrix products, arithmetic and copies ran while one was open for 7% -> 6% of each run, Pallas kernels for 0% -> 20%
where the time goes in v2:
time: 481 us; the launch traced here: 478 us
  waiting for transfers between devices  213 us (44%)
  starting transfers between devices  105 us (22%)
  Pallas kernels  96.1 us (20%)
  local copies, waits for them, and re-layouts  23.2 us (5%)
  other arithmetic  22.9 us (5%)
  between operations  17 us (4%)
    all_gather x2, waiting for transfers between devices, on_device(): lax.all_gather(features[first:last], 'col', axis=0, tiled=True)  74.8 us
    ppermute x12, waiting for transfers between devices, __init__(): self.begun = [lax.ppermute(self.part(i), 'col', inward) for i in (3, 2, 1)]  65.2 us
    ppermute x12, starting transfers between devices, __init__(): self.begun = [lax.ppermute(self.part(i), 'col', inward) for i in (3, 2, 1)]  61.5 us
    pallas_call x4, Pallas kernels, linear_product(): pl.pallas_call(functools.partial(linear_kernel, count, per_piece), out_sh...  38.5 us
    pallas_call x8, Pallas kernels, cross_product(): pl.pallas_call(cross_kernel, out_shape=jax.ShapeDtypeStruct((rows, column...  34.3 us
    ppermute x8, waiting for transfers between devices, finish(): lax.ppermute(crossed, ('row', 'col'), [(to, source) for source, to in pai...  32.7 us
    ppermute x8, waiting for transfers between devices, finish(): came = [lax.ppermute(own, ('row', 'col'), pairs) for pairs in turns]  26.2 us
    pallas_call x8, Pallas kernels, finish_cross(): pl.pallas_call(finish_kernel, out_shape=jax.ShapeDtypeStruct((rows, colum...  23.3 us
  transfers between devices with their start and end apart: 48, of which 20 were waited for; matrix products, arithmetic and copies ran while one was open for 6% of the time, Pallas kernels for 20%

profile of v2, /device:TPU:0, one launch (start us, length us, event | category | flops | bytes accessed | tf_op | source)
XLA Modules:
  0.0 477.5 jit_solution(11367798511924814368)
XLA Ops:
  18.4 74.8 %all-gather.3.cloned.1.call-done.samples = bf16[512,4096]{1,0:T(8,128)(2,1)} async-done(((bf16[128,4096]{1,0:T(8,128)(2,1)}), bf16[512,4096]{1,0:T(8,128)(2,1)}) %all-gather.3.cloned.1.call-update) | async-done | bytes 4194320 | tf_op jit(solution)/shard_map/all_gather | solution.py:223
  113.1 4.6 shard_map.68.own
  122.6 4.5 shard_map.70.own
  127.1 11.2 %collective-permute-done.4.came = bf16[512,512]{1,0:T(8,128)(2,1)S(1)} collective-permute-done((bf16[512,512]{1,0:T(8,128)(2,1)S(1)}, bf16[512,512]{1,0:T(8,128)(2,1)S(1)}, u32[]{:S(2)}, u32[]{:S(2)}) %collective-permute-start.4) | collective-permute-done | bytes 524320 | tf_op jit(solution)/shard_map/ppermute | solution.py:269
  145.1 4.5 collective-permute-done.2.came
  153.9 6.9 %collective-permute-done.came = bf16[512,512]{1,0:T(8,128)(2,1)S(1)} collective-permute-done((bf16[512,512]{1,0:T(8,128)(2,1)S(1)}, bf16[512,512]{1,0:T(8,128)(2,1)S(1)}, u32[]{:S(2)}, u32[]{:S(2)}) %collective-permute-start) | collective-permute-done | bytes 524320 | tf_op jit(solution)/shard_map/ppermute | solution.py:269
  175.2 7.6 %collective-permute-done.7.refs_4_ = bf16[512,512]{1,0:T(8,128)(2,1)S(1)} collective-permute-done((bf16[512,512]{1,0:T(8,128)(2,1)}, bf16[512,512]{1,0:T(8,128)(2,1)S(1)}, u32[]{:S(2)}, u32[]{:S(2)}) %collective-permute-start.7) | collective-permute-done | bytes 524320 | tf_op jit(solution)/shard_map/ppermute | solution.py:275
  182.8 8.9 %collective-permute-done.10.refs_7_ = bf16[512,512]{1,0:T(8,128)(2,1)} collective-permute-done((bf16[512,512]{1,0:T(8,128)(2,1)}, bf16[512,512]{1,0:T(8,128)(2,1)}, u32[]{:S(2)}, u32[]{:S(2)}) %collective-permute-start.10) | collective-permute-done | bytes 524320 | tf_op jit(solution)/shard_map/ppermute | solution.py:275
  192.7 9.5 %shard_map.72 = bf16[512,2048]{1,0:T(8,128)(2,1)} custom-call(s32[7]{0:T(128)S(1)} %stack.75.meta, bf16[512,512]{1,0:T(8,128)(2,1)S(1)} %copy-done.15, bf16[512,512]{1,0:T(8,128)(2,1)S(1)} %copy-done.14, bf16[512,512]{1,0:T(8,128)(2,1)S(1)} %copy-done.13, bf16[512,512]{1,0:T(8,128)(2,1)S(1)} %copy-done.17, ...), custom_call_target="tpu_custom_call" | custom-call | flops 4294967296 | bytes 14680064 | tf_op jit(solution)/shard_map/pallas_call | solution.py:105
  212.2 9.2 %collective-permute-done.12 = bf16[128,2048]{1,0:T(8,128)(2,1)S(1)} collective-permute-done((bf16[128,2048]{1,0:T(8,128)(2,1)}, bf16[128,2048]{1,0:T(8,128)(2,1)S(1)}, u32[]{:S(2)}, u32[]{:S(2)}) %collective-permute-start.12) | collective-permute-done | bytes 524320 | tf_op jit(solution)/shard_map/ppermute | solution.py:170
  221.4 11.2 %collective-permute-done.15 = bf16[128,2048]{1,0:T(8,128)(2,1)S(1)} collective-permute-done((bf16[128,2048]{1,0:T(8,128)(2,1)}, bf16[128,2048]{1,0:T(8,128)(2,1)S(1)}, u32[]{:S(2)}, u32[]{:S(2)}) %collective-permute-start.15) | collective-permute-done | bytes 524320 | tf_op jit(solution)/shard_map/ppermute | solution.py:170
  233.4 8.1 %collective-permute-done.16 = bf16[128,2048]{1,0:T(8,128)(2,1)} collective-permute-done((bf16[128,2048]{1,0:T(8,128)(2,1)S(1)}, bf16[128,2048]{1,0:T(8,128)(2,1)}, u32[]{:S(2)}, u32[]{:S(2)}) %collective-permute-start.16) | collective-permute-done | bytes 524320 | tf_op jit(solution)/shard_map/ppermute | solution.py:170
  275.9 9.6 %shard_map.75 = bf16[512,2048]{1,0:T(8,128)(2,1)} custom-call(s32[7]{0:T(128)S(1)} %stack.75.meta, bf16[512,512]{1,0:T(8,128)(2,1)S(1)} %copy-done.16, bf16[512,512]{1,0:T(8,128)(2,1)S(1)} %copy-done.14, bf16[512,512]{1,0:T(8,128)(2,1)S(1)} %copy-done.13, bf16[512,512]{1,0:T(8,128)(2,1)S(1)} %copy-done.18, bf16[512,512]{1,0:T(8,128)(2,1)S(1)} %copy-done.28, ...), custom_call_target="tpu_custom_call" | custom-call | flops 4294967296 | bytes 14680064 | tf_op jit(solution)/shard_map/pallas_call | solution.py:105
  290.1 16.0 %collective-permute-start.20 = (bf16[128,2048]{1,0:T(8,128)(2,1)}, bf16[128,2048]{1,0:T(8,128)(2,1)}, u32[]{:S(2)}, u32[]{:S(2)}) collective-permute-start(bf16[128,2048]{1,0:T(8,128)(2,1)} %get-tuple-element.27), channel_id=1, source_target_pairs={{0,4},{12,8},{1,5},{13,9},{2,6},{14,10},{3,7},{15,11},{16,20},{28,... | collective-permute-start | bytes 1572872 | tf_op jit(solution)/shard_map/ppermute | solution.py:170
  332.0 8.1 %collective-permute-done.24 = bf16[128,2048]{1,0:T(8,128)(2,1)} collective-permute-done((bf16[128,2048]{1,0:T(8,128)(2,1)}, bf16[128,2048]{1,0:T(8,128)(2,1)}, u32[]{:S(2)}, u32[]{:S(2)}) %collective-permute-start.24) | collective-permute-done | bytes 524320 | tf_op jit(solution)/shard_map/ppermute | solution.py:170
  344.5 6.5 %collective-permute-done.31.refs_5_ = bf16[512,512]{1,0:T(8,128)(2,1)} collective-permute-done((bf16[512,512]{1,0:T(8,128)(2,1)S(1)}, bf16[512,512]{1,0:T(8,128)(2,1)}, u32[]{:S(2)}, u32[]{:S(2)}) %collective-permute-start.31) | collective-permute-done | bytes 524320 | tf_op jit(solution)/shard_map/ppermute | solution.py:275
  351.0 9.8 %collective-permute-done.30.refs_4_ = bf16[512,512]{1,0:T(8,128)(2,1)} collective-permute-done((bf16[512,512]{1,0:T(8,128)(2,1)}, bf16[512,512]{1,0:T(8,128)(2,1)}, u32[]{:S(2)}, u32[]{:S(2)}) %collective-permute-start.30) | collective-permute-done | bytes 524320 | tf_op jit(solution)/shard_map/ppermute | solution.py:275
  360.8 9.7 %shard_map.83 = bf16[512,2048]{1,0:T(8,128)(2,1)} custom-call(s32[7]{0:T(128)S(1)} %stack.75.meta, bf16[512,512]{1,0:T(8,128)(2,1)S(1)} %copy-done.22, bf16[512,512]{1,0:T(8,128)(2,1)S(1)} %copy-done.21, bf16[512,512]{1,0:T(8,128)(2,1)S(1)} %copy-done.20, bf16[512,512]{1,0:T(8,128)(2,1)S(1)} %copy-done.19, bf16[512,512]{1,0:T(8,128)(2,1)} %collective-permute-done.30.refs_4_, ...), custom_call_target="tpu_custom_call" | custom-call | flops 4294967296 | bytes 14680064 | tf_op jit(solution)/shard_map/pallas_call | solution.py:105
  374.7 9.8 %shard_map.82 = bf16[512,2048]{1,0:T(8,128)(2,1)} custom-call(s32[7]{0:T(128)S(1)} %stack.75.meta, bf16[512,512]{1,0:T(8,128)(2,1)S(1)} %copy-done.22, bf16[512,512]{1,0:T(8,128)(2,1)S(1)} %copy-done.21, bf16[512,512]{1,0:T(8,128)(2,1)S(1)} %copy-done.20, bf16[512,512]{1,0:T(8,128)(2,1)S(1)} %copy-done.19, bf16[512,512]{1,0:T(8,128)(2,1)} %collective-permute-done.30.refs_4_, ...), custom_call_target="tpu_custom_call" | custom-call | flops 4294967296 | bytes 14680064 | tf_op jit(solution)/shard_map/pallas_call | solution.py:105
  397.8 10.4 %collective-permute-done.34 = bf16[128,2048]{1,0:T(8,128)(2,1)S(1)} collective-permute-done((bf16[128,2048]{1,0:T(8,128)(2,1)S(1)}, bf16[128,2048]{1,0:T(8,128)(2,1)S(1)}, u32[]{:S(2)}, u32[]{:S(2)}) %collective-permute-start.34) | collective-permute-done | bytes 524320 | tf_op jit(solution)/shard_map/ppermute | solution.py:170
  409.0 10.4 %collective-permute-done.38 = bf16[128,2048]{1,0:T(8,128)(2,1)S(1)} collective-permute-done((bf16[128,2048]{1,0:T(8,128)(2,1)S(1)}, bf16[128,2048]{1,0:T(8,128)(2,1)S(1)}, u32[]{:S(2)}, u32[]{:S(2)}) %collective-permute-start.38) | collective-permute-done | bytes 524320 | tf_op jit(solution)/shard_map/ppermute | solution.py:170
  428.4 24.9 %collective-permute-start.43 = (bf16[128,2048]{1,0:T(8,128)(2,1)S(1)}, bf16[128,2048]{1,0:T(8,128)(2,1)S(1)}, u32[]{:S(2)}, u32[]{:S(2)}) collective-permute-start(bf16[128,2048]{1,0:T(8,128)(2,1)S(1)} %get-tuple-element.23), channel_id=1, source_target_pairs={{0,4},{12,8},{1,5},{13,9},{2,6},{14,10},{3,7},{15,11},{16,20},{28,... | collective-permute-start | bytes 1572872 | tf_op jit(solution)/shard_map/ppermute | solution.py:170
  455.7 8.2 %collective-permute-done.36 = bf16[128,2048]{1,0:T(8,128)(2,1)S(1)} collective-permute-done((bf16[128,2048]{1,0:T(8,128)(2,1)S(1)}, bf16[128,2048]{1,0:T(8,128)(2,1)S(1)}, u32[]{:S(2)}, u32[]{:S(2)}) %collective-permute-start.36) | collective-permute-done | bytes 524320 | tf_op jit(solution)/shard_map/ppermute | solution.py:185
  464.3 5.2 %collective-permute-done.42 = bf16[128,2048]{1,0:T(8,128)(2,1)S(1)} collective-permute-done((bf16[128,2048]{1,0:T(8,128)(2,1)S(1)}, bf16[128,2048]{1,0:T(8,128)(2,1)S(1)}, u32[]{:S(2)}, u32[]{:S(2)}) %collective-permute-start.42) | collective-permute-done | bytes 524320 | tf_op jit(solution)/shard_map/ppermute | solution.py:185
  (231 shorter events, 171.0 us)
Async XLA Ops:
  6.5 86.7 %all-gather.3.cloned.1.call-start = ((), (), s32[]{:S(2)}) async-start(), calls=%async_computation | async-start | bytes 5242880 | tf_op jit(solution)/shard_map/all_gather | solution.py:223
  9.6 202.5 %all-gather.5.cloned.1.call-start = ((), (), s32[]{:S(2)}) async-start(), calls=%async_computation.1 | async-start | bytes 5242880 | tf_op jit(solution)/shard_map/all_gather | solution.py:223
  9.7 90.1 %collective-permute-start.1 = (bf16[4096,512]{1,0:T(8,128)(2,1)}, bf16[4096,512]{1,0:T(8,128)(2,1)}, u32[]{:S(2)}, u32[]{:S(2)}) collective-permute-start(bf16[4096,512]{1,0:T(8,128)(2,1)} %weight.3), channel_id=1, source_target_pairs={{0,1},{1,0},{2,3},{3,2},{4,5},{5,4},{6,7},{7,6},{8,9},{9,8},{10,11... | collective-permute-start | bytes 12582920 | tf_op jit(solution)/shard_map/ppermute | solution.py:205
  10.2 94.0 %collective-permute-start.3 = (bf16[4096,512]{1,0:T(8,128)(2,1)}, bf16[4096,512]{1,0:T(8,128)(2,1)}, u32[]{:S(2)}, u32[]{:S(2)}) collective-permute-start(bf16[4096,512]{1,0:T(8,128)(2,1)} %weight.3), channel_id=1, source_target_pairs={{0,2},{1,3},{2,0},{3,1},{4,6},{5,7},{6,4},{7,5},{8,10},{9,11},{10,... | collective-permute-start | bytes 12582920 | tf_op jit(solution)/shard_map/ppermute | solution.py:205
  104.3 68.8 %collective-permute-start.11 = (bf16[2048,1024]{1,0:T(8,128)(2,1)}, bf16[2048,1024]{1,0:T(8,128)(2,1)}, u32[]{:S(2)}, u32[]{:S(2)}) collective-permute-start(bf16[2048,1024]{1,0:T(8,128)(2,1)} %refs_8_.3), channel_id=1, source_target_pairs={{0,1},{1,0},{2,3},{3,2},{4,5},{5,4},{6,7},{7,6},{8,9},{9,8},{10,11... | collective-permute-start | bytes 12582920 | tf_op jit(solution)/shard_map/ppermute | solution.py:205
  104.8 147.9 %collective-permute-start.18 = (bf16[2048,1024]{1,0:T(8,128)(2,1)}, bf16[2048,1024]{1,0:T(8,128)(2,1)}, u32[]{:S(2)}, u32[]{:S(2)}) collective-permute-start(bf16[2048,1024]{1,0:T(8,128)(2,1)} %refs_8_.3), channel_id=1, source_target_pairs={{0,2},{1,3},{2,0},{3,1},{4,6},{5,7},{6,4},{7,5},{8,10},{9,11},{10,... | collective-permute-start | bytes 12582920 | tf_op jit(solution)/shard_map/ppermute | solution.py:205
  121.3 39.5 %collective-permute-start = (bf16[512,512]{1,0:T(8,128)(2,1)S(1)}, bf16[512,512]{1,0:T(8,128)(2,1)S(1)}, u32[]{:S(2)}, u32[]{:S(2)}) collective-permute-start(bf16[512,512]{1,0:T(8,128)(2,1)S(1)} %shard_map.64.own), channel_id=1, source_target_pairs={{16,0},{20,4},{8,24},{12,28},{17,1},{21,5},{9,25},{13,29},{18,2},{... | collective-permute-start | bytes 1572872 | tf_op jit(solution)/shard_map/ppermute | solution.py:269
  252.8 35.2 %collective-permute-start.29 = (bf16[512,512]{1,0:T(8,128)(2,1)S(1)}, bf16[512,512]{1,0:T(8,128)(2,1)S(1)}, u32[]{:S(2)}, u32[]{:S(2)}) collective-permute-start(bf16[512,512]{1,0:T(8,128)(2,1)S(1)} %shard_map.74.own), channel_id=1, source_target_pairs={{16,0},{20,4},{8,24},{12,28},{17,1},{21,5},{9,25},{13,29},{18,2},{... | collective-permute-start | bytes 1572872 | tf_op jit(solution)/shard_map/ppermute | solution.py:269
  254.1 35.2 %collective-permute-start.28 = (bf16[512,512]{1,0:T(8,128)(2,1)S(1)}, bf16[512,512]{1,0:T(8,128)(2,1)S(1)}, u32[]{:S(2)}, u32[]{:S(2)}) collective-permute-start(bf16[512,512]{1,0:T(8,128)(2,1)S(1)} %shard_map.73.own), channel_id=1, source_target_pairs={{16,0},{20,4},{8,24},{12,28},{17,1},{21,5},{9,25},{13,29},{18,2},{... | collective-permute-start | bytes 1572872 | tf_op jit(solution)/shard_map/ppermute | solution.py:269
  267.6 44.5 %collective-permute-start.27 = (bf16[512,512]{1,0:T(8,128)(2,1)S(1)}, bf16[512,512]{1,0:T(8,128)(2,1)}, u32[]{:S(2)}, u32[]{:S(2)}) collective-permute-start(bf16[512,512]{1,0:T(8,128)(2,1)S(1)} %shard_map.78.own), channel_id=1, source_target_pairs={{16,0},{20,4},{8,24},{12,28},{17,1},{21,5},{9,25},{13,29},{18,2},{... | collective-permute-start | bytes 1572872 | tf_op jit(solution)/shard_map/ppermute | solution.py:269
  271.1 48.0 %collective-permute-start.26 = (bf16[512,512]{1,0:T(8,128)(2,1)S(1)}, bf16[512,512]{1,0:T(8,128)(2,1)}, u32[]{:S(2)}, u32[]{:S(2)}) collective-permute-start(bf16[512,512]{1,0:T(8,128)(2,1)S(1)} %shard_map.76.own), channel_id=1, source_target_pairs={{16,0},{20,4},{8,24},{12,28},{17,1},{21,5},{9,25},{13,29},{18,2},{... | collective-permute-start | bytes 1572872 | tf_op jit(solution)/shard_map/ppermute | solution.py:269
  274.4 49.1 %collective-permute-start.17 = (bf16[128,2048]{1,0:T(8,128)(2,1)}, bf16[128,2048]{1,0:T(8,128)(2,1)}, u32[]{:S(2)}, u32[]{:S(2)}) collective-permute-start(bf16[128,2048]{1,0:T(8,128)(2,1)} %add_convert_fusion.13), channel_id=1, source_target_pairs={{4,8},{8,4},{5,9},{9,5},{6,10},{10,6},{7,11},{11,7},{20,24},{24,20... | collective-permute-start | bytes 1572872 | tf_op jit(solution)/shard_map/ppermute | solution.py:184
  288.0 37.5 %collective-permute-start.14 = (bf16[128,2048]{1,0:T(8,128)(2,1)}, bf16[128,2048]{1,0:T(8,128)(2,1)}, u32[]{:S(2)}, u32[]{:S(2)}) collective-permute-start(bf16[128,2048]{1,0:T(8,128)(2,1)} %add_convert_fusion.14), channel_id=1, source_target_pairs={{4,0},{8,12},{5,1},{9,13},{6,2},{10,14},{7,3},{11,15},{20,16},{24,... | collective-permute-start | bytes 1572872 | tf_op jit(solution)/shard_map/ppermute | solution.py:185
  290.1 37.6 %collective-permute-start.20 = (bf16[128,2048]{1,0:T(8,128)(2,1)}, bf16[128,2048]{1,0:T(8,128)(2,1)}, u32[]{:S(2)}, u32[]{:S(2)}) collective-permute-start(bf16[128,2048]{1,0:T(8,128)(2,1)} %get-tuple-element.27), channel_id=1, source_target_pairs={{0,4},{12,8},{1,5},{13,9},{2,6},{14,10},{3,7},{15,11},{16,20},{28,... | collective-permute-start | bytes 1572872 | tf_op jit(solution)/shard_map/ppermute | solution.py:170
  312.1 32.4 %collective-permute-start.33 = (bf16[512,512]{1,0:T(8,128)(2,1)S(1)}, bf16[512,512]{1,0:T(8,128)(2,1)S(1)}, u32[]{:S(2)}, u32[]{:S(2)}) collective-permute-start(bf16[512,512]{1,0:T(8,128)(2,1)S(1)} %copy-done.19), channel_id=1, source_target_pairs={{0,16},{4,20},{24,8},{28,12},{1,17},{5,21},{25,9},{29,13},{2,18},{... | collective-permute-start | bytes 1572872 | tf_op jit(solution)/shard_map/ppermute | solution.py:275
  325.6 35.2 %collective-permute-start.30 = (bf16[512,512]{1,0:T(8,128)(2,1)}, bf16[512,512]{1,0:T(8,128)(2,1)}, u32[]{:S(2)}, u32[]{:S(2)}) collective-permute-start(bf16[512,512]{1,0:T(8,128)(2,1)} %shard_map.77.refs_0_), channel_id=1, source_target_pairs={{0,16},{4,20},{24,8},{28,12},{1,17},{5,21},{25,9},{29,13},{2,18},{... | collective-permute-start | bytes 1572872 | tf_op jit(solution)/shard_map/ppermute | solution.py:275
  340.1 82.5 %collective-permute-start.23 = (bf16[128,2048]{1,0:T(8,128)(2,1)S(1)}, bf16[128,2048]{1,0:T(8,128)(2,1)S(1)}, u32[]{:S(2)}, u32[]{:S(2)}) collective-permute-start(bf16[128,2048]{1,0:T(8,128)(2,1)S(1)} %copy-done.35), channel_id=1, source_target_pairs={{0,4},{12,8},{1,5},{13,9},{2,6},{14,10},{3,7},{15,11},{16,20},{28,... | collective-permute-start | bytes 1572872 | tf_op jit(solution)/shard_map/ppermute | solution.py:170
  387.3 32.1 %collective-permute-start.38 = (bf16[128,2048]{1,0:T(8,128)(2,1)S(1)}, bf16[128,2048]{1,0:T(8,128)(2,1)S(1)}, u32[]{:S(2)}, u32[]{:S(2)}) collective-permute-start(bf16[128,2048]{1,0:T(8,128)(2,1)S(1)} %get-tuple-element.25), channel_id=1, source_target_pairs={{0,4},{12,8},{1,5},{13,9},{2,6},{14,10},{3,7},{15,11},{16,20},{28,... | collective-permute-start | bytes 1572872 | tf_op jit(solution)/shard_map/ppermute | solution.py:170
  391.3 37.1 %collective-permute-start.37 = (bf16[128,2048]{1,0:T(8,128)(2,1)S(1)}, bf16[128,2048]{1,0:T(8,128)(2,1)S(1)}, u32[]{:S(2)}, u32[]{:S(2)}) collective-permute-start(bf16[128,2048]{1,0:T(8,128)(2,1)S(1)} %get-tuple-element.26), channel_id=1, source_target_pairs={{0,4},{12,8},{1,5},{13,9},{2,6},{14,10},{3,7},{15,11},{16,20},{28,... | collective-permute-start | bytes 1572872 | tf_op jit(solution)/shard_map/ppermute | solution.py:170
  408.2 45.1 %collective-permute-start.25 = (bf16[128,2048]{1,0:T(8,128)(2,1)S(1)}, bf16[128,2048]{1,0:T(8,128)(2,1)S(1)}, u32[]{:S(2)}, u32[]{:S(2)}) collective-permute-start(bf16[128,2048]{1,0:T(8,128)(2,1)S(1)} %add_convert_fusion.9), channel_id=1, source_target_pairs={{4,8},{8,4},{5,9},{9,5},{6,10},{10,6},{7,11},{11,7},{20,24},{24,20... | collective-permute-start | bytes 1572872 | tf_op jit(solution)/shard_map/ppermute | solution.py:184
  421.1 32.9 %collective-permute-start.22 = (bf16[128,2048]{1,0:T(8,128)(2,1)S(1)}, bf16[128,2048]{1,0:T(8,128)(2,1)S(1)}, u32[]{:S(2)}, u32[]{:S(2)}) collective-permute-start(bf16[128,2048]{1,0:T(8,128)(2,1)S(1)} %add_convert_fusion.10), channel_id=1, source_target_pairs={{4,0},{8,12},{5,1},{9,13},{6,2},{10,14},{7,3},{11,15},{20,16},{24,... | collective-permute-start | bytes 1572872 | tf_op jit(solution)/shard_map/ppermute | solution.py:185
  422.6 33.1 %collective-permute-start.39 = (bf16[128,2048]{1,0:T(8,128)(2,1)S(1)}, bf16[128,2048]{1,0:T(8,128)(2,1)S(1)}, u32[]{:S(2)}, u32[]{:S(2)}) collective-permute-start(bf16[128,2048]{1,0:T(8,128)(2,1)S(1)} %add_convert_fusion.5), channel_id=1, source_target_pairs={{4,8},{8,4},{5,9},{9,5},{6,10},{10,6},{7,11},{11,7},{20,24},{24,20... | collective-permute-start | bytes 1572872 | tf_op jit(solution)/shard_map/ppermute | solution.py:184
  423.3 40.6 %collective-permute-start.36 = (bf16[128,2048]{1,0:T(8,128)(2,1)S(1)}, bf16[128,2048]{1,0:T(8,128)(2,1)S(1)}, u32[]{:S(2)}, u32[]{:S(2)}) collective-permute-start(bf16[128,2048]{1,0:T(8,128)(2,1)S(1)} %add_convert_fusion.6), channel_id=1, source_target_pairs={{4,0},{8,12},{5,1},{9,13},{6,2},{10,14},{7,3},{11,15},{20,16},{24,... | collective-permute-start | bytes 1572872 | tf_op jit(solution)/shard_map/ppermute | solution.py:185
  428.4 35.9 %collective-permute-start.43 = (bf16[128,2048]{1,0:T(8,128)(2,1)S(1)}, bf16[128,2048]{1,0:T(8,128)(2,1)S(1)}, u32[]{:S(2)}, u32[]{:S(2)}) collective-permute-start(bf16[128,2048]{1,0:T(8,128)(2,1)S(1)} %get-tuple-element.23), channel_id=1, source_target_pairs={{0,4},{12,8},{1,5},{13,9},{2,6},{14,10},{3,7},{15,11},{16,20},{28,... | collective-permute-start | bytes 1572872 | tf_op jit(solution)/shard_map/ppermute | solution.py:170
  (66 other events, 977.0 us)
Sparse Core Ops, SparseCore 0:
  9.8 83.4 all-gather.2
  104.4 82.4 all-gather.4

commit v3 on v2

--- a/solution.py
+++ b/solution.py
@@ -7,7 +7,7 @@
 from jax.experimental.pallas import tpu as pltpu
 from jax.sharding import PartitionSpec as P
 
-SHARES = (4, 4)
+SHARES = (2, 3, 3)
 VMEM_BYTES = 48 * 2**20
 
 
@@ -160,32 +160,43 @@
     )(meta, own, came, samples, bias)
 
 
-class LineSum:
-    def __init__(self, partial, place, size):
-        self.partial, self.place, self.size = partial, place, size
-        self.rows = partial.shape[0] // size
-        self.begun = []
-        if size == 4:
-            inward = [(0, 1), (3, 2)]
-            self.begun = [lax.ppermute(self.part(i), "col", inward) for i in (3, 2, 1)]
-
-    def part(self, if_lower):
-        upper = self.place >= self.size // 2
-        first = jnp.where(upper, self.size - 1 - if_lower, if_lower) * self.rows
-        return lax.dynamic_slice_in_dim(self.partial, first, self.rows, 0)
-
-    def end(self):
-        if self.size != 4:
-            summed = lax.psum_scatter(self.partial, "col", scatter_dimension=0, tiled=True)
-            return summed.astype(jnp.float32)
-        across, outward = [(1, 2), (2, 1)], [(1, 0), (2, 3)]
-        from_3, from_2, from_1 = self.begun
-        over_3 = lax.ppermute(added(self.part(3), from_3).astype(jnp.bfloat16), "col", across)
-        over_2 = lax.ppermute(added(self.part(2), from_2).astype(jnp.bfloat16), "col", across)
-        out_0 = lax.ppermute(added(self.part(0), over_3).astype(jnp.bfloat16), "col", outward)
-        own = lax.dynamic_slice_in_dim(self.partial, self.place * self.rows, self.rows, 0)
-        is_end = (self.place == 0) | (self.place == self.size - 1)
-        return added(own) + jnp.where(is_end, added(out_0), added(from_1, over_2))
+class LineGather:
+    def __init__(self, shard, place):
+        self.shard, self.place = shard, place
+        self.beside = lax.ppermute(shard, "col", [(0, 1), (1, 0), (2, 3), (3, 2)])
+        self.over = lax.ppermute(shard, "col", [(1, 2), (2, 1)])
+
+    def relay(self):
+        outward = [(1, 0), (2, 3)]
+        self.out = lax.ppermute(self.over, "col", outward)
+        self.over_beside = lax.ppermute(self.beside, "col", [(1, 2), (2, 1)])
+        self.out_beside = lax.ppermute(self.over_beside, "col", outward)
+
+    def whole(self):
+        place, shard = self.place, self.shard
+        is_end = (place == 0) | (place == 3)
+        lower = place < 2
+        rows = shard.shape[0]
+        whole = jnp.zeros((4 * rows, shard.shape[1]), shard.dtype)
+        for part, at in (
+            (shard, place),
+            (self.beside, place ^ 1),
+            (jnp.where(is_end, self.out, self.over), jnp.where(lower, 2, 1)),
+            (jnp.where(is_end, self.out_beside, self.over_beside), jnp.where(lower, 3, 0)),
+        ):
+            whole = lax.dynamic_update_slice_in_dim(whole, part, at * rows, 0)
+        return whole
+
+
+class PlainGather:
+    def __init__(self, shard, place):
+        self.shard = self.beside = self.over = self.out = self.over_beside = self.out_beside = shard
+
+    def relay(self):
+        pass
+
+    def whole(self):
+        return lax.all_gather(self.shard, "col", axis=0, tiled=True)
 
 
 def build(mesh):
@@ -219,10 +230,12 @@
 
         shard_rows = features.shape[0]
         starts = [shard_rows * sum(SHARES[:i]) // sum(SHARES) for i in range(len(SHARES) + 1)]
-        gathered = [
-            lax.all_gather(features[first:last], "col", axis=0, tiled=True)
-            for first, last in zip(starts, starts[1:])
-        ]
+        shards = [features[first:last] for first, last in zip(starts, starts[1:])]
+        gathers, gathered = [], {}
+        for step, shard in enumerate(shards):
+            if step > 1:
+                shard = after(shard, gathers[step - 2].beside)
+            gathers.append((LineGather if n_col == 4 else PlainGather)(shard, col))
 
         def kept_list(apart):
             out_block = (col * n_batch + (batch ^ apart)) * piece_width // block
@@ -253,29 +266,37 @@
         bias_row = cross_bias[None, :]
         near = [place for place in range(half)]
         far = [half + place for place in range(half)]
-        products, mine, theirs = {}, {}, {}
-
-        def multiply(step, group):
+        products, came, mine, theirs = {}, {}, {}, {}
+
+        latest = []
+
+        def in_turn(meta, *others):
+            return after(meta, *latest[-1:], *others)
+
+        def multiply(step, group, *others):
             for apart in group:
                 products[step, apart] = cross_product(
-                    kept_lists[apart], gathered[step], cross_pieces[apart], block
+                    in_turn(kept_lists[apart], *others), gathered[step], cross_pieces[apart], block
                 )
-            return [products[step, apart] for apart in group]
-
-        def finish(step, group):
+                latest.append(products[step, apart])
+                came[step, apart] = [
+                    lax.ppermute(products[step, apart], ("row", "col"), pairs) for pairs in turns
+                ]
+
+        def finish(step, group, *others):
             for apart in group:
                 first = (batch ^ apart) * piece_width
-                own = products[step, apart]
-                came = [lax.ppermute(own, ("row", "col"), pairs) for pairs in turns]
+                own, sent = products[step, apart], came[step, apart]
                 place = jnp.stack([(first_base + first) // piece_width, batch ^ apart])
                 crossed = finish_cross(
-                    place.astype(jnp.int32), own, sum(came[1:], came[0]), gathered[step], bias_row
+                    in_turn(place.astype(jnp.int32), *others), own, sum(sent[1:], sent[0]), gathered[step], bias_row
                 )
                 back = [
                     lax.ppermute(crossed, ("row", "col"), [(to, source) for source, to in pairs])
                     for pairs in turns
                 ]
                 mine[step, apart] = crossed
+                latest.append(crossed)
                 theirs[step, apart] = sum(back[1:], back[0])
 
         meta = jnp.stack(
@@ -284,47 +305,55 @@
             + [(batch ^ place) % half for place in range(half)]
         ).astype(jnp.int32)
 
-        def linear(step, group):
-            return linear_product(
-                meta,
+        partial = {}
+
+        def linear(step, group, *others):
+            partial[step, group[0] // half] = linear_product(
+                in_turn(meta, *others),
                 [mine[step, apart] for apart in range(n_batch)],
                 [theirs[step, apart] for apart in range(n_batch)],
                 [linear_pieces[apart] for apart in group],
             )
-
-        sums = {}
+            latest.append(partial[step, group[0] // half])
+
+        first, second, third = gathers
+        for gather in gathers:
+            gather.relay()
+        gathered.update({step: gather.whole() for step, gather in enumerate(gathers)})
+        multiply(0, near, second.beside, second.over)
+        finish(0, near, third.beside, second.out, second.over_beside)
+        cross_across = after(cross_across, latest[-1], second.out_beside, third.over)
+        arrived = spread_near({0: cross_across})
+        cross_pieces.update({half + place: arrived[place] for place in near})
+        multiply(0, far[:1], gathered[1])
+        multiply(0, far[1:])
+        multiply(1, near)
+        finish(0, far, third.out, third.over_beside)
+        multiply(1, far)
+        finish(1, near)
+        linear(0, near)
+        multiply(2, near)
+        finish(1, far)
+        multiply(2, far)
+        linear(1, near)
+        finish(2, near + far)
+        linear_across = after(linear_across, latest[-1])
+        arrived = spread_near({0: linear_across})
+        linear_pieces.update({half + place: arrived[place] for place in near})
+        linear(2, near)
         for step in chunks:
-            last = step == chunks[-1]
-            if step:
-                gathered[step] = after(gathered[step], *sums[step - 1, 0].begun)
-            sent = multiply(step, near)
-            if not step:
-                cross_across = after(cross_across, *sent)
-                arrived = spread_near({0: cross_across})
-                cross_pieces.update({half + place: arrived[place] for place in near})
-            sent = multiply(step, far)
-            if last:
-                linear_across = after(linear_across, *sent)
-                arrived = spread_near({0: linear_across})
-                linear_pieces.update({half + place: arrived[place] for place in near})
-                for past in range(step):
-                    sums[past, 1] = LineSum(linear(past, far), col, n_col)
-            finish(step, near + far)
-            if last and step:
-                mine[step, 0] = after(mine[step, 0], *sums[step - 1, 1].begun[:2])
-            sums[step, 0] = LineSum(linear(step, near), col, n_col)
-            if last:
-                sums[step, 1] = LineSum(linear(step, far), col, n_col)
+            linear(step, far)
 
         out = jnp.zeros((shard_rows, mixed_width * n_batch), jnp.bfloat16)
-        for step in chunks:
-            for group in range(2):
+        for group in range(2):
+            for step in chunks:
+                summed = lax.psum_scatter(
+                    partial[step, group], "col", scatter_dimension=0, tiled=True
+                )
                 first = ((batch // half) ^ group) * half * mixed_width
                 bias = lax.dynamic_slice_in_dim(linear_bias, first, half * mixed_width)
                 out = lax.dynamic_update_slice(
-                    out,
-                    (sums[step, group].end() + bias).astype(jnp.bfloat16),
-                    (starts[step], first),
+                    out, (added(summed) + bias).astype(jnp.bfloat16), (starts[step], first)
                 )
         return out
 

time: 481 us -> 515 us (1.071)
  Pallas kernels: 96.1 us -> 144 us
  starting transfers between devices: 105 us -> 71.8 us
  local copies, waits for them, and re-layouts: 23.2 us -> 45.3 us
    reduce_scatter x0 -> x6, waiting for transfers between devices: none -> 94.9 us  [on_device(): lax.psum_scatter(partial[step, group], 'col', scatter_dimension=0, tiled=...]
    all_gather x2 -> x0, waiting for transfers between devices: 74.8 us -> none  [on_device(): lax.all_gather(features[first:last], 'col', axis=0, tiled=True)]
    ppermute x32 -> x27, starting transfers between devices: 83.5 us -> 42.4 us  [the longest x12 15.6 us: multiply(): lax.ppermute(products[step, apart], ('row', 'col'), pairs)]
    pallas_call x8 -> x12, Pallas kernels: 34.3 us -> 60.5 us  [cross_product(): pl.pallas_call(cross_kernel, out_shape=jax.ShapeDtypeStruct((rows, column...]
    ppermute x32 -> x27, waiting for transfers between devices: 105 us -> 82.8 us  [the longest x3 28.7 us: relay(): self.out_beside = lax.ppermute(self.over_beside, 'col', outward)]
    unnamed x84 -> x118, local copies, waits for them, and re-layouts: 11.7 us -> 28.9 us
    pallas_call x4 -> x6, Pallas kernels: 38.5 us -> 50.1 us  [linear_product(): pl.pallas_call(functools.partial(linear_kernel, count, per_piece), out_sh...]
    ppermute x8 -> x12, starting transfers between devices: 16.1 us -> 27.1 us  [finish(): lax.ppermute(crossed, ('row', 'col'), [(to, source) for source, to in pai...]
  transfers between devices with their start and end apart: 48 -> 51, of which waited for: 20 -> 19; matrix products, arithmetic and copies ran while one was open for 6% -> 7% of each run, Pallas kernels for 20% -> 28%
where the time goes in v3:
time: 515 us; the launch traced here: 511 us
  waiting for transfers between devices  208 us (40%)
  Pallas kernels  144 us (28%)
  starting transfers between devices  71.8 us (14%)
  local copies, waits for them, and re-layouts  45.3 us (9%)
  other arithmetic  24.5 us (5%)
  between operations  17.1 us (3%)
    reduce_scatter x6, waiting for transfers between devices, on_device(): lax.psum_scatter(partial[step, group], 'col', scatter_dimension=0, tiled=...  94.9 us
    pallas_call x12, Pallas kernels, cross_product(): pl.pallas_call(cross_kernel, out_shape=jax.ShapeDtypeStruct((rows, column...  60.5 us
    pallas_call x6, Pallas kernels, linear_product(): pl.pallas_call(functools.partial(linear_kernel, count, per_piece), out_sh...  50.1 us
    pallas_call x12, Pallas kernels, finish_cross(): pl.pallas_call(finish_kernel, out_shape=jax.ShapeDtypeStruct((rows, colum...  33.3 us
    ppermute x12, waiting for transfers between devices, finish(): lax.ppermute(crossed, ('row', 'col'), [(to, source) for source, to in pai...  30.5 us
    unnamed x118, local copies, waits for them, and re-layouts  28.9 us
    ppermute x3, waiting for transfers between devices, relay(): self.out_beside = lax.ppermute(self.over_beside, 'col', outward)  28.7 us
    ppermute x12, starting transfers between devices, finish(): lax.ppermute(crossed, ('row', 'col'), [(to, source) for source, to in pai...  27.1 us
  transfers between devices with their start and end apart: 51, of which 19 were waited for; matrix products, arithmetic and copies ran while one was open for 7% of the time, Pallas kernels for 28%

profile of v3, /device:TPU:0, one launch (start us, length us, event | category | flops | bytes accessed | tf_op | source)
XLA Modules:
  0.0 510.9 jit_solution(13055578824528458440)
XLA Ops:
  31.7 11.5 %collective-permute-done = bf16[96,4096]{1,0:T(8,128)(2,1)} collective-permute-done((bf16[96,4096]{1,0:T(8,128)(2,1)}, bf16[96,4096]{1,0:T(8,128)(2,1)}, u32[]{:S(2)}, u32[]{:S(2)}) %collective-permute-start) | collective-permute-done | bytes 786464 | tf_op jit(solution)/shard_map/ppermute | solution.py:166
  58.1 13.1 %collective-permute-done.8 = bf16[96,4096]{1,0:T(8,128)(2,1)S(1)} collective-permute-done((bf16[96,4096]{1,0:T(8,128)(2,1)}, bf16[96,4096]{1,0:T(8,128)(2,1)S(1)}, u32[]{:S(2)}, u32[]{:S(2)}) %collective-permute-start.8) | collective-permute-done | bytes 786464 | tf_op jit(solution)/shard_map/ppermute | solution.py:166
  72.7 8.8 %collective-permute-done.6 = bf16[64,4096]{1,0:T(8,128)(2,1)S(1)} collective-permute-done((bf16[64,4096]{1,0:T(8,128)(2,1)S(1)}, bf16[64,4096]{1,0:T(8,128)(2,1)S(1)}, u32[]{:S(2)}, u32[]{:S(2)}) %collective-permute-start.6) | collective-permute-done | bytes 524320 | tf_op jit(solution)/shard_map/ppermute | solution.py:173
  93.6 10.4 %collective-permute-done.9 = bf16[96,4096]{1,0:T(8,128)(2,1)S(1)} collective-permute-done((bf16[96,4096]{1,0:T(8,128)(2,1)S(1)}, bf16[96,4096]{1,0:T(8,128)(2,1)S(1)}, u32[]{:S(2)}, u32[]{:S(2)}) %collective-permute-start.9) | collective-permute-done | bytes 786464 | tf_op jit(solution)/shard_map/ppermute | solution.py:171
  129.9 7.0 %shard_map.68.own = bf16[256,512]{1,0:T(8,128)(2,1)S(1)} custom-call(s32[9]{0:T(128)S(1)} %pad_add_fusion.3.meta, bf16[256,4096]{1,0:T(8,128)(2,1)} %select_dynamic-update-slice_fusion.4.samples, bf16[4096,512]{1,0:T(8,128)(2,1)} %collective-permute-done.14.weight), custom_call_target="tpu_custom_call" | custom-call | flops 536870912 | bytes 3407872 | tf_op jit(solution)/shard_map/pallas_call | solution.py:38
  138.3 6.2 %shard_map.69.own = bf16[256,512]{1,0:T(8,128)(2,1)} custom-call(s32[9]{0:T(128)S(1)} %pad_add_fusion.2.meta, bf16[256,4096]{1,0:T(8,128)(2,1)} %select_dynamic-update-slice_fusion.4.samples, bf16[4096,512]{1,0:T(8,128)(2,1)} %collective-permute-done.16.weight), custom_call_target="tpu_custom_call" | custom-call | flops 536870912 | bytes 3407872 | tf_op jit(solution)/shard_map/pallas_call | solution.py:38
  161.6 10.2 %collective-permute-start.23 = (bf16[256,512]{1,0:T(8,128)(2,1)S(1)}, bf16[256,512]{1,0:T(8,128)(2,1)}, u32[]{:S(2)}, u32[]{:S(2)}) collective-permute-start(bf16[256,512]{1,0:T(8,128)(2,1)S(1)} %copy-done.10), channel_id=1, source_target_pairs={{0,16},{4,20},{24,8},{28,12},{1,17},{5,21},{25,9},{29,13},{2,18},{... | collective-permute-start | bytes 786440 | tf_op jit(solution)/shard_map/ppermute | solution.py:295
  185.1 6.6 %shard_map.74.own = bf16[384,512]{1,0:T(8,128)(2,1)S(1)} custom-call(s32[9]{0:T(128)S(1)} %pad_add_fusion.3.meta, bf16[384,4096]{1,0:T(8,128)(2,1)S(1)} %select_dynamic-update-slice_fusion.2.samples, bf16[4096,512]{1,0:T(8,128)(2,1)} %collective-permute-done.14.weight), custom_call_target="tpu_custom_call" | custom-call | flops 805306368 | bytes 4063232 | tf_op jit(solution)/shard_map/pallas_call | solution.py:38
  205.9 7.9 %shard_map.78 = bf16[256,2048]{1,0:T(8,128)(2,1)} custom-call(s32[7]{0:T(128)S(1)} %stack.43.meta, bf16[256,512]{1,0:T(8,128)(2,1)S(1)} %copy-done.10, bf16[256,512]{1,0:T(8,128)(2,1)S(1)} %copy-done.11, bf16[256,512]{1,0:T(8,128)(2,1)S(1)} %copy-done.13, bf16[256,512]{1,0:T(8,128)(2,1)S(1)} %copy-done.15, bf16[256,512]{1,0:T(8,128)(2,1)} %collective-permute-done.23.refs_4_, ...), custom_call_target="tpu_custom_call" | custom-call | flops 2147483648 | bytes 11534336 | tf_op jit(solution)/shard_map/pallas_call | solution.py:105
  218.9 16.7 %collective-permute-done.28 = bf16[96,4096]{1,0:T(8,128)(2,1)} collective-permute-done((bf16[96,4096]{1,0:T(8,128)(2,1)}, bf16[96,4096]{1,0:T(8,128)(2,1)}, u32[]{:S(2)}, u32[]{:S(2)}) %collective-permute-start.28) | collective-permute-done | bytes 786464 | tf_op jit(solution)/shard_map/ppermute | solution.py:173
  257.6 7.0 %shard_map.83.own = bf16[384,512]{1,0:T(8,128)(2,1)S(1)} custom-call(s32[9]{0:T(128)S(1)} %pad_add_fusion.3.meta, bf16[384,4096]{1,0:T(8,128)(2,1)} %select_dynamic-update-slice_fusion.samples, bf16[4096,512]{1,0:T(8,128)(2,1)} %collective-permute-done.14.weight), custom_call_target="tpu_custom_call" | custom-call | flops 805306368 | bytes 4063232 | tf_op jit(solution)/shard_map/pallas_call | solution.py:38
  265.3 5.9 %shard_map.84.own = bf16[384,512]{1,0:T(8,128)(2,1)S(1)} custom-call(s32[9]{0:T(128)S(1)} %pad_add_fusion.2.meta, bf16[384,4096]{1,0:T(8,128)(2,1)} %select_dynamic-update-slice_fusion.samples, bf16[4096,512]{1,0:T(8,128)(2,1)} %collective-permute-done.16.weight), custom_call_target="tpu_custom_call" | custom-call | flops 805306368 | bytes 4063232 | tf_op jit(solution)/shard_map/pallas_call | solution.py:38
  275.5 8.5 %shard_map.85 = bf16[384,2048]{1,0:T(8,128)(2,1)} custom-call(s32[7]{0:T(128)S(1)} %stack.43.meta, bf16[384,512]{1,0:T(8,128)(2,1)S(1)} %copy-done.1, bf16[384,512]{1,0:T(8,128)(2,1)S(1)} %copy-done.2, bf16[384,512]{1,0:T(8,128)(2,1)S(1)} %copy-done.3, bf16[384,512]{1,0:T(8,128)(2,1)S(1)} %copy-done.4, bf16[384,512]{1,0:T(8,128)(2,1)S(1)} %copy-done.21, ...), custom_call_target="tpu_custom_call" | custom-call | flops 3221225472 | bytes 13107200 | tf_op jit(solution)/shard_map/pallas_call | solution.py:105
  290.8 9.0 %collective-permute-done.35.came = bf16[384,512]{1,0:T(8,128)(2,1)S(1)} collective-permute-done((bf16[384,512]{1,0:T(8,128)(2,1)}, bf16[384,512]{1,0:T(8,128)(2,1)S(1)}, u32[]{:S(2)}, u32[]{:S(2)}) %collective-permute-start.35) | collective-permute-done | bytes 393248 | tf_op jit(solution)/shard_map/ppermute | solution.py:283
  329.3 8.3 %collective-permute-done.41.refs_6_ = bf16[384,512]{1,0:T(8,128)(2,1)S(1)} collective-permute-done((bf16[384,512]{1,0:T(8,128)(2,1)S(1)}, bf16[384,512]{1,0:T(8,128)(2,1)S(1)}, u32[]{:S(2)}, u32[]{:S(2)}) %collective-permute-start.41) | collective-permute-done | bytes 393248 | tf_op jit(solution)/shard_map/ppermute | solution.py:295
  337.6 8.4 %collective-permute-done.40.refs_5_ = bf16[384,512]{1,0:T(8,128)(2,1)S(1)} collective-permute-done((bf16[384,512]{1,0:T(8,128)(2,1)S(1)}, bf16[384,512]{1,0:T(8,128)(2,1)S(1)}, u32[]{:S(2)}, u32[]{:S(2)}) %collective-permute-start.40) | collective-permute-done | bytes 393248 | tf_op jit(solution)/shard_map/ppermute | solution.py:295
  346.0 8.0 %collective-permute-done.39.refs_4_ = bf16[384,512]{1,0:T(8,128)(2,1)S(1)} collective-permute-done((bf16[384,512]{1,0:T(8,128)(2,1)S(1)}, bf16[384,512]{1,0:T(8,128)(2,1)S(1)}, u32[]{:S(2)}, u32[]{:S(2)}) %collective-permute-start.39) | collective-permute-done | bytes 393248 | tf_op jit(solution)/shard_map/ppermute | solution.py:295
  355.1 8.5 %shard_map.90 = bf16[384,2048]{1,0:T(8,128)(2,1)} custom-call(s32[7]{0:T(128)S(1)} %stack.43.meta, bf16[384,512]{1,0:T(8,128)(2,1)S(1)} %copy-done.5, bf16[384,512]{1,0:T(8,128)(2,1)S(1)} %copy-done.6, bf16[384,512]{1,0:T(8,128)(2,1)S(1)} %copy-done.7, bf16[384,512]{1,0:T(8,128)(2,1)S(1)} %copy-done.8, bf16[384,512]{1,0:T(8,128)(2,1)S(1)} %collective-permute-done.39.refs_4_, ...), custom_call_target="tpu_custom_call" | custom-call | flops 3221225472 | bytes 13107200 | tf_op jit(solution)/shard_map/pallas_call | solution.py:105
  369.6 8.1 %shard_map.91 = bf16[256,2048]{1,0:T(8,128)(2,1)} custom-call(s32[7]{0:T(128)S(1)} %stack.43.meta, bf16[256,512]{1,0:T(8,128)(2,1)S(1)} %copy-done.10, bf16[256,512]{1,0:T(8,128)(2,1)S(1)} %copy-done.12, bf16[256,512]{1,0:T(8,128)(2,1)S(1)} %copy-done.14, bf16[256,512]{1,0:T(8,128)(2,1)S(1)} %copy-done.16, bf16[256,512]{1,0:T(8,128)(2,1)} %collective-permute-done.23.refs_4_, ...), custom_call_target="tpu_custom_call" | custom-call | flops 2147483648 | bytes 11534336 | tf_op jit(solution)/shard_map/pallas_call | solution.py:105
  381.8 8.5 %shard_map.92 = bf16[384,2048]{1,0:T(8,128)(2,1)} custom-call(s32[7]{0:T(128)S(1)} %stack.43.meta, bf16[384,512]{1,0:T(8,128)(2,1)S(1)} %copy-done.1, bf16[384,512]{1,0:T(8,128)(2,1)S(1)} %copy-done.2, bf16[384,512]{1,0:T(8,128)(2,1)S(1)} %copy-done.3, bf16[384,512]{1,0:T(8,128)(2,1)S(1)} %copy-done.4, bf16[384,512]{1,0:T(8,128)(2,1)S(1)} %copy-done.22, ...), custom_call_target="tpu_custom_call" | custom-call | flops 3221225472 | bytes 13107200 | tf_op jit(solution)/shard_map/pallas_call | solution.py:105
  393.4 8.5 %shard_map.93 = bf16[384,2048]{1,0:T(8,128)(2,1)} custom-call(s32[7]{0:T(128)S(1)} %stack.43.meta, bf16[384,512]{1,0:T(8,128)(2,1)S(1)} %copy-done.5, bf16[384,512]{1,0:T(8,128)(2,1)S(1)} %copy-done.6, bf16[384,512]{1,0:T(8,128)(2,1)S(1)} %copy-done.7, bf16[384,512]{1,0:T(8,128)(2,1)S(1)} %copy-done.9, bf16[384,512]{1,0:T(8,128)(2,1)S(1)} %copy-done.34, ...), custom_call_target="tpu_custom_call" | custom-call | flops 3221225472 | bytes 13107200 | tf_op jit(solution)/shard_map/pallas_call | solution.py:105
  405.2 24.4 %reduce-scatter.13.cloned.1.call-done = bf16[64,2048]{1,0:T(8,128)(2,1)} async-done(((bf16[256,2048]{1,0:T(8,128)(2,1)}), bf16[64,2048]{1,0:T(8,128)(2,1)}) %reduce-scatter.13.cloned.1.call-update) | async-done | bytes 262160 | tf_op jit(solution)/shard_map/reduce_scatter | solution.py:350
  430.6 35.1 %reduce-scatter.15.cloned.1.call-done = bf16[96,2048]{1,0:T(8,128)(2,1)} async-done(((bf16[384,2048]{1,0:T(8,128)(2,1)}), bf16[96,2048]{1,0:T(8,128)(2,1)}) %reduce-scatter.15.cloned.1.call-update) | async-done | bytes 393232 | tf_op jit(solution)/shard_map/reduce_scatter | solution.py:350
  466.8 35.4 %reduce-scatter.17.cloned.1.call-done = bf16[96,2048]{1,0:T(8,128)(2,1)} async-done(((bf16[384,2048]{1,0:T(8,128)(2,1)}), bf16[96,2048]{1,0:T(8,128)(2,1)}) %reduce-scatter.17.cloned.1.call-update) | async-done | bytes 393232 | tf_op jit(solution)/shard_map/reduce_scatter | solution.py:350
  (284 shorter events, 211.8 us)
Async XLA Ops:
  6.5 395.5 %reduce-scatter.7.cloned.1.call-start = ((), (), s32[]{:S(2)}) async-start(), calls=%async_computation.6 | async-start | bytes 1310720 | tf_op jit(solution)/shard_map/reduce_scatter | solution.py:350
  14.7 74.2 %collective-permute-start.7 = (bf16[4096,512]{1,0:T(8,128)(2,1)}, bf16[4096,512]{1,0:T(8,128)(2,1)}, u32[]{:S(2)}, u32[]{:S(2)}) collective-permute-start(bf16[4096,512]{1,0:T(8,128)(2,1)} %weight.5), channel_id=1, source_target_pairs={{0,1},{1,0},{2,3},{3,2},{4,5},{5,4},{6,7},{7,6},{8,9},{9,8},{10,11... | collective-permute-start | bytes 12582920 | tf_op jit(solution)/shard_map/ppermute | solution.py:216
  14.7 104.5 %collective-permute-start.14 = (bf16[4096,512]{1,0:T(8,128)(2,1)}, bf16[4096,512]{1,0:T(8,128)(2,1)}, u32[]{:S(2)}, u32[]{:S(2)}) collective-permute-start(bf16[4096,512]{1,0:T(8,128)(2,1)} %weight.5), channel_id=1, source_target_pairs={{0,2},{1,3},{2,0},{3,1},{4,6},{5,7},{6,4},{7,5},{8,10},{9,11},{10,... | collective-permute-start | bytes 12582920 | tf_op jit(solution)/shard_map/ppermute | solution.py:216
  54.3 28.6 %collective-permute-start.10 = (bf16[96,4096]{1,0:T(8,128)(2,1)}, bf16[96,4096]{1,0:T(8,128)(2,1)}, u32[]{:S(2)}, u32[]{:S(2)}) collective-permute-start(bf16[96,4096]{1,0:T(8,128)(2,1)} %collective-permute-done), channel_id=1, source_target_pairs={{4,8},{8,4},{5,9},{9,5},{6,10},{10,6},{7,11},{11,7},{20,24},{24,20... | collective-permute-start | bytes 2359304 | tf_op jit(solution)/shard_map/ppermute | solution.py:172
  71.1 44.9 %collective-permute-start.15 = (bf16[96,4096]{1,0:T(8,128)(2,1)}, bf16[96,4096]{1,0:T(8,128)(2,1)}, u32[]{:S(2)}, u32[]{:S(2)}) collective-permute-start(bf16[96,4096]{1,0:T(8,128)(2,1)} %get-tuple-element.40), channel_id=1, source_target_pairs={{4,8},{8,4},{5,9},{9,5},{6,10},{10,6},{7,11},{11,7},{20,24},{24,20... | collective-permute-start | bytes 2359304 | tf_op jit(solution)/shard_map/ppermute | solution.py:167
  82.8 36.4 %collective-permute-start.13 = (bf16[96,4096]{1,0:T(8,128)(2,1)}, bf16[96,4096]{1,0:T(8,128)(2,1)}, u32[]{:S(2)}, u32[]{:S(2)}) collective-permute-start(bf16[96,4096]{1,0:T(8,128)(2,1)} %collective-permute-done.10), channel_id=1, source_target_pairs={{4,0},{8,12},{5,1},{9,13},{6,2},{10,14},{7,3},{11,15},{20,16},{24,... | collective-permute-start | bytes 2359304 | tf_op jit(solution)/shard_map/ppermute | solution.py:173
  119.2 85.3 %collective-permute-start.27 = (bf16[2048,1024]{1,0:T(8,128)(2,1)}, bf16[2048,1024]{1,0:T(8,128)(2,1)}, u32[]{:S(2)}, u32[]{:S(2)}) collective-permute-start(bf16[2048,1024]{1,0:T(8,128)(2,1)} %refs_8_.5), channel_id=1, source_target_pairs={{0,1},{1,0},{2,3},{3,2},{4,5},{5,4},{6,7},{7,6},{8,9},{9,8},{10,11... | collective-permute-start | bytes 12582920 | tf_op jit(solution)/shard_map/ppermute | solution.py:216
  126.8 28.6 %collective-permute-start.18 = (bf16[96,4096]{1,0:T(8,128)(2,1)}, bf16[96,4096]{1,0:T(8,128)(2,1)}, u32[]{:S(2)}, u32[]{:S(2)}) collective-permute-start(bf16[96,4096]{1,0:T(8,128)(2,1)} %copy-done.46), channel_id=1, source_target_pairs={{4,8},{8,4},{5,9},{9,5},{6,10},{10,6},{7,11},{11,7},{20,24},{24,20... | collective-permute-start | bytes 2359304 | tf_op jit(solution)/shard_map/ppermute | solution.py:172
  144.5 29.9 %collective-permute-start.20 = (bf16[256,512]{1,0:T(8,128)(2,1)}, bf16[256,512]{1,0:T(8,128)(2,1)}, u32[]{:S(2)}, u32[]{:S(2)}) collective-permute-start(bf16[256,512]{1,0:T(8,128)(2,1)} %shard_map.69.own), channel_id=1, source_target_pairs={{16,0},{20,4},{8,24},{12,28},{17,1},{21,5},{9,25},{13,29},{18,2},{... | collective-permute-start | bytes 786440 | tf_op jit(solution)/shard_map/ppermute | solution.py:283
  161.6 43.0 %collective-permute-start.23 = (bf16[256,512]{1,0:T(8,128)(2,1)S(1)}, bf16[256,512]{1,0:T(8,128)(2,1)}, u32[]{:S(2)}, u32[]{:S(2)}) collective-permute-start(bf16[256,512]{1,0:T(8,128)(2,1)S(1)} %copy-done.10), channel_id=1, source_target_pairs={{0,16},{4,20},{24,8},{28,12},{1,17},{5,21},{25,9},{29,13},{2,18},{... | collective-permute-start | bytes 786440 | tf_op jit(solution)/shard_map/ppermute | solution.py:295
  174.4 31.4 %collective-permute-start.24 = (bf16[256,512]{1,0:T(8,128)(2,1)}, bf16[256,512]{1,0:T(8,128)(2,1)}, u32[]{:S(2)}, u32[]{:S(2)}) collective-permute-start(bf16[256,512]{1,0:T(8,128)(2,1)} %shard_map.67.refs_1_), channel_id=1, source_target_pairs={{0,16},{4,20},{24,8},{28,12},{1,17},{5,21},{25,9},{29,13},{2,18},{... | collective-permute-start | bytes 786440 | tf_op jit(solution)/shard_map/ppermute | solution.py:295
  204.5 113.4 %collective-permute-start.43 = (bf16[2048,1024]{1,0:T(8,128)(2,1)}, bf16[2048,1024]{1,0:T(8,128)(2,1)}, u32[]{:S(2)}, u32[]{:S(2)}) collective-permute-start(bf16[2048,1024]{1,0:T(8,128)(2,1)} %refs_8_.5), channel_id=1, source_target_pairs={{0,2},{1,3},{2,0},{3,1},{4,6},{5,7},{6,4},{7,5},{8,10},{9,11},{10,... | collective-permute-start | bytes 12582920 | tf_op jit(solution)/shard_map/ppermute | solution.py:216
  204.6 31.0 %collective-permute-start.28 = (bf16[96,4096]{1,0:T(8,128)(2,1)}, bf16[96,4096]{1,0:T(8,128)(2,1)}, u32[]{:S(2)}, u32[]{:S(2)}) collective-permute-start(bf16[96,4096]{1,0:T(8,128)(2,1)} %collective-permute-done.18), channel_id=1, source_target_pairs={{4,0},{8,12},{5,1},{9,13},{6,2},{10,14},{7,3},{11,15},{20,16},{24,... | collective-permute-start | bytes 2359304 | tf_op jit(solution)/shard_map/ppermute | solution.py:173
  213.9 189.1 %reduce-scatter.9.cloned.1.call-start = ((), (), s32[]{:S(2)}) async-start(), calls=%async_computation.7 | async-start | bytes 1966080 | tf_op jit(solution)/shard_map/reduce_scatter | solution.py:350
  216.3 32.8 %collective-permute-start.29 = (bf16[384,512]{1,0:T(8,128)(2,1)S(1)}, bf16[384,512]{1,0:T(8,128)(2,1)}, u32[]{:S(2)}, u32[]{:S(2)}) collective-permute-start(bf16[384,512]{1,0:T(8,128)(2,1)S(1)} %copy-done.38), channel_id=1, source_target_pairs={{16,0},{20,4},{8,24},{12,28},{17,1},{21,5},{9,25},{13,29},{18,2},{... | collective-permute-start | bytes 1179656 | tf_op jit(solution)/shard_map/ppermute | solution.py:283
  217.6 34.4 %collective-permute-start.30 = (bf16[384,512]{1,0:T(8,128)(2,1)S(1)}, bf16[384,512]{1,0:T(8,128)(2,1)}, u32[]{:S(2)}, u32[]{:S(2)}) collective-permute-start(bf16[384,512]{1,0:T(8,128)(2,1)S(1)} %copy-done.36), channel_id=1, source_target_pairs={{16,0},{20,4},{8,24},{12,28},{17,1},{21,5},{9,25},{13,29},{18,2},{... | collective-permute-start | bytes 1179656 | tf_op jit(solution)/shard_map/ppermute | solution.py:283
  237.8 34.2 %collective-permute-start.32 = (bf16[384,512]{1,0:T(8,128)(2,1)S(1)}, bf16[384,512]{1,0:T(8,128)(2,1)S(1)}, u32[]{:S(2)}, u32[]{:S(2)}) collective-permute-start(bf16[384,512]{1,0:T(8,128)(2,1)S(1)} %copy-done.2), channel_id=1, source_target_pairs={{0,16},{4,20},{24,8},{28,12},{1,17},{5,21},{25,9},{29,13},{2,18},{... | collective-permute-start | bytes 1179656 | tf_op jit(solution)/shard_map/ppermute | solution.py:295
  239.1 33.6 %collective-permute-start.31 = (bf16[384,512]{1,0:T(8,128)(2,1)S(1)}, bf16[384,512]{1,0:T(8,128)(2,1)S(1)}, u32[]{:S(2)}, u32[]{:S(2)}) collective-permute-start(bf16[384,512]{1,0:T(8,128)(2,1)S(1)} %copy-done.1), channel_id=1, source_target_pairs={{0,16},{4,20},{24,8},{28,12},{1,17},{5,21},{25,9},{29,13},{2,18},{... | collective-permute-start | bytes 1179656 | tf_op jit(solution)/shard_map/ppermute | solution.py:295
  285.5 118.6 %reduce-scatter.11.cloned.1.call-start = ((), (), s32[]{:S(2)}) async-start(), calls=%async_computation.8 | async-start | bytes 1966080 | tf_op jit(solution)/shard_map/reduce_scatter | solution.py:350
  318.0 48.7 %collective-permute-start.44 = (bf16[2048,1024]{1,0:T(8,128)(2,1)}, bf16[2048,1024]{1,0:T(8,128)(2,1)}, u32[]{:S(2)}, u32[]{:S(2)}) collective-permute-start(bf16[2048,1024]{1,0:T(8,128)(2,1)} %collective-permute-done.43.refs_8_), channel_id=1, source_target_pairs={{0,1},{1,0},{2,3},{3,2},{4,5},{5,4},{6,7},{7,6},{8,9},{9,8},{10,11... | collective-permute-start | bytes 12582920 | tf_op jit(solution)/shard_map/ppermute | solution.py:216
  322.2 31.8 %collective-permute-start.39 = (bf16[384,512]{1,0:T(8,128)(2,1)S(1)}, bf16[384,512]{1,0:T(8,128)(2,1)S(1)}, u32[]{:S(2)}, u32[]{:S(2)}) collective-permute-start(bf16[384,512]{1,0:T(8,128)(2,1)S(1)} %copy-done.5), channel_id=1, source_target_pairs={{0,16},{4,20},{24,8},{28,12},{1,17},{5,21},{25,9},{29,13},{2,18},{... | collective-permute-start | bytes 1179656 | tf_op jit(solution)/shard_map/ppermute | solution.py:295
  366.6 63.0 %reduce-scatter.13.cloned.1.call-start = ((), (), s32[]{:S(2)}) async-start(), calls=%async_computation.9 | async-start | bytes 1310720 | tf_op jit(solution)/shard_map/reduce_scatter | solution.py:350
  377.7 88.1 %reduce-scatter.15.cloned.1.call-start = ((), (), s32[]{:S(2)}) async-start(), calls=%async_computation.10 | async-start | bytes 1966080 | tf_op jit(solution)/shard_map/reduce_scatter | solution.py:350
  390.3 111.9 %reduce-scatter.17.cloned.1.call-start = ((), (), s32[]{:S(2)}) async-start(), calls=%async_computation.11 | async-start | bytes 1966080 | tf_op jit(solution)/shard_map/reduce_scatter | solution.py:350
  (86 other events, 911.1 us)
Sparse Core Ops, SparseCore 0:
  214.0 29.2 reduce-scatter.6
  285.7 34.2 reduce-scatter.8
  366.8 34.3 reduce-scatter.10
  403.4 26.1 reduce-scatter.12
  431.7 33.9 reduce-scatter.14
  467.9 34.2 reduce-scatter.16

commit v4 on v2

v4 whole, which is shorter than its diff:
```python
import functools

import jax
import jax.numpy as jnp
from jax import lax
from jax.experimental import pallas as pl
from jax.experimental.pallas import tpu as pltpu
from jax.sharding import PartitionSpec as P

SHARES = (4, 4)
VMEM_BYTES = 48 * 2**20


def far_and_near(size, bit):
    return [(place, place ^ bit) for place in range(size)]


def cross_kernel(steps, meta, samples, *refs):
    weights, out, total = refs[:-2], refs[-2], refs[-1]
    step = lax.rem(pl.program_id(0), steps)
    piece = pl.program_id(0) // steps

    @pl.when(step == 0)
    def _():
        total[...] = jnp.zeros_like(total)

    for place, weight in enumerate(weights):

        @pl.when((piece == place) & (step < meta[place * (steps + 1)]))
        def _():
            total[...] += jnp.dot(samples[...], weight[...], preferred_element_type=jnp.float32)

    @pl.when(step == steps - 1)
    def _():
        out[...] = total[...].astype(out.dtype)


def cross_product(meta, samples, weights, block):
    rows, depth = samples.shape
    columns = weights[0].shape[1]
    steps = depth // block

    def listed(place, step, meta):
        return meta[place * (steps + 1) + 1 + step]

    def weight_spec(place):
        return pl.BlockSpec(
            (block, columns),
            lambda i, meta: (listed(place, jnp.clip(i - place * steps, 0, steps - 1), meta), 0),
        )

    return pl.pallas_call(
        functools.partial(cross_kernel, steps),
        out_shape=jax.ShapeDtypeStruct((rows, columns * len(weights)), jnp.bfloat16),
        grid_spec=pltpu.PrefetchScalarGridSpec(
            num_scalar_prefetch=1,
            grid=(len(weights) * steps,),
            in_specs=[
                pl.BlockSpec(
                    (rows, block), lambda i, meta: (0, listed(i // steps, lax.rem(i, steps), meta))
                ),
                *(weight_spec(place) for place in range(len(weights))),
            ],
            out_specs=pl.BlockSpec((rows, columns), lambda i, meta: (0, i // steps)),
            scratch_shapes=[pltpu.VMEM((rows, columns), jnp.float32)],
        ),
        compiler_params=pltpu.CompilerParams(vmem_limit_bytes=VMEM_BYTES),
        cost_estimate=pl.CostEstimate(
            flops=rows * depth * columns * len(weights),
            bytes_accessed=(rows * depth + depth * columns + 2 * rows * columns) * len(weights),
            transcendentals=0,
        ),
    )(meta, samples, *weights)


def linear_kernel(groups, parts, per_piece, meta, *refs):
    mine, theirs = refs[:groups], refs[groups : 2 * groups]
    weights, out, joined, sems = refs[2 * groups : -3], refs[-3], refs[-2], refs[-1]
    step = pl.program_id(0)
    pieces = sems.shape[0]
    width = joined.shape[1] // pieces
    in_group = pieces // groups

    @pl.when(step == 0)
    def _():
        def copy(sources, apart):
            columns = pl.ds(pl.multiple_of(meta[1 + apart] * width, width), width)
            source = sources[apart // in_group]
            first = apart % in_group * width
            return pltpu.make_async_copy(
                source.at[:, pl.ds(first, width)], joined.at[:, columns], sems.at[apart]
            )

        @pl.when(meta[0] == 1)
        def _():
            for apart in range(pieces):
                copy(mine, apart).start()
            for apart in range(pieces):
                copy(mine, apart).wait()

        @pl.when(meta[0] == 0)
        def _():
            for apart in range(pieces):
                copy(theirs, apart).start()
            for apart in range(pieces):
                copy(theirs, apart).wait()

    depth = joined.shape[1] // parts
    for place in range(len(weights) // parts):

        @pl.when(step // per_piece == place)
        def _():
            total = jnp.dot(
                joined[:, :depth], weights[place * parts][...], preferred_element_type=jnp.float32
            )
            for part in range(1, parts):
                total += jnp.dot(
                    joined[:, part * depth : (part + 1) * depth],
                    weights[place * parts + part][...],
                    preferred_element_type=jnp.float32,
                )
            out[...] = total.astype(out.dtype)


def linear_product(meta, pieces, mine, theirs, weights):
    groups, parts = len(mine), len(weights[0])
    rows = mine[0].shape[0]
    depth, columns = weights[0][0].shape
    whole_depth = depth * parts
    tile = min(columns, 512)
    per_piece = columns // tile
    anywhere = pl.BlockSpec(memory_space=pl.ANY)

    def weight_spec(place):
        return pl.BlockSpec(
            (depth, tile),
            lambda i, meta: (0, jnp.clip(i - place * per_piece, 0, per_piece - 1)),
        )

    def out_index(i, meta):
        return 0, meta[1 + pieces + i // per_piece] * per_piece + i % per_piece

    return pl.pallas_call(
        functools.partial(linear_kernel, groups, parts, per_piece),
        out_shape=jax.ShapeDtypeStruct((rows, columns * len(weights)), jnp.bfloat16),
        grid_spec=pltpu.PrefetchScalarGridSpec(
            num_scalar_prefetch=1,
            grid=(per_piece * len(weights),),
            in_specs=[anywhere] * (2 * groups)
            + [weight_spec(place) for place in range(len(weights)) for _ in range(parts)],
            out_specs=pl.BlockSpec((rows, tile), out_index),
            scratch_shapes=[
                pltpu.VMEM((rows, whole_depth), jnp.bfloat16),
                pltpu.SemaphoreType.DMA((pieces,)),
            ],
        ),
        compiler_params=pltpu.CompilerParams(vmem_limit_bytes=VMEM_BYTES),
        cost_estimate=pl.CostEstimate(
            flops=2 * rows * whole_depth * columns * len(weights),
            bytes_accessed=2 * rows * whole_depth
            + 2 * (whole_depth + rows) * columns * len(weights),
            transcendentals=0,
        ),
    )(meta, *mine, *theirs, *(part for weight in weights for part in weight))


def after(value, *others):
    return lax.optimization_barrier((value, *others))[0]


def added(*terms):
    return sum(term.astype(jnp.float32) for term in terms)


def finish_kernel(meta, own, came, samples, bias, out):
    base = samples[...].astype(jnp.float32)
    hidden = own[...].astype(jnp.float32) + came[...].astype(jnp.float32)
    out[...] = (base * (hidden + bias[...]) + base).astype(out.dtype)


def finish_cross(meta, own, came, samples, bias, pieces):
    rows, columns = own.shape[0], own.shape[1] // pieces
    part = pl.BlockSpec((rows, columns), lambda i, meta: (0, i))
    return pl.pallas_call(
        finish_kernel,
        out_shape=jax.ShapeDtypeStruct(own.shape, jnp.bfloat16),
        grid_spec=pltpu.PrefetchScalarGridSpec(
            num_scalar_prefetch=1,
            grid=(pieces,),
            in_specs=[
                part,
                part,
                pl.BlockSpec((rows, columns), lambda i, meta: (0, meta[2 * i])),
                pl.BlockSpec((1, columns), lambda i, meta: (0, meta[2 * i + 1])),
            ],
            out_specs=part,
        ),
        compiler_params=pltpu.CompilerParams(vmem_limit_bytes=VMEM_BYTES),
        cost_estimate=pl.CostEstimate(
            flops=4 * rows * columns * pieces,
            bytes_accessed=8 * rows * columns * pieces,
            transcendentals=0,
        ),
    )(meta, own, came, samples, bias)


class LineSum:
    def __init__(self, partial, place, size):
        self.partial, self.place, self.size = partial, place, size
        self.rows = partial.shape[0] // size
        self.begun = []
        if size == 4:
            inward = [(0, 1), (3, 2)]
            self.begun = [lax.ppermute(self.part(i), "col", inward) for i in (3, 2, 1)]

    def part(self, if_lower):
        upper = self.place >= self.size // 2
        first = jnp.where(upper, self.size - 1 - if_lower, if_lower) * self.rows
        return lax.dynamic_slice_in_dim(self.partial, first, self.rows, 0)

    def end(self):
        if self.size != 4:
            summed = lax.psum_scatter(self.partial, "col", scatter_dimension=0, tiled=True)
            return summed.astype(jnp.float32)
        across, outward = [(1, 2), (2, 1)], [(1, 0), (2, 3)]
        from_3, from_2, from_1 = self.begun
        over_3 = lax.ppermute(added(self.part(3), from_3).astype(jnp.bfloat16), "col", across)
        over_2 = lax.ppermute(added(self.part(2), from_2).astype(jnp.bfloat16), "col", across)
        out_0 = lax.ppermute(added(self.part(0), over_3).astype(jnp.bfloat16), "col", outward)
        own = lax.dynamic_slice_in_dim(self.partial, self.place * self.rows, self.rows, 0)
        is_end = (self.place == 0) | (self.place == self.size - 1)
        return added(own) + jnp.where(is_end, added(out_0), added(from_1, over_2))


def build(mesh):
    n_row, n_col, n_batch = (mesh.shape[name] for name in ("row", "col", "batch"))

    def on_device(features, cross_weight, cross_bias, pattern, linear_weight, linear_bias):
        input_width, piece_width = cross_weight.shape
        width = input_width * n_row
        output_width = piece_width * n_batch
        mixed_width = linear_weight.shape[1]
        block = width // pattern.shape[0]
        in_blocks = input_width // block
        row, col, batch = (lax.axis_index(name) for name in ("row", "col", "batch"))
        half = n_batch // 2

        def to_batch(shard, bit):
            return lax.ppermute(shard, "batch", far_and_near(n_batch, bit))

        def spread_near(pieces):
            bit = half // 2
            while bit:
                for apart in list(pieces):
                    pieces[apart | bit] = to_batch(pieces[apart], bit)
                bit //= 2
            return pieces

        cross_across = to_batch(cross_weight, half)
        parts = jnp.split(linear_weight, 2, axis=0)
        linear_across = [to_batch(part, half) for part in parts]
        cross_pieces = spread_near({0: cross_weight})
        linear_pieces = {
            place: [piece] for place, piece in spread_near({0: linear_weight}).items()
        }

        shard_rows = features.shape[0]
        starts = [shard_rows * sum(SHARES[:i]) // sum(SHARES) for i in range(len(SHARES) + 1)]
        shards = [features[first:last] for first, last in zip(starts, starts[1:])]
        gathered = [lax.all_gather(shard, "col", axis=0, tiled=True) for shard in shards]

        def kept_list(apart):
            out_block = (col * n_batch + (batch ^ apart)) * piece_width // block
            kept = lax.dynamic_slice(pattern, (out_block, row * in_blocks), (1, in_blocks))[0]
            number = jnp.sum(kept)
            rank = jnp.cumsum(kept) - 1
            slots = jnp.minimum(jnp.arange(in_blocks), jnp.maximum(number - 1, 0))
            match = (rank[None, :] == slots[:, None]) & (kept[None, :] == 1)
            listed = jnp.sum(jnp.where(match, jnp.arange(in_blocks)[None, :], 0), axis=1)
            return jnp.concatenate([number[None], listed]).astype(jnp.int32)

        kept_lists = [kept_list(apart) for apart in range(n_batch)]

        def owner_of(column):
            return column * output_width // input_width

        is_owner = row == col * output_width // input_width
        turns = [
            [
                ((owner_of(c) + turn) % n_row * n_col + c, owner_of(c) * n_col + c)
                for c in range(n_col)
            ]
            for turn in range(1, n_row)
        ]
        first_base = jnp.where(is_owner, col * output_width - row * input_width, 0)

        chunks = range(len(SHARES))
        bias_row = cross_bias[None, :]
        near, far = 0, 1
        in_group = [list(range(half)), list(range(half, n_batch))]
        products, came, mine, theirs, partial = {}, {}, {}, {}, {}
        latest = []

        def in_turn(meta, *others):
            return after(meta.astype(jnp.int32), *latest[-1:], *others)

        def multiply(step, group, *others):
            lists = jnp.concatenate([kept_lists[apart] for apart in in_group[group]])
            product = cross_product(
                in_turn(lists, *others),
                gathered[step],
                [cross_pieces[apart] for apart in in_group[group]],
                block,
            )
            latest.append(product)
            sent = [lax.ppermute(product, ("row", "col"), pairs) for pairs in turns]
            products[step, group], came[step, group] = product, sum(sent[1:], sent[0])

        def finish(step, group, *others):
            places = []
            for apart in in_group[group]:
                places += [first_base // piece_width + (batch ^ apart), batch ^ apart]
            crossed = finish_cross(
                in_turn(jnp.stack(places), *others),
                products[step, group],
                came[step, group],
                gathered[step],
                bias_row,
                half,
            )
            latest.append(crossed)
            back = [
                lax.ppermute(crossed, ("row", "col"), [(to, source) for source, to in pairs])
                for pairs in turns
            ]
            mine[step, group], theirs[step, group] = crossed, sum(back[1:], back[0])

        meta = jnp.stack(
            [is_owner.astype(jnp.int32)]
            + [batch ^ place for place in range(n_batch)]
            + [(batch ^ place) % half for place in range(half)]
        )

        def linear(step, group, *others):
            product = linear_product(
                in_turn(meta, *others),
                n_batch,
                [mine[step, g] for g in (near, far)],
                [theirs[step, g] for g in (near, far)],
                [linear_pieces[apart] for apart in in_group[group]],
            )
            latest.append(product)
            partial[step, group] = product

        def spread_far_cross(*others):
            arrived = spread_near({0: after(cross_across, *others)})
            cross_pieces.update({half + place: arrived[place] for place in range(half)})

        def spread_far_linear():
            arrived = [spread_near({0: part}) for part in linear_across]
            for place in range(half):
                linear_pieces[half + place] = [part[place] for part in arrived]

        begun = {}
        multiply(0, near)
        spread_far_cross(latest[-1])
        multiply(0, far)
        finish(0, near)
        finish(0, far)
        linear(0, near, gathered[1])
        summed_first = lax.psum_scatter(
            partial[0, near], "col", scatter_dimension=0, tiled=True
        )
        multiply(1, near, linear_across[0])
        multiply(1, far)
        linear_across[1] = after(linear_across[1], latest[-1])
        spread_far_linear()
        finish(1, near)
        linear(0, far)
        begun[0] = LineSum(partial[0, far], col, n_col)
        finish(1, far, summed_first, *begun[0].begun[:1])
        linear(1, far)
        begun[1] = LineSum(partial[1, far], col, n_col)
        linear(1, near)

        out = jnp.zeros((shard_rows, mixed_width * n_batch), jnp.bfloat16)
        for step, group in ((0, near), (0, far), (1, far), (1, near)):
            if group == far:
                summed = begun[step].end()
            elif step == 0:
                summed = summed_first
            else:
                summed = lax.psum_scatter(
                    partial[step, group], "col", scatter_dimension=0, tiled=True
                )
            first = ((batch // half) ^ group) * half * mixed_width
            bias = lax.dynamic_slice_in_dim(linear_bias, first, half * mixed_width)
            out = lax.dynamic_update_slice(
                out, (added(summed) + bias).astype(jnp.bfloat16), (starts[step], first)
            )
        return out

    return on_device


def solution(mesh):
    return jax.shard_map(
        build(mesh),
        mesh=mesh,
        in_specs=(
            P(("col", "batch"), "row"),
            P("row", ("col", "batch")),
            P("col"),
            P(),
            P("col", ("row", "batch")),
            P("row"),
        ),
        out_specs=P(("col", "batch"), "row"),
        check_vma=False,
    )
```

time: 481 us -> 438 us (0.911)
  starting transfers between devices: 105 us -> 53.4 us
  waiting for transfers between devices: 213 us -> 248 us
  Pallas kernels: 96.1 us -> 84.7 us
  other arithmetic: 22.9 us -> 13.4 us
    ppermute x12 -> x6, starting transfers between devices: 61.5 us -> 25.6 us  [__init__(): self.begun = [lax.ppermute(self.part(i), 'col', inward) for i in (3, 2, 1)]]
    ppermute x8 -> x4, waiting for transfers between devices: 26.2 us -> 48.8 us  [multiply(): sent = [lax.ppermute(product, ('row', 'col'), pairs) for pairs in turns]]
    all_gather x2, waiting for transfers between devices: 74.8 us -> 96.8 us  [on_device(): lax.all_gather(shard, 'col', axis=0, tiled=True)]
    ppermute x12 -> x6, waiting for transfers between devices: 65.2 us -> 51.2 us  [__init__(): self.begun = [lax.ppermute(self.part(i), 'col', inward) for i in (3, 2, 1)]]
    pallas_call x20 -> x12, Pallas kernels: 96.1 us -> 84.7 us  [the longest x4 40.3 us: linear_product(): pl.pallas_call(functools.partial(linear_kernel, groups, parts, per_piece)...]
    ppermute x8 -> x4, waiting for transfers between devices: 32.7 us -> 23.1 us  [finish(): lax.ppermute(crossed, ('row', 'col'), [(to, source) for source, to in pai...]
    ppermute x4 -> x2, waiting for transfers between devices: 13.4 us -> 22.9 us  [end(): lax.ppermute(added(self.part(0), over_3).astype(jnp.bfloat16), 'col', out...]
    ppermute x8 -> x4, starting transfers between devices: 16.1 us -> 8.71 us  [finish(): lax.ppermute(crossed, ('row', 'col'), [(to, source) for source, to in pai...]
  transfers between devices with their start and end apart: 48 -> 32, of which waited for: 20 -> 16; matrix products, arithmetic and copies ran while one was open for 6% -> 4% of each run, Pallas kernels for 20% -> 19%
where the time goes in v4:
time: 438 us
  waiting for transfers between devices  248 us (57%)
  Pallas kernels  84.7 us (19%)
  starting transfers between devices  53.4 us (12%)
  local copies, waits for them, and re-layouts  21.4 us (5%)
  between operations  16.5 us (4%)
  other arithmetic  13.4 us (3%)
    all_gather x2, waiting for transfers between devices, on_device(): lax.all_gather(shard, 'col', axis=0, tiled=True)  96.8 us
    ppermute x6, waiting for transfers between devices, __init__(): self.begun = [lax.ppermute(self.part(i), 'col', inward) for i in (3, 2, 1)]  51.2 us
    ppermute x4, waiting for transfers between devices, multiply(): sent = [lax.ppermute(product, ('row', 'col'), pairs) for pairs in turns]  48.8 us
    pallas_call x4, Pallas kernels, linear_product(): pl.pallas_call(functools.partial(linear_kernel, groups, parts, per_piece)...  40.3 us
    pallas_call x4, Pallas kernels, cross_product(): pl.pallas_call(functools.partial(cross_kernel, steps), out_shape=jax.Shap...  33.9 us
    ppermute x6, starting transfers between devices, __init__(): self.begun = [lax.ppermute(self.part(i), 'col', inward) for i in (3, 2, 1)]  25.6 us
    ppermute x4, waiting for transfers between devices, finish(): lax.ppermute(crossed, ('row', 'col'), [(to, source) for source, to in pai...  23.1 us
    ppermute x2, waiting for transfers between devices, end(): lax.ppermute(added(self.part(0), over_3).astype(jnp.bfloat16), 'col', out...  22.9 us
  transfers between devices with their start and end apart: 32, of which 16 were waited for; matrix products, arithmetic and copies ran while one was open for 4% of the time, Pallas kernels for 19%

profile of v4, /device:TPU:0, one launch (start us, length us, event | category | flops | bytes accessed | tf_op | source)
XLA Modules:
  0.0 437.7 jit_solution(878361149037221091)
XLA Ops:
  18.4 74.9 %all-gather.3.cloned.1.call-done.samples = bf16[512,4096]{1,0:T(8,128)(2,1)} async-done(((bf16[128,4096]{1,0:T(8,128)(2,1)}), bf16[512,4096]{1,0:T(8,128)(2,1)}) %all-gather.3.cloned.1.call-update) | async-done | bytes 4194320 | tf_op jit(solution)/shard_map/all_gather | solution.py:270
  95.5 8.8 %shard_map.64.own = bf16[512,1024]{1,0:T(8,128)(2,1)S(1)} custom-call(s32[18]{0:T(128)S(1)} %pad_add_fusion.3.meta, bf16[512,4096]{1,0:T(8,128)(2,1)S(1)} %copy-done, bf16[4096,512]{1,0:T(8,128)(2,1)} %refs_0_.3, bf16[4096,512]{1,0:T(8,128)(2,1)} %collective-permute-done.refs_1_), custom_call_target="tpu_custom_call" | custom-call | flops 2147483648 | bytes 9437184 | tf_op jit(solution)/shard_map/pallas_call | solution.py:52
  114.4 8.4 %shard_map.65.own = bf16[512,1024]{1,0:T(8,128)(2,1)S(1)} custom-call(s32[18]{0:T(128)S(1)} %pad_add_fusion.2.meta, bf16[512,4096]{1,0:T(8,128)(2,1)S(1)} %copy-done.1, bf16[4096,512]{1,0:T(8,128)(2,1)} %collective-permute-done.1.refs_0_, bf16[4096,512]{1,0:T(8,128)(2,1)} %collective-permute-done.2.refs_1_), custom_call_target="tpu_custom_call" | custom-call | flops 2147483648 | bytes 9437184 | tf_op jit(solution)/shard_map/pallas_call | solution.py:52
  129.4 8.2 %collective-permute-done.3.came = bf16[512,1024]{1,0:T(8,128)(2,1)S(1)} collective-permute-done((bf16[512,1024]{1,0:T(8,128)(2,1)S(1)}, bf16[512,1024]{1,0:T(8,128)(2,1)S(1)}, u32[]{:S(2)}, u32[]{:S(2)}) %collective-permute-start.3) | collective-permute-done | bytes 1048608 | tf_op jit(solution)/shard_map/ppermute | solution.py:316
  144.6 14.6 %collective-permute-done.4.came = bf16[512,1024]{1,0:T(8,128)(2,1)} collective-permute-done((bf16[512,1024]{1,0:T(8,128)(2,1)S(1)}, bf16[512,1024]{1,0:T(8,128)(2,1)}, u32[]{:S(2)}, u32[]{:S(2)}) %collective-permute-start.4) | collective-permute-done | bytes 1048608 | tf_op jit(solution)/shard_map/ppermute | solution.py:316
  165.0 21.9 %all-gather.5.cloned.1.call-done.samples = bf16[512,4096]{1,0:T(8,128)(2,1)} async-done(((bf16[128,4096]{1,0:T(8,128)(2,1)}), bf16[512,4096]{1,0:T(8,128)(2,1)}) %all-gather.5.cloned.1.call-update) | async-done | bytes 4194320 | tf_op jit(solution)/shard_map/all_gather | solution.py:270
  187.1 9.6 %shard_map.68 = bf16[512,2048]{1,0:T(8,128)(2,1)} custom-call(s32[7]{0:T(128)S(1)} %stack.67.meta, bf16[512,1024]{1,0:T(8,128)(2,1)S(1)} %shard_map.66.refs_0_, bf16[512,1024]{1,0:T(8,128)(2,1)S(1)} %shard_map.67.refs_1_, bf16[512,1024]{1,0:T(8,128)(2,1)} %collective-permute-done.5.refs_2_, bf16[512,1024]{1,0:T(8,128)(2,1)S(1)} %collective-permute-done.6.refs_3_, ...), custom_call_target="tpu_custom_call" | custom-call | flops 4294967296 | bytes 12582912 | tf_op jit(solution)/shard_map/pallas_call | solution.py:143
  199.1 8.9 %shard_map.69.own = bf16[512,1024]{1,0:T(8,128)(2,1)S(1)} custom-call(s32[18]{0:T(128)S(1)} %pad_add_fusion.3.meta, bf16[512,4096]{1,0:T(8,128)(2,1)S(1)} %copy-done.2, bf16[4096,512]{1,0:T(8,128)(2,1)} %refs_0_.3, bf16[4096,512]{1,0:T(8,128)(2,1)} %collective-permute-done.refs_1_), custom_call_target="tpu_custom_call" | custom-call | flops 2147483648 | bytes 9437184 | tf_op jit(solution)/shard_map/pallas_call | solution.py:52
  208.0 7.8 %shard_map.70.own = bf16[512,1024]{1,0:T(8,128)(2,1)S(1)} custom-call(s32[18]{0:T(128)S(1)} %pad_add_fusion.2.meta, bf16[512,4096]{1,0:T(8,128)(2,1)S(1)} %copy-done.2, bf16[4096,512]{1,0:T(8,128)(2,1)} %collective-permute-done.1.refs_0_, bf16[4096,512]{1,0:T(8,128)(2,1)} %collective-permute-done.2.refs_1_), custom_call_target="tpu_custom_call" | custom-call | flops 2147483648 | bytes 9437184 | tf_op jit(solution)/shard_map/pallas_call | solution.py:52
  215.8 4.6 %collective-permute-done.10.refs_5_ = bf16[1024,1024]{1,0:T(8,128)(2,1)} collective-permute-done((bf16[1024,1024]{1,0:T(8,128)(2,1)}, bf16[1024,1024]{1,0:T(8,128)(2,1)}, u32[]{:S(2)}, u32[]{:S(2)}) %collective-permute-start.10) | collective-permute-done | bytes 2097184 | tf_op jit(solution)/shard_map/ppermute | solution.py:249
  223.2 25.9 %collective-permute-done.9.came = bf16[512,1024]{1,0:T(8,128)(2,1)} collective-permute-done((bf16[512,1024]{1,0:T(8,128)(2,1)S(1)}, bf16[512,1024]{1,0:T(8,128)(2,1)}, u32[]{:S(2)}, u32[]{:S(2)}) %collective-permute-start.9) | collective-permute-done | bytes 1048608 | tf_op jit(solution)/shard_map/ppermute | solution.py:316
  252.4 9.5 %shard_map.72 = bf16[512,2048]{1,0:T(8,128)(2,1)} custom-call(s32[7]{0:T(128)S(1)} %stack.67.meta, bf16[512,1024]{1,0:T(8,128)(2,1)S(1)} %shard_map.66.refs_0_, bf16[512,1024]{1,0:T(8,128)(2,1)S(1)} %copy-done.4, bf16[512,1024]{1,0:T(8,128)(2,1)} %collective-permute-done.5.refs_2_, bf16[512,1024]{1,0:T(8,128)(2,1)S(1)} %copy-done.9, ...), custom_call_target="tpu_custom_call" | custom-call | flops 4294967296 | bytes 12582912 | tf_op jit(solution)/shard_map/pallas_call | solution.py:143
  264.5 4.5 %collective-permute-start.13 = (bf16[128,2048]{1,0:T(8,128)(2,1)S(1)}, bf16[128,2048]{1,0:T(8,128)(2,1)S(1)}, u32[]{:S(2)}, u32[]{:S(2)}) collective-permute-start(bf16[128,2048]{1,0:T(8,128)(2,1)S(1)} %get-tuple-element.44), channel_id=1, source_target_pairs={{0,4},{12,8},{1,5},{13,9},{2,6},{14,10},{3,7},{15,11},{16,20},{28,... | collective-permute-start | bytes 1572872 | tf_op jit(solution)/shard_map/ppermute | solution.py:214
  271.5 8.6 %collective-permute-done.13 = bf16[128,2048]{1,0:T(8,128)(2,1)S(1)} collective-permute-done((bf16[128,2048]{1,0:T(8,128)(2,1)S(1)}, bf16[128,2048]{1,0:T(8,128)(2,1)S(1)}, u32[]{:S(2)}, u32[]{:S(2)}) %collective-permute-start.13) | collective-permute-done | bytes 524320 | tf_op jit(solution)/shard_map/ppermute | solution.py:214
  285.9 5.2 %collective-permute-start.17 = (bf16[128,2048]{1,0:T(8,128)(2,1)}, bf16[128,2048]{1,0:T(8,128)(2,1)}, u32[]{:S(2)}, u32[]{:S(2)}) collective-permute-start(bf16[128,2048]{1,0:T(8,128)(2,1)} %get-tuple-element.45), channel_id=1, source_target_pairs={{0,4},{12,8},{1,5},{13,9},{2,6},{14,10},{3,7},{15,11},{16,20},{28,... | collective-permute-start | bytes 1572872 | tf_op jit(solution)/shard_map/ppermute | solution.py:214
  295.3 20.8 %collective-permute-done.21.refs_3_ = bf16[512,1024]{1,0:T(8,128)(2,1)S(1)} collective-permute-done((bf16[512,1024]{1,0:T(8,128)(2,1)S(1)}, bf16[512,1024]{1,0:T(8,128)(2,1)S(1)}, u32[]{:S(2)}, u32[]{:S(2)}) %collective-permute-start.21) | collective-permute-done | bytes 1048608 | tf_op jit(solution)/shard_map/ppermute | solution.py:333
  316.1 10.5 %shard_map.74 = bf16[512,2048]{1,0:T(8,128)(2,1)} custom-call(s32[7]{0:T(128)S(1)} %stack.67.meta, bf16[512,1024]{1,0:T(8,128)(2,1)} %shard_map.71.refs_0_, bf16[512,1024]{1,0:T(8,128)(2,1)S(1)} %shard_map.73.refs_1_, bf16[512,1024]{1,0:T(8,128)(2,1)S(1)} %collective-permute-done.20.refs_2_, bf16[512,1024]{1,0:T(8,128)(2,1)S(1)} %collective-permute-done.21.refs_3_, ...), custom_call_target="tpu_custom_call" | custom-call | flops 4294967296 | bytes 12582912 | tf_op jit(solution)/shard_map/pallas_call | solution.py:143
  326.6 10.7 %shard_map.75 = bf16[512,2048]{1,0:T(8,128)(2,1)} custom-call(s32[7]{0:T(128)S(1)} %stack.67.meta, bf16[512,1024]{1,0:T(8,128)(2,1)} %shard_map.71.refs_0_, bf16[512,1024]{1,0:T(8,128)(2,1)S(1)} %shard_map.73.refs_1_, bf16[512,1024]{1,0:T(8,128)(2,1)S(1)} %collective-permute-done.20.refs_2_, bf16[512,1024]{1,0:T(8,128)(2,1)S(1)} %collective-permute-done.21.refs_3_, ...), custom_call_target="tpu_custom_call" | custom-call | flops 4294967296 | bytes 12582912 | tf_op jit(solution)/shard_map/pallas_call | solution.py:143
  343.4 7.7 %collective-permute-start.26 = (bf16[128,2048]{1,0:T(8,128)(2,1)S(1)}, bf16[128,2048]{1,0:T(8,128)(2,1)S(1)}, u32[]{:S(2)}, u32[]{:S(2)}) collective-permute-start(bf16[128,2048]{1,0:T(8,128)(2,1)S(1)} %get-tuple-element.42), channel_id=1, source_target_pairs={{0,4},{12,8},{1,5},{13,9},{2,6},{14,10},{3,7},{15,11},{16,20},{28,... | collective-permute-start | bytes 1572872 | tf_op jit(solution)/shard_map/ppermute | solution.py:214
  351.1 8.4 %collective-permute-done.22 = bf16[128,2048]{1,0:T(8,128)(2,1)S(1)} collective-permute-done((bf16[128,2048]{1,0:T(8,128)(2,1)S(1)}, bf16[128,2048]{1,0:T(8,128)(2,1)S(1)}, u32[]{:S(2)}, u32[]{:S(2)}) %collective-permute-start.22) | collective-permute-done | bytes 524320 | tf_op jit(solution)/shard_map/ppermute | solution.py:214
  361.8 18.5 %collective-permute-done.26 = bf16[128,2048]{1,0:T(8,128)(2,1)S(1)} collective-permute-done((bf16[128,2048]{1,0:T(8,128)(2,1)S(1)}, bf16[128,2048]{1,0:T(8,128)(2,1)S(1)}, u32[]{:S(2)}, u32[]{:S(2)}) %collective-permute-start.26) | collective-permute-done | bytes 524320 | tf_op jit(solution)/shard_map/ppermute | solution.py:214
  380.4 4.4 %collective-permute-start.25 = (bf16[128,2048]{1,0:T(8,128)(2,1)S(1)}, bf16[128,2048]{1,0:T(8,128)(2,1)S(1)}, u32[]{:S(2)}, u32[]{:S(2)}) collective-permute-start(bf16[128,2048]{1,0:T(8,128)(2,1)S(1)} %get-tuple-element.43), channel_id=1, source_target_pairs={{0,4},{12,8},{1,5},{13,9},{2,6},{14,10},{3,7},{15,11},{16,20},{28,... | collective-permute-start | bytes 1572872 | tf_op jit(solution)/shard_map/ppermute | solution.py:214
  390.4 15.6 %collective-permute-done.25 = bf16[128,2048]{1,0:T(8,128)(2,1)S(1)} collective-permute-done((bf16[128,2048]{1,0:T(8,128)(2,1)S(1)}, bf16[128,2048]{1,0:T(8,128)(2,1)S(1)}, u32[]{:S(2)}, u32[]{:S(2)}) %collective-permute-start.25) | collective-permute-done | bytes 524320 | tf_op jit(solution)/shard_map/ppermute | solution.py:214
  406.0 21.5 %collective-permute-done.24 = bf16[128,2048]{1,0:T(8,128)(2,1)S(1)} collective-permute-done((bf16[128,2048]{1,0:T(8,128)(2,1)S(1)}, bf16[128,2048]{1,0:T(8,128)(2,1)S(1)}, u32[]{:S(2)}, u32[]{:S(2)}) %collective-permute-start.24) | collective-permute-done | bytes 524320 | tf_op jit(solution)/shard_map/ppermute | solution.py:229
  (138 shorter events, 81.5 us)
Async XLA Ops:
  6.5 86.7 %all-gather.3.cloned.1.call-start = ((), (), s32[]{:S(2)}) async-start(), calls=%async_computation.2 | async-start | bytes 5242880 | tf_op jit(solution)/shard_map/all_gather | solution.py:270
  9.7 177.2 %all-gather.5.cloned.1.call-start = ((), (), s32[]{:S(2)}) async-start(), calls=%async_computation.3 | async-start | bytes 5242880 | tf_op jit(solution)/shard_map/all_gather | solution.py:270
  10.2 94.0 %collective-permute-start.1 = (bf16[4096,512]{1,0:T(8,128)(2,1)}, bf16[4096,512]{1,0:T(8,128)(2,1)}, u32[]{:S(2)}, u32[]{:S(2)}) collective-permute-start(bf16[4096,512]{1,0:T(8,128)(2,1)} %refs_0_.3), channel_id=1, source_target_pairs={{0,2},{1,3},{2,0},{3,1},{4,6},{5,7},{6,4},{7,5},{8,10},{9,11},{10,... | collective-permute-start | bytes 12582920 | tf_op jit(solution)/shard_map/ppermute | solution.py:249
  104.4 175.7 %reduce-scatter.3.cloned.1.call-start = ((), (), s32[]{:S(2)}) async-start(), calls=%async_computation.4 | async-start | bytes 2621440 | tf_op jit(solution)/shard_map/reduce_scatter | solution.py:371
  104.4 82.5 %collective-permute-start.7 = (bf16[2048,1024]{1,0:T(8,128)(2,1)}, bf16[2048,1024]{1,0:T(8,128)(2,1)}, u32[]{:S(2)}, u32[]{:S(2)}) collective-permute-start(bf16[2048,1024]{1,0:T(8,128)(2,1)} %refs_4_.3), channel_id=1, source_target_pairs={{0,1},{1,0},{2,3},{3,2},{4,5},{5,4},{6,7},{7,6},{8,9},{9,8},{10,11... | collective-permute-start | bytes 12582920 | tf_op jit(solution)/shard_map/ppermute | solution.py:249
  109.7 27.9 %collective-permute-start.3 = (bf16[512,1024]{1,0:T(8,128)(2,1)S(1)}, bf16[512,1024]{1,0:T(8,128)(2,1)S(1)}, u32[]{:S(2)}, u32[]{:S(2)}) collective-permute-start(bf16[512,1024]{1,0:T(8,128)(2,1)S(1)} %shard_map.64.own), channel_id=1, source_target_pairs={{16,0},{20,4},{8,24},{12,28},{17,1},{21,5},{9,25},{13,29},{18,2},{... | collective-permute-start | bytes 3145736 | tf_op jit(solution)/shard_map/ppermute | solution.py:316
  122.9 36.4 %collective-permute-start.4 = (bf16[512,1024]{1,0:T(8,128)(2,1)S(1)}, bf16[512,1024]{1,0:T(8,128)(2,1)}, u32[]{:S(2)}, u32[]{:S(2)}) collective-permute-start(bf16[512,1024]{1,0:T(8,128)(2,1)S(1)} %shard_map.65.own), channel_id=1, source_target_pairs={{16,0},{20,4},{8,24},{12,28},{17,1},{21,5},{9,25},{13,29},{18,2},{... | collective-permute-start | bytes 3145736 | tf_op jit(solution)/shard_map/ppermute | solution.py:316
  126.6 70.2 %collective-permute-start.8 = (bf16[1024,1024]{1,0:T(8,128)(2,1)}, bf16[1024,1024]{1,0:T(8,128)(2,1)}, u32[]{:S(2)}, u32[]{:S(2)}) collective-permute-start(bf16[1024,1024]{1,0:T(8,128)(2,1)} %get-tuple-element.40), channel_id=1, source_target_pairs={{0,2},{1,3},{2,0},{3,1},{4,6},{5,7},{6,4},{7,5},{8,10},{9,11},{10,... | collective-permute-start | bytes 6291464 | tf_op jit(solution)/shard_map/ppermute | solution.py:249
  142.1 44.8 %collective-permute-start.5 = (bf16[512,1024]{1,0:T(8,128)(2,1)S(1)}, bf16[512,1024]{1,0:T(8,128)(2,1)}, u32[]{:S(2)}, u32[]{:S(2)}) collective-permute-start(bf16[512,1024]{1,0:T(8,128)(2,1)S(1)} %shard_map.66.refs_0_), channel_id=1, source_target_pairs={{0,16},{4,20},{24,8},{28,12},{1,17},{5,21},{25,9},{29,13},{2,18},{... | collective-permute-start | bytes 3145736 | tf_op jit(solution)/shard_map/ppermute | solution.py:333
  163.1 57.3 %collective-permute-start.10 = (bf16[1024,1024]{1,0:T(8,128)(2,1)}, bf16[1024,1024]{1,0:T(8,128)(2,1)}, u32[]{:S(2)}, u32[]{:S(2)}) collective-permute-start(bf16[1024,1024]{1,0:T(8,128)(2,1)} %get-tuple-element.39), channel_id=1, source_target_pairs={{0,2},{1,3},{2,0},{3,1},{4,6},{5,7},{6,4},{7,5},{8,10},{9,11},{10,... | collective-permute-start | bytes 6291464 | tf_op jit(solution)/shard_map/ppermute | solution.py:249
  196.8 231.1 %reduce-scatter.5.cloned.1.call-start = ((), (), s32[]{:S(2)}) async-start(), calls=%async_computation.5 | async-start | bytes 2621440 | tf_op jit(solution)/shard_map/reduce_scatter | solution.py:393
  196.8 55.5 %collective-permute-start.11 = (bf16[1024,1024]{1,0:T(8,128)(2,1)}, bf16[1024,1024]{1,0:T(8,128)(2,1)}, u32[]{:S(2)}, u32[]{:S(2)}) collective-permute-start(bf16[1024,1024]{1,0:T(8,128)(2,1)} %collective-permute-done.8.refs_4_), channel_id=1, source_target_pairs={{0,1},{1,0},{2,3},{3,2},{4,5},{5,4},{6,7},{7,6},{8,9},{9,8},{10,11... | collective-permute-start | bytes 6291464 | tf_op jit(solution)/shard_map/ppermute | solution.py:249
  220.4 31.9 %collective-permute-start.12 = (bf16[1024,1024]{1,0:T(8,128)(2,1)}, bf16[1024,1024]{1,0:T(8,128)(2,1)}, u32[]{:S(2)}, u32[]{:S(2)}) collective-permute-start(bf16[1024,1024]{1,0:T(8,128)(2,1)} %collective-permute-done.10.refs_5_), channel_id=1, source_target_pairs={{0,1},{1,0},{2,3},{3,2},{4,5},{5,4},{6,7},{7,6},{8,9},{9,8},{10,11... | collective-permute-start | bytes 6291464 | tf_op jit(solution)/shard_map/ppermute | solution.py:249
  220.4 28.7 %collective-permute-start.9 = (bf16[512,1024]{1,0:T(8,128)(2,1)S(1)}, bf16[512,1024]{1,0:T(8,128)(2,1)}, u32[]{:S(2)}, u32[]{:S(2)}) collective-permute-start(bf16[512,1024]{1,0:T(8,128)(2,1)S(1)} %shard_map.69.own), channel_id=1, source_target_pairs={{16,0},{20,4},{8,24},{12,28},{17,1},{21,5},{9,25},{13,29},{18,2},{... | collective-permute-start | bytes 3145736 | tf_op jit(solution)/shard_map/ppermute | solution.py:316
  221.8 59.1 %collective-permute-start.19 = (bf16[512,1024]{1,0:T(8,128)(2,1)S(1)}, bf16[512,1024]{1,0:T(8,128)(2,1)}, u32[]{:S(2)}, u32[]{:S(2)}) collective-permute-start(bf16[512,1024]{1,0:T(8,128)(2,1)S(1)} %shard_map.70.own), channel_id=1, source_target_pairs={{16,0},{20,4},{8,24},{12,28},{17,1},{21,5},{9,25},{13,29},{18,2},{... | collective-permute-start | bytes 3145736 | tf_op jit(solution)/shard_map/ppermute | solution.py:316
  269.0 26.3 %collective-permute-start.20 = (bf16[512,1024]{1,0:T(8,128)(2,1)}, bf16[512,1024]{1,0:T(8,128)(2,1)S(1)}, u32[]{:S(2)}, u32[]{:S(2)}) collective-permute-start(bf16[512,1024]{1,0:T(8,128)(2,1)} %shard_map.71.refs_0_), channel_id=1, source_target_pairs={{0,16},{4,20},{24,8},{28,12},{1,17},{5,21},{25,9},{29,13},{2,18},{... | collective-permute-start | bytes 3145736 | tf_op jit(solution)/shard_map/ppermute | solution.py:333
  283.3 32.7 %collective-permute-start.21 = (bf16[512,1024]{1,0:T(8,128)(2,1)S(1)}, bf16[512,1024]{1,0:T(8,128)(2,1)S(1)}, u32[]{:S(2)}, u32[]{:S(2)}) collective-permute-start(bf16[512,1024]{1,0:T(8,128)(2,1)S(1)} %shard_map.73.refs_1_), channel_id=1, source_target_pairs={{0,16},{4,20},{24,8},{28,12},{1,17},{5,21},{25,9},{29,13},{2,18},{... | collective-permute-start | bytes 3145736 | tf_op jit(solution)/shard_map/ppermute | solution.py:333
  285.9 55.6 %collective-permute-start.17 = (bf16[128,2048]{1,0:T(8,128)(2,1)}, bf16[128,2048]{1,0:T(8,128)(2,1)}, u32[]{:S(2)}, u32[]{:S(2)}) collective-permute-start(bf16[128,2048]{1,0:T(8,128)(2,1)} %get-tuple-element.45), channel_id=1, source_target_pairs={{0,4},{12,8},{1,5},{13,9},{2,6},{14,10},{3,7},{15,11},{16,20},{28,... | collective-permute-start | bytes 1572872 | tf_op jit(solution)/shard_map/ppermute | solution.py:214
  291.1 94.8 %collective-permute-start.16 = (bf16[128,2048]{1,0:T(8,128)(2,1)}, bf16[128,2048]{1,0:T(8,128)(2,1)}, u32[]{:S(2)}, u32[]{:S(2)}) collective-permute-start(bf16[128,2048]{1,0:T(8,128)(2,1)} %get-tuple-element.46), channel_id=1, source_target_pairs={{0,4},{12,8},{1,5},{13,9},{2,6},{14,10},{3,7},{15,11},{16,20},{28,... | collective-permute-start | bytes 1572872 | tf_op jit(solution)/shard_map/ppermute | solution.py:214
  342.7 44.9 %collective-permute-start.18 = (bf16[128,2048]{1,0:T(8,128)(2,1)S(1)}, bf16[128,2048]{1,0:T(8,128)(2,1)S(1)}, u32[]{:S(2)}, u32[]{:S(2)}) collective-permute-start(bf16[128,2048]{1,0:T(8,128)(2,1)S(1)} %add_convert_fusion.6), channel_id=1, source_target_pairs={{4,8},{8,4},{5,9},{9,5},{6,10},{10,6},{7,11},{11,7},{20,24},{24,20... | collective-permute-start | bytes 1572872 | tf_op jit(solution)/shard_map/ppermute | solution.py:228
  343.4 37.0 %collective-permute-start.26 = (bf16[128,2048]{1,0:T(8,128)(2,1)S(1)}, bf16[128,2048]{1,0:T(8,128)(2,1)S(1)}, u32[]{:S(2)}, u32[]{:S(2)}) collective-permute-start(bf16[128,2048]{1,0:T(8,128)(2,1)S(1)} %get-tuple-element.42), channel_id=1, source_target_pairs={{0,4},{12,8},{1,5},{13,9},{2,6},{14,10},{3,7},{15,11},{16,20},{28,... | collective-permute-start | bytes 1572872 | tf_op jit(solution)/shard_map/ppermute | solution.py:214
  360.5 28.5 %collective-permute-start.15 = (bf16[128,2048]{1,0:T(8,128)(2,1)S(1)}, bf16[128,2048]{1,0:T(8,128)(2,1)S(1)}, u32[]{:S(2)}, u32[]{:S(2)}) collective-permute-start(bf16[128,2048]{1,0:T(8,128)(2,1)S(1)} %add_convert_fusion.7), channel_id=1, source_target_pairs={{4,0},{8,12},{5,1},{9,13},{6,2},{10,14},{7,3},{11,15},{20,16},{24,... | collective-permute-start | bytes 1572872 | tf_op jit(solution)/shard_map/ppermute | solution.py:229
  380.4 25.7 %collective-permute-start.25 = (bf16[128,2048]{1,0:T(8,128)(2,1)S(1)}, bf16[128,2048]{1,0:T(8,128)(2,1)S(1)}, u32[]{:S(2)}, u32[]{:S(2)}) collective-permute-start(bf16[128,2048]{1,0:T(8,128)(2,1)S(1)} %get-tuple-element.43), channel_id=1, source_target_pairs={{0,4},{12,8},{1,5},{13,9},{2,6},{14,10},{3,7},{15,11},{16,20},{28,... | collective-permute-start | bytes 1572872 | tf_op jit(solution)/shard_map/ppermute | solution.py:214
  385.9 41.6 %collective-permute-start.24 = (bf16[128,2048]{1,0:T(8,128)(2,1)S(1)}, bf16[128,2048]{1,0:T(8,128)(2,1)S(1)}, u32[]{:S(2)}, u32[]{:S(2)}) collective-permute-start(bf16[128,2048]{1,0:T(8,128)(2,1)S(1)} %add_convert_fusion.3), channel_id=1, source_target_pairs={{4,0},{8,12},{5,1},{9,13},{6,2},{10,14},{7,3},{11,15},{20,16},{24,... | collective-permute-start | bytes 1572872 | tf_op jit(solution)/shard_map/ppermute | solution.py:229
  (29 other events, 399.0 us)
Sparse Core Ops, SparseCore 0:
  9.8 83.4 all-gather.2
  104.5 82.3 all-gather.4
  196.9 47.2 reduce-scatter.2
  339.0 71.7 reduce-scatter.4

commit v5 on v4

--- a/solution.py
+++ b/solution.py
@@ -232,6 +232,45 @@
         return added(own) + jnp.where(is_end, added(out_0), added(from_1, over_2))
 
 
+class LineGather:
+    def __init__(self, shard, place):
+        self.shard, self.place = shard, place
+        self.beside = lax.ppermute(shard, "col", [(0, 1), (1, 0), (2, 3), (3, 2)])
+        self.over = lax.ppermute(shard, "col", [(1, 2), (2, 1)])
+
+    def relay(self):
+        outward = [(1, 0), (2, 3)]
+        self.out = lax.ppermute(self.over, "col", outward)
+        self.over_beside = lax.ppermute(self.beside, "col", [(1, 2), (2, 1)])
+        self.out_beside = lax.ppermute(self.over_beside, "col", outward)
+
+    def whole(self):
+        place, shard = self.place, self.shard
+        is_end = (place == 0) | (place == 3)
+        lower = place < 2
+        rows = shard.shape[0]
+        whole = jnp.zeros((4 * rows, shard.shape[1]), shard.dtype)
+        for part, at in (
+            (shard, place),
+            (self.beside, place ^ 1),
+            (jnp.where(is_end, self.out, self.over), jnp.where(lower, 2, 1)),
+            (jnp.where(is_end, self.out_beside, self.over_beside), jnp.where(lower, 3, 0)),
+        ):
+            whole = lax.dynamic_update_slice_in_dim(whole, part, at * rows, 0)
+        return whole
+
+
+class PlainGather:
+    def __init__(self, shard, place):
+        self.shard = self.beside = self.over = self.out = self.over_beside = self.out_beside = shard
+
+    def relay(self):
+        pass
+
+    def whole(self):
+        return lax.all_gather(self.shard, "col", axis=0, tiled=True)
+
+
 def build(mesh):
     n_row, n_col, n_batch = (mesh.shape[name] for name in ("row", "col", "batch"))
 
@@ -259,7 +298,6 @@
         cross_across = to_batch(cross_weight, half)
         parts = jnp.split(linear_weight, 2, axis=0)
         linear_across = [to_batch(part, half) for part in parts]
-        cross_pieces = spread_near({0: cross_weight})
         linear_pieces = {
             place: [piece] for place, piece in spread_near({0: linear_weight}).items()
         }
@@ -267,7 +305,12 @@
         shard_rows = features.shape[0]
         starts = [shard_rows * sum(SHARES[:i]) // sum(SHARES) for i in range(len(SHARES) + 1)]
         shards = [features[first:last] for first, last in zip(starts, starts[1:])]
-        gathered = [lax.all_gather(shard, "col", axis=0, tiled=True) for shard in shards]
+        gathers = [(LineGather if n_col == 4 else PlainGather)(shard, col) for shard in shards]
+        for gather in gathers:
+            gather.relay()
+        gathered = [gather.whole() for gather in gathers]
+        cross_pieces = spread_near({0: after(cross_weight, gathers[0].beside)})
+        cross_pieces[0] = cross_weight
 
         def kept_list(apart):
             out_block = (col * n_batch + (batch ^ apart)) * piece_width // block
@@ -362,26 +405,27 @@
                 linear_pieces[half + place] = [part[place] for part in arrived]
 
         begun = {}
-        multiply(0, near)
+        later = gathers[1]
+        multiply(0, near, later.beside, later.over, later.over_beside)
         spread_far_cross(latest[-1])
+        finish(0, near, later.out)
         multiply(0, far)
-        finish(0, near)
+        multiply(1, near, linear_across[0])
         finish(0, far)
-        linear(0, near, gathered[1])
+        multiply(1, far)
+        finish(1, near)
+        linear(0, near)
         summed_first = lax.psum_scatter(
             partial[0, near], "col", scatter_dimension=0, tiled=True
         )
-        multiply(1, near, linear_across[0])
-        multiply(1, far)
+        finish(1, far)
         linear_across[1] = after(linear_across[1], latest[-1])
         spread_far_linear()
-        finish(1, near)
         linear(0, far)
         begun[0] = LineSum(partial[0, far], col, n_col)
-        finish(1, far, summed_first, *begun[0].begun[:1])
-        linear(1, far)
+        linear(1, near, *begun[0].begun[:1])
+        linear(1, far, summed_first)
         begun[1] = LineSum(partial[1, far], col, n_col)
-        linear(1, near)
 
         out = jnp.zeros((shard_rows, mixed_width * n_batch), jnp.bfloat16)
         for step, group in ((0, near), (0, far), (1, far), (1, near)):

time: 438 us -> 430 us (0.982)
  waiting for transfers between devices: 248 us -> 205 us
  starting transfers between devices: 53.4 us -> 76.5 us
  Pallas kernels: 84.7 us -> 90.8 us
    ppermute x0 -> x10, waiting for transfers between devices: none -> 107 us  [the longest x2 45.2 us: relay(): self.out = lax.ppermute(self.over, 'col', outward)]
    all_gather x2 -> x0, waiting for transfers between devices: 96.8 us -> none  [on_device(): lax.all_gather(shard, 'col', axis=0, tiled=True)]
    ppermute x4, waiting for transfers between devices: 48.8 us -> 1.41 us  [multiply(): sent = [lax.ppermute(product, ('row', 'col'), pairs) for pairs in turns]]
    ppermute x0 -> x10, starting transfers between devices: none -> 17.6 us  [the longest x2 6.75 us: __init__(): self.beside = lax.ppermute(shard, 'col', [(0, 1), (1, 0), (2, 3), (3, 2)])]
    ppermute x6, waiting for transfers between devices: 51.2 us -> 59.3 us  [__init__(): self.begun = [lax.ppermute(self.part(i), 'col', inward) for i in (3, 2, 1)]]
    unnamed x42 -> x26, local copies, waits for them, and re-layouts: 11.4 us -> 3.35 us
    ppermute x4, starting transfers between devices: 8.71 us -> 16.5 us  [finish(): lax.ppermute(crossed, ('row', 'col'), [(to, source) for source, to in pai...]
    ppermute x2, waiting for transfers between devices: 22.9 us -> 15.8 us  [end(): lax.ppermute(added(self.part(0), over_3).astype(jnp.bfloat16), 'col', out...]
  transfers between devices with their start and end apart: 32 -> 40, of which waited for: 16 -> 16; matrix products, arithmetic and copies ran while one was open for 4% -> 6% of each run, Pallas kernels for 19% -> 21%
where the time goes in v5:
time: 430 us; the launch traced here: 426 us
  waiting for transfers between devices  205 us (48%)
  Pallas kernels  90.8 us (21%)
  starting transfers between devices  76.5 us (18%)
  local copies, waits for them, and re-layouts  19.7 us (5%)
  other arithmetic  17.3 us (4%)
  between operations  16.6 us (4%)
    ppermute x6, waiting for transfers between devices, __init__(): self.begun = [lax.ppermute(self.part(i), 'col', inward) for i in (3, 2, 1)]  59.3 us
    ppermute x2, waiting for transfers between devices, relay(): self.out = lax.ppermute(self.over, 'col', outward)  45.2 us
    pallas_call x4, Pallas kernels, linear_product(): pl.pallas_call(functools.partial(linear_kernel, groups, parts, per_piece)...  40.8 us
    pallas_call x4, Pallas kernels, cross_product(): pl.pallas_call(functools.partial(cross_kernel, steps), out_shape=jax.Shap...  39.2 us
    ppermute x2, waiting for transfers between devices, relay(): self.out_beside = lax.ppermute(self.over_beside, 'col', outward)  31.9 us
    ppermute x2, waiting for transfers between devices, __init__(): self.beside = lax.ppermute(shard, 'col', [(0, 1), (1, 0), (2, 3), (3, 2)])  30.1 us
    ppermute x6, starting transfers between devices, __init__(): self.begun = [lax.ppermute(self.part(i), 'col', inward) for i in (3, 2, 1)]  25.3 us
    ppermute x4, waiting for transfers between devices, finish(): lax.ppermute(crossed, ('row', 'col'), [(to, source) for source, to in pai...  21.6 us
  transfers between devices with their start and end apart: 40, of which 16 were waited for; matrix products, arithmetic and copies ran while one was open for 6% of the time, Pallas kernels for 21%

profile of v5, /device:TPU:0, one launch (start us, length us, event | category | flops | bytes accessed | tf_op | source)
XLA Modules:
  0.0 426.5 jit_solution(10988927881028578074)
XLA Ops:
  24.9 13.5 %collective-permute-done.3 = bf16[128,4096]{1,0:T(8,128)(2,1)} collective-permute-done((bf16[128,4096]{1,0:T(8,128)(2,1)}, bf16[128,4096]{1,0:T(8,128)(2,1)}, u32[]{:S(2)}, u32[]{:S(2)}) %collective-permute-start.3) | collective-permute-done | bytes 1048608 | tf_op jit(solution)/shard_map/ppermute | solution.py:238
  43.2 16.7 %collective-permute-done = bf16[128,4096]{1,0:T(8,128)(2,1)S(1)} collective-permute-done((bf16[128,4096]{1,0:T(8,128)(2,1)}, bf16[128,4096]{1,0:T(8,128)(2,1)S(1)}, u32[]{:S(2)}, u32[]{:S(2)}) %collective-permute-start) | collective-permute-done | bytes 1048608 | tf_op jit(solution)/shard_map/ppermute | solution.py:238
  64.8 23.8 %collective-permute-done.5 = bf16[128,4096]{1,0:T(8,128)(2,1)S(1)} collective-permute-done((bf16[128,4096]{1,0:T(8,128)(2,1)}, bf16[128,4096]{1,0:T(8,128)(2,1)S(1)}, u32[]{:S(2)}, u32[]{:S(2)}) %collective-permute-start.5) | collective-permute-done | bytes 1048608 | tf_op jit(solution)/shard_map/ppermute | solution.py:243
  89.0 22.0 %collective-permute-done.7 = bf16[128,4096]{1,0:T(8,128)(2,1)S(1)} collective-permute-done((bf16[128,4096]{1,0:T(8,128)(2,1)S(1)}, bf16[128,4096]{1,0:T(8,128)(2,1)S(1)}, u32[]{:S(2)}, u32[]{:S(2)}) %collective-permute-start.7) | collective-permute-done | bytes 1048608 | tf_op jit(solution)/shard_map/ppermute | solution.py:245
  111.3 9.5 %shard_map.64.own = bf16[512,1024]{1,0:T(8,128)(2,1)S(1)} custom-call(s32[18]{0:T(128)S(1)} %pad_add_fusion.3.meta, bf16[512,4096]{1,0:T(8,128)(2,1)S(1)} %select_dynamic-update-slice_fusion.2.samples, bf16[4096,512]{1,0:T(8,128)(2,1)} %refs_0_.3, bf16[4096,512]{1,0:T(8,128)(2,1)} %collective-permute-done.8.refs_1_), custom_call_target="tpu_custom_call" | custom-call | flops 2147483648 | bytes 9437184 | tf_op jit(solution)/shard_map/pallas_call | solution.py:52
  136.6 21.4 %collective-permute-done.9 = bf16[128,4096]{1,0:T(8,128)(2,1)S(1)} collective-permute-done((bf16[128,4096]{1,0:T(8,128)(2,1)}, bf16[128,4096]{1,0:T(8,128)(2,1)S(1)}, u32[]{:S(2)}, u32[]{:S(2)}) %collective-permute-start.9) | collective-permute-done | bytes 1048608 | tf_op jit(solution)/shard_map/ppermute | solution.py:243
  163.7 9.3 %shard_map.66.own = bf16[512,1024]{1,0:T(8,128)(2,1)S(1)} custom-call(s32[18]{0:T(128)S(1)} %pad_add_fusion.1.meta, bf16[512,4096]{1,0:T(8,128)(2,1)S(1)} %copy-done.1, bf16[4096,512]{1,0:T(8,128)(2,1)} %collective-permute-done.11.refs_0_, bf16[4096,512]{1,0:T(8,128)(2,1)} %collective-permute-done.12.refs_1_), custom_call_target="tpu_custom_call" | custom-call | flops 2147483648 | bytes 9437184 | tf_op jit(solution)/shard_map/pallas_call | solution.py:52
  174.3 9.9 %collective-permute-done.14 = bf16[128,4096]{1,0:T(8,128)(2,1)S(1)} collective-permute-done((bf16[128,4096]{1,0:T(8,128)(2,1)}, bf16[128,4096]{1,0:T(8,128)(2,1)S(1)}, u32[]{:S(2)}, u32[]{:S(2)}) %collective-permute-start.14) | collective-permute-done | bytes 1048608 | tf_op jit(solution)/shard_map/ppermute | solution.py:245
  185.5 9.9 %shard_map.67.own = bf16[512,1024]{1,0:T(8,128)(2,1)S(1)} custom-call(s32[18]{0:T(128)S(1)} %pad_add_fusion.3.meta, bf16[512,4096]{1,0:T(8,128)(2,1)} %select_dynamic-update-slice_fusion.samples, bf16[4096,512]{1,0:T(8,128)(2,1)} %refs_0_.3, bf16[4096,512]{1,0:T(8,128)(2,1)} %collective-permute-done.8.refs_1_), custom_call_target="tpu_custom_call" | custom-call | flops 2147483648 | bytes 9437184 | tf_op jit(solution)/shard_map/pallas_call | solution.py:52
  198.5 6.5 %collective-permute-start.17 = (bf16[512,1024]{1,0:T(8,128)(2,1)S(1)}, bf16[512,1024]{1,0:T(8,128)(2,1)}, u32[]{:S(2)}, u32[]{:S(2)}) collective-permute-start(bf16[512,1024]{1,0:T(8,128)(2,1)S(1)} %shard_map.65.refs_0_), channel_id=1, source_target_pairs={{0,16},{4,20},{24,8},{28,12},{1,17},{5,21},{25,9},{29,13},{2,18},{... | collective-permute-start | bytes 3145736 | tf_op jit(solution)/shard_map/ppermute | solution.py:376
  210.5 10.5 %shard_map.69.own = bf16[512,1024]{1,0:T(8,128)(2,1)S(1)} custom-call(s32[18]{0:T(128)S(1)} %pad_add_fusion.1.meta, bf16[512,4096]{1,0:T(8,128)(2,1)} %select_dynamic-update-slice_fusion.samples, bf16[4096,512]{1,0:T(8,128)(2,1)} %collective-permute-done.11.refs_0_, bf16[4096,512]{1,0:T(8,128)(2,1)} %collective-permute-done.12.refs_1_), custom_call_target="tpu_custom_call" | custom-call | flops 2147483648 | bytes 9437184 | tf_op jit(solution)/shard_map/pallas_call | solution.py:52
  227.6 19.5 %collective-permute-done.18.refs_3_ = bf16[512,1024]{1,0:T(8,128)(2,1)} collective-permute-done((bf16[512,1024]{1,0:T(8,128)(2,1)}, bf16[512,1024]{1,0:T(8,128)(2,1)}, u32[]{:S(2)}, u32[]{:S(2)}) %collective-permute-start.18) | collective-permute-done | bytes 1048608 | tf_op jit(solution)/shard_map/ppermute | solution.py:376
  247.1 10.7 %shard_map.71 = bf16[512,2048]{1,0:T(8,128)(2,1)} custom-call(s32[7]{0:T(128)S(1)} %stack.67.meta, bf16[512,1024]{1,0:T(8,128)(2,1)S(1)} %shard_map.65.refs_0_, bf16[512,1024]{1,0:T(8,128)(2,1)} %shard_map.68.refs_1_, bf16[512,1024]{1,0:T(8,128)(2,1)} %collective-permute-done.17.refs_2_, bf16[512,1024]{1,0:T(8,128)(2,1)} %collective-permute-done.18.refs_3_, ...), custom_call_target="tpu_custom_call" | custom-call | flops 4294967296 | bytes 12582912 | tf_op jit(solution)/shard_map/pallas_call | solution.py:143
  262.2 5.5 %collective-permute-start.30 = (bf16[512,1024]{1,0:T(8,128)(2,1)S(1)}, bf16[512,1024]{1,0:T(8,128)(2,1)}, u32[]{:S(2)}, u32[]{:S(2)}) collective-permute-start(bf16[512,1024]{1,0:T(8,128)(2,1)S(1)} %copy-done.3), channel_id=1, source_target_pairs={{0,16},{4,20},{24,8},{28,12},{1,17},{5,21},{25,9},{29,13},{2,18},{... | collective-permute-start | bytes 3145736 | tf_op jit(solution)/shard_map/ppermute | solution.py:376
  270.0 10.8 %shard_map.73 = bf16[512,2048]{1,0:T(8,128)(2,1)} custom-call(s32[7]{0:T(128)S(1)} %stack.67.meta, bf16[512,1024]{1,0:T(8,128)(2,1)S(1)} %shard_map.65.refs_0_, bf16[512,1024]{1,0:T(8,128)(2,1)} %shard_map.68.refs_1_, bf16[512,1024]{1,0:T(8,128)(2,1)} %collective-permute-done.17.refs_2_, bf16[512,1024]{1,0:T(8,128)(2,1)} %collective-permute-done.18.refs_3_, ...), custom_call_target="tpu_custom_call" | custom-call | flops 4294967296 | bytes 12582912 | tf_op jit(solution)/shard_map/pallas_call | solution.py:143
  283.2 4.9 %collective-permute-start.24 = (bf16[128,2048]{1,0:T(8,128)(2,1)S(1)}, bf16[128,2048]{1,0:T(8,128)(2,1)}, u32[]{:S(2)}, u32[]{:S(2)}) collective-permute-start(bf16[128,2048]{1,0:T(8,128)(2,1)S(1)} %get-tuple-element.48), channel_id=1, source_target_pairs={{0,4},{12,8},{1,5},{13,9},{2,6},{14,10},{3,7},{15,11},{16,20},{28,... | collective-permute-start | bytes 1572872 | tf_op jit(solution)/shard_map/ppermute | solution.py:214
  292.2 18.5 %collective-permute-done.24 = bf16[128,2048]{1,0:T(8,128)(2,1)} collective-permute-done((bf16[128,2048]{1,0:T(8,128)(2,1)S(1)}, bf16[128,2048]{1,0:T(8,128)(2,1)}, u32[]{:S(2)}, u32[]{:S(2)}) %collective-permute-start.24) | collective-permute-done | bytes 524320 | tf_op jit(solution)/shard_map/ppermute | solution.py:214
  311.9 9.7 %shard_map.74 = bf16[512,2048]{1,0:T(8,128)(2,1)} custom-call(s32[7]{0:T(128)S(1)} %stack.67.meta, bf16[512,1024]{1,0:T(8,128)(2,1)S(1)} %copy-done.3, bf16[512,1024]{1,0:T(8,128)(2,1)S(1)} %copy-done.5, bf16[512,1024]{1,0:T(8,128)(2,1)} %collective-permute-done.30.refs_2_, bf16[512,1024]{1,0:T(8,128)(2,1)} %collective-permute-done.31.refs_3_, ...), custom_call_target="tpu_custom_call" | custom-call | flops 4294967296 | bytes 12582912 | tf_op jit(solution)/shard_map/pallas_call | solution.py:143
  321.7 9.6 %shard_map.75 = bf16[512,2048]{1,0:T(8,128)(2,1)} custom-call(s32[7]{0:T(128)S(1)} %stack.67.meta, bf16[512,1024]{1,0:T(8,128)(2,1)S(1)} %copy-done.3, bf16[512,1024]{1,0:T(8,128)(2,1)S(1)} %copy-done.5, bf16[512,1024]{1,0:T(8,128)(2,1)} %collective-permute-done.30.refs_2_, bf16[512,1024]{1,0:T(8,128)(2,1)} %collective-permute-done.31.refs_3_, ...), custom_call_target="tpu_custom_call" | custom-call | flops 4294967296 | bytes 12582912 | tf_op jit(solution)/shard_map/pallas_call | solution.py:143
  340.8 7.6 %collective-permute-start.36 = (bf16[128,2048]{1,0:T(8,128)(2,1)S(1)}, bf16[128,2048]{1,0:T(8,128)(2,1)S(1)}, u32[]{:S(2)}, u32[]{:S(2)}) collective-permute-start(bf16[128,2048]{1,0:T(8,128)(2,1)S(1)} %get-tuple-element.46), channel_id=1, source_target_pairs={{0,4},{12,8},{1,5},{13,9},{2,6},{14,10},{3,7},{15,11},{16,20},{28,... | collective-permute-start | bytes 1572872 | tf_op jit(solution)/shard_map/ppermute | solution.py:214
  348.4 12.1 %collective-permute-done.32 = bf16[128,2048]{1,0:T(8,128)(2,1)S(1)} collective-permute-done((bf16[128,2048]{1,0:T(8,128)(2,1)S(1)}, bf16[128,2048]{1,0:T(8,128)(2,1)S(1)}, u32[]{:S(2)}, u32[]{:S(2)}) %collective-permute-start.32) | collective-permute-done | bytes 524320 | tf_op jit(solution)/shard_map/ppermute | solution.py:214
  362.8 19.5 %collective-permute-done.36 = bf16[128,2048]{1,0:T(8,128)(2,1)S(1)} collective-permute-done((bf16[128,2048]{1,0:T(8,128)(2,1)S(1)}, bf16[128,2048]{1,0:T(8,128)(2,1)S(1)}, u32[]{:S(2)}, u32[]{:S(2)}) %collective-permute-start.36) | collective-permute-done | bytes 524320 | tf_op jit(solution)/shard_map/ppermute | solution.py:214
  391.0 9.2 %collective-permute-done.35 = bf16[128,2048]{1,0:T(8,128)(2,1)S(1)} collective-permute-done((bf16[128,2048]{1,0:T(8,128)(2,1)S(1)}, bf16[128,2048]{1,0:T(8,128)(2,1)S(1)}, u32[]{:S(2)}, u32[]{:S(2)}) %collective-permute-start.35) | collective-permute-done | bytes 524320 | tf_op jit(solution)/shard_map/ppermute | solution.py:214
  400.2 15.8 %collective-permute-done.34 = bf16[128,2048]{1,0:T(8,128)(2,1)S(1)} collective-permute-done((bf16[128,2048]{1,0:T(8,128)(2,1)S(1)}, bf16[128,2048]{1,0:T(8,128)(2,1)S(1)}, u32[]{:S(2)}, u32[]{:S(2)}) %collective-permute-start.34) | collective-permute-done | bytes 524320 | tf_op jit(solution)/shard_map/ppermute | solution.py:229
  (145 shorter events, 103.5 us)
Async XLA Ops:
  6.5 315.1 %reduce-scatter.3.cloned.1.call-start = ((), (), s32[]{:S(2)}) async-start(), calls=%async_computation.2 | async-start | bytes 2621440 | tf_op jit(solution)/shard_map/reduce_scatter | solution.py:418
  17.4 42.5 %collective-permute-start = (bf16[128,4096]{1,0:T(8,128)(2,1)}, bf16[128,4096]{1,0:T(8,128)(2,1)S(1)}, u32[]{:S(2)}, u32[]{:S(2)}) collective-permute-start(bf16[128,4096]{1,0:T(8,128)(2,1)} %get-tuple-element.53), channel_id=1, source_target_pairs={{0,4},{4,0},{8,12},{12,8},{1,5},{5,1},{9,13},{13,9},{2,6},{6,2},{1... | collective-permute-start | bytes 3145736 | tf_op jit(solution)/shard_map/ppermute | solution.py:238
  21.1 99.8 %collective-permute-start.11 = (bf16[4096,512]{1,0:T(8,128)(2,1)}, bf16[4096,512]{1,0:T(8,128)(2,1)}, u32[]{:S(2)}, u32[]{:S(2)}) collective-permute-start(bf16[4096,512]{1,0:T(8,128)(2,1)} %refs_0_.3), channel_id=1, source_target_pairs={{0,2},{1,3},{2,0},{3,1},{4,6},{5,7},{6,4},{7,5},{8,10},{9,11},{10,... | collective-permute-start | bytes 12582920 | tf_op jit(solution)/shard_map/ppermute | solution.py:288
  38.4 73.0 %collective-permute-start.8 = (bf16[4096,512]{1,0:T(8,128)(2,1)}, bf16[4096,512]{1,0:T(8,128)(2,1)}, u32[]{:S(2)}, u32[]{:S(2)}) collective-permute-start(bf16[4096,512]{1,0:T(8,128)(2,1)} %refs_0_.3), channel_id=1, source_target_pairs={{0,1},{1,0},{2,3},{3,2},{4,5},{5,4},{6,7},{7,6},{8,9},{9,8},{10,11... | collective-permute-start | bytes 12582920 | tf_op jit(solution)/shard_map/ppermute | solution.py:288
  41.9 46.7 %collective-permute-start.5 = (bf16[128,4096]{1,0:T(8,128)(2,1)}, bf16[128,4096]{1,0:T(8,128)(2,1)S(1)}, u32[]{:S(2)}, u32[]{:S(2)}) collective-permute-start(bf16[128,4096]{1,0:T(8,128)(2,1)} %collective-permute-done.4), channel_id=1, source_target_pairs={{4,0},{8,12},{5,1},{9,13},{6,2},{10,14},{7,3},{11,15},{20,16},{24,... | collective-permute-start | bytes 3145736 | tf_op jit(solution)/shard_map/ppermute | solution.py:243
  62.2 48.8 %collective-permute-start.7 = (bf16[128,4096]{1,0:T(8,128)(2,1)S(1)}, bf16[128,4096]{1,0:T(8,128)(2,1)S(1)}, u32[]{:S(2)}, u32[]{:S(2)}) collective-permute-start(bf16[128,4096]{1,0:T(8,128)(2,1)S(1)} %collective-permute-done.6), channel_id=1, source_target_pairs={{4,0},{8,12},{5,1},{9,13},{6,2},{10,14},{7,3},{11,15},{20,16},{24,... | collective-permute-start | bytes 3145736 | tf_op jit(solution)/shard_map/ppermute | solution.py:245
  120.9 42.8 %collective-permute-start.12 = (bf16[4096,512]{1,0:T(8,128)(2,1)}, bf16[4096,512]{1,0:T(8,128)(2,1)}, u32[]{:S(2)}, u32[]{:S(2)}) collective-permute-start(bf16[4096,512]{1,0:T(8,128)(2,1)} %collective-permute-done.11.refs_0_), channel_id=1, source_target_pairs={{0,1},{1,0},{2,3},{3,2},{4,5},{5,4},{6,7},{7,6},{8,9},{9,8},{10,11... | collective-permute-start | bytes 12582920 | tf_op jit(solution)/shard_map/ppermute | solution.py:288
  121.0 105.7 %collective-permute-start.19 = (bf16[2048,1024]{1,0:T(8,128)(2,1)}, bf16[2048,1024]{1,0:T(8,128)(2,1)}, u32[]{:S(2)}, u32[]{:S(2)}) collective-permute-start(bf16[2048,1024]{1,0:T(8,128)(2,1)} %refs_4_.3), channel_id=1, source_target_pairs={{0,1},{1,0},{2,3},{3,2},{4,5},{5,4},{6,7},{7,6},{8,9},{9,8},{10,11... | collective-permute-start | bytes 12582920 | tf_op jit(solution)/shard_map/ppermute | solution.py:288
  126.2 59.4 %collective-permute-start.13 = (bf16[1024,1024]{1,0:T(8,128)(2,1)}, bf16[1024,1024]{1,0:T(8,128)(2,1)}, u32[]{:S(2)}, u32[]{:S(2)}) collective-permute-start(bf16[1024,1024]{1,0:T(8,128)(2,1)} %get-tuple-element.44), channel_id=1, source_target_pairs={{0,2},{1,3},{2,0},{3,1},{4,6},{5,7},{6,4},{7,5},{8,10},{9,11},{10,... | collective-permute-start | bytes 6291464 | tf_op jit(solution)/shard_map/ppermute | solution.py:288
  173.0 32.0 %collective-permute-start.15 = (bf16[512,1024]{1,0:T(8,128)(2,1)S(1)}, bf16[512,1024]{1,0:T(8,128)(2,1)}, u32[]{:S(2)}, u32[]{:S(2)}) collective-permute-start(bf16[512,1024]{1,0:T(8,128)(2,1)S(1)} %shard_map.66.own), channel_id=1, source_target_pairs={{16,0},{20,4},{8,24},{12,28},{17,1},{21,5},{9,25},{13,29},{18,2},{... | collective-permute-start | bytes 3145736 | tf_op jit(solution)/shard_map/ppermute | solution.py:359
  196.8 64.9 %collective-permute-start.21 = (bf16[1024,1024]{1,0:T(8,128)(2,1)}, bf16[1024,1024]{1,0:T(8,128)(2,1)}, u32[]{:S(2)}, u32[]{:S(2)}) collective-permute-start(bf16[1024,1024]{1,0:T(8,128)(2,1)} %get-tuple-element.43), channel_id=1, source_target_pairs={{0,2},{1,3},{2,0},{3,1},{4,6},{5,7},{6,4},{7,5},{8,10},{9,11},{10,... | collective-permute-start | bytes 6291464 | tf_op jit(solution)/shard_map/ppermute | solution.py:288
  198.5 29.1 %collective-permute-start.17 = (bf16[512,1024]{1,0:T(8,128)(2,1)S(1)}, bf16[512,1024]{1,0:T(8,128)(2,1)}, u32[]{:S(2)}, u32[]{:S(2)}) collective-permute-start(bf16[512,1024]{1,0:T(8,128)(2,1)S(1)} %shard_map.65.refs_0_), channel_id=1, source_target_pairs={{0,16},{4,20},{24,8},{28,12},{1,17},{5,21},{25,9},{29,13},{2,18},{... | collective-permute-start | bytes 3145736 | tf_op jit(solution)/shard_map/ppermute | solution.py:376
  208.2 38.9 %collective-permute-start.18 = (bf16[512,1024]{1,0:T(8,128)(2,1)}, bf16[512,1024]{1,0:T(8,128)(2,1)}, u32[]{:S(2)}, u32[]{:S(2)}) collective-permute-start(bf16[512,1024]{1,0:T(8,128)(2,1)} %shard_map.68.refs_1_), channel_id=1, source_target_pairs={{0,16},{4,20},{24,8},{28,12},{1,17},{5,21},{25,9},{29,13},{2,18},{... | collective-permute-start | bytes 3145736 | tf_op jit(solution)/shard_map/ppermute | solution.py:376
  221.8 36.3 %collective-permute-start.20 = (bf16[512,1024]{1,0:T(8,128)(2,1)S(1)}, bf16[512,1024]{1,0:T(8,128)(2,1)}, u32[]{:S(2)}, u32[]{:S(2)}) collective-permute-start(bf16[512,1024]{1,0:T(8,128)(2,1)S(1)} %shard_map.69.own), channel_id=1, source_target_pairs={{16,0},{20,4},{8,24},{12,28},{17,1},{21,5},{9,25},{13,29},{18,2},{... | collective-permute-start | bytes 3145736 | tf_op jit(solution)/shard_map/ppermute | solution.py:359
  257.8 158.6 %reduce-scatter.5.cloned.1.call-start = ((), (), s32[]{:S(2)}) async-start(), calls=%async_computation.3 | async-start | bytes 2621440 | tf_op jit(solution)/shard_map/reduce_scatter | solution.py:437
  262.2 48.5 %collective-permute-start.30 = (bf16[512,1024]{1,0:T(8,128)(2,1)S(1)}, bf16[512,1024]{1,0:T(8,128)(2,1)}, u32[]{:S(2)}, u32[]{:S(2)}) collective-permute-start(bf16[512,1024]{1,0:T(8,128)(2,1)S(1)} %copy-done.3), channel_id=1, source_target_pairs={{0,16},{4,20},{24,8},{28,12},{1,17},{5,21},{25,9},{29,13},{2,18},{... | collective-permute-start | bytes 3145736 | tf_op jit(solution)/shard_map/ppermute | solution.py:376
  267.7 44.2 %collective-permute-start.31 = (bf16[512,1024]{1,0:T(8,128)(2,1)}, bf16[512,1024]{1,0:T(8,128)(2,1)}, u32[]{:S(2)}, u32[]{:S(2)}) collective-permute-start(bf16[512,1024]{1,0:T(8,128)(2,1)} %copy-done.4), channel_id=1, source_target_pairs={{0,16},{4,20},{24,8},{28,12},{1,17},{5,21},{25,9},{29,13},{2,18},{... | collective-permute-start | bytes 3145736 | tf_op jit(solution)/shard_map/ppermute | solution.py:376
  288.0 99.8 %collective-permute-start.27 = (bf16[128,2048]{1,0:T(8,128)(2,1)}, bf16[128,2048]{1,0:T(8,128)(2,1)}, u32[]{:S(2)}, u32[]{:S(2)}) collective-permute-start(bf16[128,2048]{1,0:T(8,128)(2,1)} %get-tuple-element.50), channel_id=1, source_target_pairs={{0,4},{12,8},{1,5},{13,9},{2,6},{14,10},{3,7},{15,11},{16,20},{28,... | collective-permute-start | bytes 1572872 | tf_op jit(solution)/shard_map/ppermute | solution.py:214
  290.1 48.8 %collective-permute-start.28 = (bf16[128,2048]{1,0:T(8,128)(2,1)S(1)}, bf16[128,2048]{1,0:T(8,128)(2,1)}, u32[]{:S(2)}, u32[]{:S(2)}) collective-permute-start(bf16[128,2048]{1,0:T(8,128)(2,1)S(1)} %get-tuple-element.49), channel_id=1, source_target_pairs={{0,4},{12,8},{1,5},{13,9},{2,6},{14,10},{3,7},{15,11},{16,20},{28,... | collective-permute-start | bytes 1572872 | tf_op jit(solution)/shard_map/ppermute | solution.py:214
  332.8 27.7 %collective-permute-start.32 = (bf16[128,2048]{1,0:T(8,128)(2,1)S(1)}, bf16[128,2048]{1,0:T(8,128)(2,1)S(1)}, u32[]{:S(2)}, u32[]{:S(2)}) collective-permute-start(bf16[128,2048]{1,0:T(8,128)(2,1)S(1)} %get-tuple-element.45), channel_id=1, source_target_pairs={{0,4},{12,8},{1,5},{13,9},{2,6},{14,10},{3,7},{15,11},{16,20},{28,... | collective-permute-start | bytes 1572872 | tf_op jit(solution)/shard_map/ppermute | solution.py:214
  340.1 49.4 %collective-permute-start.29 = (bf16[128,2048]{1,0:T(8,128)(2,1)S(1)}, bf16[128,2048]{1,0:T(8,128)(2,1)S(1)}, u32[]{:S(2)}, u32[]{:S(2)}) collective-permute-start(bf16[128,2048]{1,0:T(8,128)(2,1)S(1)} %add_convert_fusion.6), channel_id=1, source_target_pairs={{4,8},{8,4},{5,9},{9,5},{6,10},{10,6},{7,11},{11,7},{20,24},{24,20... | collective-permute-start | bytes 1572872 | tf_op jit(solution)/shard_map/ppermute | solution.py:228
  340.8 41.5 %collective-permute-start.36 = (bf16[128,2048]{1,0:T(8,128)(2,1)S(1)}, bf16[128,2048]{1,0:T(8,128)(2,1)S(1)}, u32[]{:S(2)}, u32[]{:S(2)}) collective-permute-start(bf16[128,2048]{1,0:T(8,128)(2,1)S(1)} %get-tuple-element.46), channel_id=1, source_target_pairs={{0,4},{12,8},{1,5},{13,9},{2,6},{14,10},{3,7},{15,11},{16,20},{28,... | collective-permute-start | bytes 1572872 | tf_op jit(solution)/shard_map/ppermute | solution.py:214
  361.5 28.1 %collective-permute-start.26 = (bf16[128,2048]{1,0:T(8,128)(2,1)S(1)}, bf16[128,2048]{1,0:T(8,128)(2,1)S(1)}, u32[]{:S(2)}, u32[]{:S(2)}) collective-permute-start(bf16[128,2048]{1,0:T(8,128)(2,1)S(1)} %add_convert_fusion.7), channel_id=1, source_target_pairs={{4,0},{8,12},{5,1},{9,13},{6,2},{10,14},{7,3},{11,15},{20,16},{24,... | collective-permute-start | bytes 1572872 | tf_op jit(solution)/shard_map/ppermute | solution.py:229
  387.9 28.1 %collective-permute-start.34 = (bf16[128,2048]{1,0:T(8,128)(2,1)S(1)}, bf16[128,2048]{1,0:T(8,128)(2,1)S(1)}, u32[]{:S(2)}, u32[]{:S(2)}) collective-permute-start(bf16[128,2048]{1,0:T(8,128)(2,1)S(1)} %add_convert_fusion.3), channel_id=1, source_target_pairs={{4,0},{8,12},{5,1},{9,13},{6,2},{10,14},{7,3},{11,15},{20,16},{24,... | collective-permute-start | bytes 1572872 | tf_op jit(solution)/shard_map/ppermute | solution.py:229
  (29 other events, 504.3 us)
Sparse Core Ops, SparseCore 0:
  258.0 59.5 reduce-scatter.2
  321.8 71.1 reduce-scatter.4

commit v6 on v4

--- a/solution.py
+++ b/solution.py
@@ -218,15 +218,26 @@
         first = jnp.where(upper, self.size - 1 - if_lower, if_lower) * self.rows
         return lax.dynamic_slice_in_dim(self.partial, first, self.rows, 0)
 
+    def middle(self):
+        self.over = []
+        if self.size == 4:
+            self.over = [
+                lax.ppermute(
+                    added(self.part(i), came).astype(jnp.bfloat16), "col", [(1, 2), (2, 1)]
+                )
+                for i, came in zip((3, 2), self.begun)
+            ]
+        return self.over
+
     def end(self):
         if self.size != 4:
             summed = lax.psum_scatter(self.partial, "col", scatter_dimension=0, tiled=True)
             return summed.astype(jnp.float32)
-        across, outward = [(1, 2), (2, 1)], [(1, 0), (2, 3)]
-        from_3, from_2, from_1 = self.begun
-        over_3 = lax.ppermute(added(self.part(3), from_3).astype(jnp.bfloat16), "col", across)
-        over_2 = lax.ppermute(added(self.part(2), from_2).astype(jnp.bfloat16), "col", across)
-        out_0 = lax.ppermute(added(self.part(0), over_3).astype(jnp.bfloat16), "col", outward)
+        over_3, over_2 = self.over
+        from_1 = self.begun[2]
+        out_0 = lax.ppermute(
+            added(self.part(0), over_3).astype(jnp.bfloat16), "col", [(1, 0), (2, 3)]
+        )
         own = lax.dynamic_slice_in_dim(self.partial, self.place * self.rows, self.rows, 0)
         is_end = (self.place == 0) | (self.place == self.size - 1)
         return added(own) + jnp.where(is_end, added(out_0), added(from_1, over_2))
@@ -298,6 +309,12 @@
         bias_row = cross_bias[None, :]
         near, far = 0, 1
         in_group = [list(range(half)), list(range(half, n_batch))]
+        places = {}
+        for group in (near, far):
+            listed = []
+            for apart in in_group[group]:
+                listed += [first_base // piece_width + (batch ^ apart), batch ^ apart]
+            places[group] = jnp.stack(listed)
         products, came, mine, theirs, partial = {}, {}, {}, {}, {}
         latest = []
 
@@ -317,11 +334,8 @@
             products[step, group], came[step, group] = product, sum(sent[1:], sent[0])
 
         def finish(step, group, *others):
-            places = []
-            for apart in in_group[group]:
-                places += [first_base // piece_width + (batch ^ apart), batch ^ apart]
             crossed = finish_cross(
-                in_turn(jnp.stack(places), *others),
+                in_turn(places[group], *others),
                 products[step, group],
                 came[step, group],
                 gathered[step],
@@ -362,26 +376,27 @@
                 linear_pieces[half + place] = [part[place] for part in arrived]
 
         begun = {}
-        multiply(0, near)
+        multiply(0, near, meta, *kept_lists, *places.values())
         spread_far_cross(latest[-1])
         multiply(0, far)
         finish(0, near)
         finish(0, far)
-        linear(0, near, gathered[1])
+        multiply(1, near, linear_across[0])
+        multiply(1, far)
+        linear(0, near)
         summed_first = lax.psum_scatter(
             partial[0, near], "col", scatter_dimension=0, tiled=True
         )
-        multiply(1, near, linear_across[0])
-        multiply(1, far)
+        finish(1, near)
+        finish(1, far)
         linear_across[1] = after(linear_across[1], latest[-1])
         spread_far_linear()
-        finish(1, near)
-        linear(0, far)
+        linear(0, far, summed_first, theirs[1, near], theirs[1, far])
         begun[0] = LineSum(partial[0, far], col, n_col)
-        finish(1, far, summed_first, *begun[0].begun[:1])
-        linear(1, far)
+        linear(1, near)
+        linear(1, far, *begun[0].middle()[:1])
         begun[1] = LineSum(partial[1, far], col, n_col)
-        linear(1, near)
+        begun[1].middle()
 
         out = jnp.zeros((shard_rows, mixed_width * n_batch), jnp.bfloat16)
         for step, group in ((0, near), (0, far), (1, far), (1, near)):

time: 438 us -> 463 us (1.057)
  waiting for transfers between devices: 248 us -> 273 us
  starting transfers between devices: 53.4 us -> 43.7 us
    ppermute x4, waiting for transfers between devices: 48.8 us -> 76.8 us  [multiply(): sent = [lax.ppermute(product, ('row', 'col'), pairs) for pairs in turns]]
    all_gather x2, waiting for transfers between devices: 96.8 us -> 75.7 us  [on_device(): lax.all_gather(shard, 'col', axis=0, tiled=True)]
    ppermute x4, waiting for transfers between devices: 23.1 us -> 43.3 us  [finish(): lax.ppermute(crossed, ('row', 'col'), [(to, source) for source, to in pai...]
    ppermute x6, waiting for transfers between devices: 51.2 us -> 59.4 us  [__init__(): self.begun = [lax.ppermute(self.part(i), 'col', inward) for i in (3, 2, 1)]]
    ppermute x6, starting transfers between devices: 25.6 us -> 17.7 us  [__init__(): self.begun = [lax.ppermute(self.part(i), 'col', inward) for i in (3, 2, 1)]]
    ppermute x8, waiting for transfers between devices: 5.47 us -> 0.02 us  [to_batch(): return lax.ppermute(shard, 'batch', far_and_near(n_batch, bit))]
    ppermute x6, waiting for transfers between devices: 22.9 us -> 18.2 us  [the longest x2 18.1 us: end(): lax.ppermute(added(self.part(0), over_3).astype(jnp.bfloat16), 'col', [(1...]
    unnamed x42 -> x22, local copies, waits for them, and re-layouts: 11.4 us -> 7.82 us
  transfers between devices with their start and end apart: 32 -> 32, of which waited for: 16 -> 13; matrix products, arithmetic and copies ran while one was open for 4% -> 5% of each run, Pallas kernels for 19% -> 17%
where the time goes in v6:
time: 463 us; the launch traced here: 462 us
  waiting for transfers between devices  273 us (59%)
  Pallas kernels  88.4 us (19%)
  starting transfers between devices  43.7 us (9%)
  local copies, waits for them, and re-layouts  22.4 us (5%)
  other arithmetic  17.7 us (4%)
  between operations  16.3 us (4%)
    ppermute x4, waiting for transfers between devices, multiply(): sent = [lax.ppermute(product, ('row', 'col'), pairs) for pairs in turns]  76.8 us
    all_gather x2, waiting for transfers between devices, on_device(): lax.all_gather(shard, 'col', axis=0, tiled=True)  75.7 us
    ppermute x6, waiting for transfers between devices, __init__(): self.begun = [lax.ppermute(self.part(i), 'col', inward) for i in (3, 2, 1)]  59.4 us
    ppermute x4, waiting for transfers between devices, finish(): lax.ppermute(crossed, ('row', 'col'), [(to, source) for source, to in pai...  43.3 us
    pallas_call x4, Pallas kernels, linear_product(): pl.pallas_call(functools.partial(linear_kernel, groups, parts, per_piece)...  40.8 us
    pallas_call x4, Pallas kernels, cross_product(): pl.pallas_call(functools.partial(cross_kernel, steps), out_shape=jax.Shap...  37.8 us
    ppermute x2, waiting for transfers between devices, end(): lax.ppermute(added(self.part(0), over_3).astype(jnp.bfloat16), 'col', [(1...  18.1 us
    ppermute x6, starting transfers between devices, __init__(): self.begun = [lax.ppermute(self.part(i), 'col', inward) for i in (3, 2, 1)]  17.7 us
  transfers between devices with their start and end apart: 32, of which 13 were waited for; matrix products, arithmetic and copies ran while one was open for 5% of the time, Pallas kernels for 17%

profile of v6, /device:TPU:0, one launch (start us, length us, event | category | flops | bytes accessed | tf_op | source)
XLA Modules:
  0.0 461.9 jit_solution(9042804166712431232)
XLA Ops:
  6.5 3.1 fusion.5
  18.8 74.5 %all-gather.3.cloned.1.call-done.samples = bf16[512,4096]{1,0:T(8,128)(2,1)} async-done(((bf16[128,4096]{1,0:T(8,128)(2,1)}), bf16[512,4096]{1,0:T(8,128)(2,1)}) %all-gather.3.cloned.1.call-update) | async-done | bytes 4194320 | tf_op jit(solution)/shard_map/all_gather | solution.py:281
  95.4 10.2 %shard_map.64.own = bf16[512,1024]{1,0:T(8,128)(2,1)S(1)} custom-call(s32[18]{0:T(128)S(1)} %pad_add_fusion.1.meta, bf16[512,4096]{1,0:T(8,128)(2,1)S(1)} %copy-done.1, bf16[4096,512]{1,0:T(8,128)(2,1)} %refs_0_.3, bf16[4096,512]{1,0:T(8,128)(2,1)} %collective-permute-done.refs_1_), custom_call_target="tpu_custom_call" | custom-call | flops 2147483648 | bytes 9437184 | tf_op jit(solution)/shard_map/pallas_call | solution.py:52
  106.3 4.7 %fusion.4 = (bf16[1024,1024]{1,0:T(8,128)(2,1)}, bf16[1024,1024]{1,0:T(8,128)(2,1)}) fusion(bf16[2048,1024]{1,0:T(8,128)(2,1)} %refs_4_.3), kind=kLoop, calls=%fused_computation.40 | loop fusion | bytes 8388608 | tf_op jit(solution)/shard_map/split | solution.py:271
  119.3 8.7 %shard_map.65.own = bf16[512,1024]{1,0:T(8,128)(2,1)S(1)} custom-call(s32[18]{0:T(128)S(1)} %pad_add_fusion.meta, bf16[512,4096]{1,0:T(8,128)(2,1)S(1)} %copy-done.2, bf16[4096,512]{1,0:T(8,128)(2,1)} %collective-permute-done.1.refs_0_, bf16[4096,512]{1,0:T(8,128)(2,1)} %collective-permute-done.2.refs_1_), custom_call_target="tpu_custom_call" | custom-call | flops 2147483648 | bytes 9437184 | tf_op jit(solution)/shard_map/pallas_call | solution.py:52
  129.3 14.5 %collective-permute-done.3.came = bf16[512,1024]{1,0:T(8,128)(2,1)S(1)} collective-permute-done((bf16[512,1024]{1,0:T(8,128)(2,1)S(1)}, bf16[512,1024]{1,0:T(8,128)(2,1)S(1)}, u32[]{:S(2)}, u32[]{:S(2)}) %collective-permute-start.3) | collective-permute-done | bytes 1048608 | tf_op jit(solution)/shard_map/ppermute | solution.py:333
  148.5 17.2 %collective-permute-done.4.came = bf16[512,1024]{1,0:T(8,128)(2,1)S(1)} collective-permute-done((bf16[512,1024]{1,0:T(8,128)(2,1)S(1)}, bf16[512,1024]{1,0:T(8,128)(2,1)S(1)}, u32[]{:S(2)}, u32[]{:S(2)}) %collective-permute-start.4) | collective-permute-done | bytes 1048608 | tf_op jit(solution)/shard_map/ppermute | solution.py:333
  176.3 10.1 %shard_map.68.own = bf16[512,1024]{1,0:T(8,128)(2,1)S(1)} custom-call(s32[18]{0:T(128)S(1)} %pad_add_fusion.1.meta, bf16[512,4096]{1,0:T(8,128)(2,1)S(1)} %copy-done, bf16[4096,512]{1,0:T(8,128)(2,1)} %refs_0_.3, bf16[4096,512]{1,0:T(8,128)(2,1)} %collective-permute-done.refs_1_), custom_call_target="tpu_custom_call" | custom-call | flops 2147483648 | bytes 9437184 | tf_op jit(solution)/shard_map/pallas_call | solution.py:52
  186.5 8.7 %shard_map.69.own = bf16[512,1024]{1,0:T(8,128)(2,1)S(1)} custom-call(s32[18]{0:T(128)S(1)} %pad_add_fusion.meta, bf16[512,4096]{1,0:T(8,128)(2,1)S(1)} %copy-done, bf16[4096,512]{1,0:T(8,128)(2,1)} %collective-permute-done.1.refs_0_, bf16[4096,512]{1,0:T(8,128)(2,1)} %collective-permute-done.2.refs_1_), custom_call_target="tpu_custom_call" | custom-call | flops 2147483648 | bytes 9437184 | tf_op jit(solution)/shard_map/pallas_call | solution.py:52
  195.2 10.7 %shard_map.70 = bf16[512,2048]{1,0:T(8,128)(2,1)} custom-call(s32[7]{0:T(128)S(1)} %stack.57.meta, bf16[512,1024]{1,0:T(8,128)(2,1)S(1)} %shard_map.66.refs_0_, bf16[512,1024]{1,0:T(8,128)(2,1)} %shard_map.67.refs_1_, bf16[512,1024]{1,0:T(8,128)(2,1)} %collective-permute-done.6.refs_2_, bf16[512,1024]{1,0:T(8,128)(2,1)} %collective-permute-done.7.refs_3_, ...), custom_call_target="tpu_custom_call" | custom-call | flops 4294967296 | bytes 12582912 | tf_op jit(solution)/shard_map/pallas_call | solution.py:143
  208.7 25.8 %collective-permute-done.9.came = bf16[512,1024]{1,0:T(8,128)(2,1)S(1)} collective-permute-done((bf16[512,1024]{1,0:T(8,128)(2,1)S(1)}, bf16[512,1024]{1,0:T(8,128)(2,1)S(1)}, u32[]{:S(2)}, u32[]{:S(2)}) %collective-permute-start.9) | collective-permute-done | bytes 1048608 | tf_op jit(solution)/shard_map/ppermute | solution.py:333
  236.8 19.3 %collective-permute-done.10.came = bf16[512,1024]{1,0:T(8,128)(2,1)S(1)} collective-permute-done((bf16[512,1024]{1,0:T(8,128)(2,1)S(1)}, bf16[512,1024]{1,0:T(8,128)(2,1)S(1)}, u32[]{:S(2)}, u32[]{:S(2)}) %collective-permute-start.10) | collective-permute-done | bytes 1048608 | tf_op jit(solution)/shard_map/ppermute | solution.py:333
  262.3 21.1 %collective-permute-done.12.refs_3_ = bf16[512,1024]{1,0:T(8,128)(2,1)S(1)} collective-permute-done((bf16[512,1024]{1,0:T(8,128)(2,1)S(1)}, bf16[512,1024]{1,0:T(8,128)(2,1)S(1)}, u32[]{:S(2)}, u32[]{:S(2)}) %collective-permute-start.12) | collective-permute-done | bytes 1048608 | tf_op jit(solution)/shard_map/ppermute | solution.py:347
  283.4 22.2 %collective-permute-done.11.refs_2_ = bf16[512,1024]{1,0:T(8,128)(2,1)} collective-permute-done((bf16[512,1024]{1,0:T(8,128)(2,1)S(1)}, bf16[512,1024]{1,0:T(8,128)(2,1)}, u32[]{:S(2)}, u32[]{:S(2)}) %collective-permute-start.11) | collective-permute-done | bytes 1048608 | tf_op jit(solution)/shard_map/ppermute | solution.py:347
  306.9 10.6 %shard_map.73 = bf16[512,2048]{1,0:T(8,128)(2,1)} custom-call(s32[7]{0:T(128)S(1)} %stack.57.meta, bf16[512,1024]{1,0:T(8,128)(2,1)S(1)} %copy-done.4, bf16[512,1024]{1,0:T(8,128)(2,1)} %shard_map.67.refs_1_, bf16[512,1024]{1,0:T(8,128)(2,1)} %collective-permute-done.6.refs_2_, bf16[512,1024]{1,0:T(8,128)(2,1)} %collective-permute-done.7.refs_3_, ...), custom_call_target="tpu_custom_call" | custom-call | flops 4294967296 | bytes 12582912 | tf_op jit(solution)/shard_map/pallas_call | solution.py:143
  321.4 11.4 %collective-permute-done.16 = bf16[128,2048]{1,0:T(8,128)(2,1)S(1)} collective-permute-done((bf16[128,2048]{1,0:T(8,128)(2,1)S(1)}, bf16[128,2048]{1,0:T(8,128)(2,1)S(1)}, u32[]{:S(2)}, u32[]{:S(2)}) %collective-permute-start.16) | collective-permute-done | bytes 524320 | tf_op jit(solution)/shard_map/ppermute | solution.py:214
  335.2 7.6 %collective-permute-start.20 = (bf16[128,2048]{1,0:T(8,128)(2,1)}, bf16[128,2048]{1,0:T(8,128)(2,1)}, u32[]{:S(2)}, u32[]{:S(2)}) collective-permute-start(bf16[128,2048]{1,0:T(8,128)(2,1)} %get-tuple-element.47), channel_id=1, source_target_pairs={{0,4},{12,8},{1,5},{13,9},{2,6},{14,10},{3,7},{15,11},{16,20},{28,... | collective-permute-start | bytes 1572872 | tf_op jit(solution)/shard_map/ppermute | solution.py:214
  342.8 9.7 %shard_map.74 = bf16[512,2048]{1,0:T(8,128)(2,1)} custom-call(s32[7]{0:T(128)S(1)} %stack.57.meta, bf16[512,1024]{1,0:T(8,128)(2,1)S(1)} %shard_map.71.refs_0_, bf16[512,1024]{1,0:T(8,128)(2,1)S(1)} %shard_map.72.refs_1_, bf16[512,1024]{1,0:T(8,128)(2,1)} %collective-permute-done.11.refs_2_, bf16[512,1024]{1,0:T(8,128)(2,1)S(1)} %collective-permute-done.12.refs_3_, ...), custom_call_target="tpu_custom_call" | custom-call | flops 4294967296 | bytes 12582912 | tf_op jit(solution)/shard_map/pallas_call | solution.py:143
  352.5 9.7 %shard_map.75 = bf16[512,2048]{1,0:T(8,128)(2,1)} custom-call(s32[7]{0:T(128)S(1)} %stack.57.meta, bf16[512,1024]{1,0:T(8,128)(2,1)S(1)} %shard_map.71.refs_0_, bf16[512,1024]{1,0:T(8,128)(2,1)S(1)} %shard_map.72.refs_1_, bf16[512,1024]{1,0:T(8,128)(2,1)} %collective-permute-done.11.refs_2_, bf16[512,1024]{1,0:T(8,128)(2,1)S(1)} %collective-permute-done.12.refs_3_, ...), custom_call_target="tpu_custom_call" | custom-call | flops 4294967296 | bytes 12582912 | tf_op jit(solution)/shard_map/pallas_call | solution.py:143
  370.2 3.8 collective-permute-start.26
  375.5 14.5 %collective-permute-done.22 = bf16[128,2048]{1,0:T(8,128)(2,1)} collective-permute-done((bf16[128,2048]{1,0:T(8,128)(2,1)}, bf16[128,2048]{1,0:T(8,128)(2,1)}, u32[]{:S(2)}, u32[]{:S(2)}) %collective-permute-start.22) | collective-permute-done | bytes 524320 | tf_op jit(solution)/shard_map/ppermute | solution.py:214
  393.2 33.5 %collective-permute-done.26 = bf16[128,2048]{1,0:T(8,128)(2,1)S(1)} collective-permute-done((bf16[128,2048]{1,0:T(8,128)(2,1)S(1)}, bf16[128,2048]{1,0:T(8,128)(2,1)S(1)}, u32[]{:S(2)}, u32[]{:S(2)}) %collective-permute-start.26) | collective-permute-done | bytes 524320 | tf_op jit(solution)/shard_map/ppermute | solution.py:214
  433.0 10.5 %collective-permute-done.18 = bf16[128,2048]{1,0:T(8,128)(2,1)S(1)} collective-permute-done((bf16[128,2048]{1,0:T(8,128)(2,1)S(1)}, bf16[128,2048]{1,0:T(8,128)(2,1)S(1)}, u32[]{:S(2)}, u32[]{:S(2)}) %collective-permute-start.18) | collective-permute-done | bytes 524320 | tf_op jit(solution)/shard_map/ppermute | solution.py:238
  444.7 7.6 %collective-permute-done.24 = bf16[128,2048]{1,0:T(8,128)(2,1)S(1)} collective-permute-done((bf16[128,2048]{1,0:T(8,128)(2,1)S(1)}, bf16[128,2048]{1,0:T(8,128)(2,1)S(1)}, u32[]{:S(2)}, u32[]{:S(2)}) %collective-permute-start.24) | collective-permute-done | bytes 524320 | tf_op jit(solution)/shard_map/ppermute | solution.py:238
  (118 shorter events, 75.9 us)
Async XLA Ops:
  6.5 86.7 %all-gather.3.cloned.1.call-start = ((), (), s32[]{:S(2)}) async-start(), calls=%async_computation.2 | async-start | bytes 5242880 | tf_op jit(solution)/shard_map/all_gather | solution.py:281
  9.6 164.5 %all-gather.5.cloned.1.call-start = ((), (), s32[]{:S(2)}) async-start(), calls=%async_computation.3 | async-start | bytes 5242880 | tf_op jit(solution)/shard_map/all_gather | solution.py:281
  10.2 95.5 %collective-permute-start.1 = (bf16[4096,512]{1,0:T(8,128)(2,1)}, bf16[4096,512]{1,0:T(8,128)(2,1)}, u32[]{:S(2)}, u32[]{:S(2)}) collective-permute-start(bf16[4096,512]{1,0:T(8,128)(2,1)} %refs_0_.3), channel_id=1, source_target_pairs={{0,2},{1,3},{2,0},{3,1},{4,6},{5,7},{6,4},{7,5},{8,10},{9,11},{10,... | collective-permute-start | bytes 12582920 | tf_op jit(solution)/shard_map/ppermute | solution.py:260
  12.8 292.8 %reduce-scatter.3.cloned.1.call-start = ((), (), s32[]{:S(2)}) async-start(), calls=%async_computation.4 | async-start | bytes 2621440 | tf_op jit(solution)/shard_map/reduce_scatter | solution.py:387
  105.8 89.4 %collective-permute-start.8 = (bf16[2048,1024]{1,0:T(8,128)(2,1)}, bf16[2048,1024]{1,0:T(8,128)(2,1)}, u32[]{:S(2)}, u32[]{:S(2)}) collective-permute-start(bf16[2048,1024]{1,0:T(8,128)(2,1)} %refs_4_.3), channel_id=1, source_target_pairs={{0,1},{1,0},{2,3},{3,2},{4,5},{5,4},{6,7},{7,6},{8,9},{9,8},{10,11... | collective-permute-start | bytes 12582920 | tf_op jit(solution)/shard_map/ppermute | solution.py:260
  110.9 62.0 %collective-permute-start.5 = (bf16[1024,1024]{1,0:T(8,128)(2,1)}, bf16[1024,1024]{1,0:T(8,128)(2,1)}, u32[]{:S(2)}, u32[]{:S(2)}) collective-permute-start(bf16[1024,1024]{1,0:T(8,128)(2,1)} %get-tuple-element.42), channel_id=1, source_target_pairs={{0,2},{1,3},{2,0},{3,1},{4,6},{5,7},{6,4},{7,5},{8,10},{9,11},{10,... | collective-permute-start | bytes 6291464 | tf_op jit(solution)/shard_map/ppermute | solution.py:260
  115.8 28.0 %collective-permute-start.3 = (bf16[512,1024]{1,0:T(8,128)(2,1)S(1)}, bf16[512,1024]{1,0:T(8,128)(2,1)S(1)}, u32[]{:S(2)}, u32[]{:S(2)}) collective-permute-start(bf16[512,1024]{1,0:T(8,128)(2,1)S(1)} %shard_map.64.own), channel_id=1, source_target_pairs={{16,0},{20,4},{8,24},{12,28},{17,1},{21,5},{9,25},{13,29},{18,2},{... | collective-permute-start | bytes 3145736 | tf_op jit(solution)/shard_map/ppermute | solution.py:333
  128.0 37.7 %collective-permute-start.4 = (bf16[512,1024]{1,0:T(8,128)(2,1)S(1)}, bf16[512,1024]{1,0:T(8,128)(2,1)S(1)}, u32[]{:S(2)}, u32[]{:S(2)}) collective-permute-start(bf16[512,1024]{1,0:T(8,128)(2,1)S(1)} %shard_map.65.own), channel_id=1, source_target_pairs={{16,0},{20,4},{8,24},{12,28},{17,1},{21,5},{9,25},{13,29},{18,2},{... | collective-permute-start | bytes 3145736 | tf_op jit(solution)/shard_map/ppermute | solution.py:333
  146.1 49.1 %collective-permute-start.6 = (bf16[512,1024]{1,0:T(8,128)(2,1)S(1)}, bf16[512,1024]{1,0:T(8,128)(2,1)}, u32[]{:S(2)}, u32[]{:S(2)}) collective-permute-start(bf16[512,1024]{1,0:T(8,128)(2,1)S(1)} %shard_map.66.refs_0_), channel_id=1, source_target_pairs={{0,16},{4,20},{24,8},{28,12},{1,17},{5,21},{25,9},{29,13},{2,18},{... | collective-permute-start | bytes 3145736 | tf_op jit(solution)/shard_map/ppermute | solution.py:347
  168.8 26.4 %collective-permute-start.7 = (bf16[512,1024]{1,0:T(8,128)(2,1)}, bf16[512,1024]{1,0:T(8,128)(2,1)}, u32[]{:S(2)}, u32[]{:S(2)}) collective-permute-start(bf16[512,1024]{1,0:T(8,128)(2,1)} %shard_map.67.refs_1_), channel_id=1, source_target_pairs={{0,16},{4,20},{24,8},{28,12},{1,17},{5,21},{25,9},{29,13},{2,18},{... | collective-permute-start | bytes 3145736 | tf_op jit(solution)/shard_map/ppermute | solution.py:347
  171.2 87.2 %collective-permute-start.13 = (bf16[1024,1024]{1,0:T(8,128)(2,1)}, bf16[1024,1024]{1,0:T(8,128)(2,1)}, u32[]{:S(2)}, u32[]{:S(2)}) collective-permute-start(bf16[1024,1024]{1,0:T(8,128)(2,1)} %get-tuple-element.41), channel_id=1, source_target_pairs={{0,2},{1,3},{2,0},{3,1},{4,6},{5,7},{6,4},{7,5},{8,10},{9,11},{10,... | collective-permute-start | bytes 6291464 | tf_op jit(solution)/shard_map/ppermute | solution.py:260
  206.0 247.4 %reduce-scatter.5.cloned.1.call-start = ((), (), s32[]{:S(2)}) async-start(), calls=%async_computation.5 | async-start | bytes 2621440 | tf_op jit(solution)/shard_map/reduce_scatter | solution.py:408
  206.0 28.5 %collective-permute-start.9 = (bf16[512,1024]{1,0:T(8,128)(2,1)S(1)}, bf16[512,1024]{1,0:T(8,128)(2,1)S(1)}, u32[]{:S(2)}, u32[]{:S(2)}) collective-permute-start(bf16[512,1024]{1,0:T(8,128)(2,1)S(1)} %shard_map.68.own), channel_id=1, source_target_pairs={{16,0},{20,4},{8,24},{12,28},{17,1},{21,5},{9,25},{13,29},{18,2},{... | collective-permute-start | bytes 3145736 | tf_op jit(solution)/shard_map/ppermute | solution.py:333
  207.3 48.8 %collective-permute-start.10 = (bf16[512,1024]{1,0:T(8,128)(2,1)S(1)}, bf16[512,1024]{1,0:T(8,128)(2,1)S(1)}, u32[]{:S(2)}, u32[]{:S(2)}) collective-permute-start(bf16[512,1024]{1,0:T(8,128)(2,1)S(1)} %shard_map.69.own), channel_id=1, source_target_pairs={{16,0},{20,4},{8,24},{12,28},{17,1},{21,5},{9,25},{13,29},{18,2},{... | collective-permute-start | bytes 3145736 | tf_op jit(solution)/shard_map/ppermute | solution.py:333
  208.6 97.0 %collective-permute-start.14 = (bf16[1024,1024]{1,0:T(8,128)(2,1)}, bf16[1024,1024]{1,0:T(8,128)(2,1)}, u32[]{:S(2)}, u32[]{:S(2)}) collective-permute-start(bf16[1024,1024]{1,0:T(8,128)(2,1)} %collective-permute-done.5.refs_4_), channel_id=1, source_target_pairs={{0,1},{1,0},{2,3},{3,2},{4,5},{5,4},{6,7},{7,6},{8,9},{9,8},{10,11... | collective-permute-start | bytes 6291464 | tf_op jit(solution)/shard_map/ppermute | solution.py:260
  258.4 47.2 %collective-permute-start.15 = (bf16[1024,1024]{1,0:T(8,128)(2,1)}, bf16[1024,1024]{1,0:T(8,128)(2,1)}, u32[]{:S(2)}, u32[]{:S(2)}) collective-permute-start(bf16[1024,1024]{1,0:T(8,128)(2,1)} %collective-permute-done.13.refs_5_), channel_id=1, source_target_pairs={{0,1},{1,0},{2,3},{3,2},{4,5},{5,4},{6,7},{7,6},{8,9},{9,8},{10,11... | collective-permute-start | bytes 6291464 | tf_op jit(solution)/shard_map/ppermute | solution.py:260
  260.0 45.6 %collective-permute-start.11 = (bf16[512,1024]{1,0:T(8,128)(2,1)S(1)}, bf16[512,1024]{1,0:T(8,128)(2,1)}, u32[]{:S(2)}, u32[]{:S(2)}) collective-permute-start(bf16[512,1024]{1,0:T(8,128)(2,1)S(1)} %shard_map.71.refs_0_), channel_id=1, source_target_pairs={{0,16},{4,20},{24,8},{28,12},{1,17},{5,21},{25,9},{29,13},{2,18},{... | collective-permute-start | bytes 3145736 | tf_op jit(solution)/shard_map/ppermute | solution.py:347
  335.2 33.1 %collective-permute-start.20 = (bf16[128,2048]{1,0:T(8,128)(2,1)}, bf16[128,2048]{1,0:T(8,128)(2,1)}, u32[]{:S(2)}, u32[]{:S(2)}) collective-permute-start(bf16[128,2048]{1,0:T(8,128)(2,1)} %get-tuple-element.47), channel_id=1, source_target_pairs={{0,4},{12,8},{1,5},{13,9},{2,6},{14,10},{3,7},{15,11},{16,20},{28,... | collective-permute-start | bytes 1572872 | tf_op jit(solution)/shard_map/ppermute | solution.py:214
  364.8 25.2 %collective-permute-start.22 = (bf16[128,2048]{1,0:T(8,128)(2,1)}, bf16[128,2048]{1,0:T(8,128)(2,1)}, u32[]{:S(2)}, u32[]{:S(2)}) collective-permute-start(bf16[128,2048]{1,0:T(8,128)(2,1)} %get-tuple-element.43), channel_id=1, source_target_pairs={{0,4},{12,8},{1,5},{13,9},{2,6},{14,10},{3,7},{15,11},{16,20},{28,... | collective-permute-start | bytes 1572872 | tf_op jit(solution)/shard_map/ppermute | solution.py:214
  367.0 62.2 %collective-permute-start.19 = (bf16[128,2048]{1,0:T(8,128)(2,1)}, bf16[128,2048]{1,0:T(8,128)(2,1)S(1)}, u32[]{:S(2)}, u32[]{:S(2)}) collective-permute-start(bf16[128,2048]{1,0:T(8,128)(2,1)} %get-tuple-element.48), channel_id=1, source_target_pairs={{0,4},{12,8},{1,5},{13,9},{2,6},{14,10},{3,7},{15,11},{16,20},{28,... | collective-permute-start | bytes 1572872 | tf_op jit(solution)/shard_map/ppermute | solution.py:214
  369.5 63.4 %collective-permute-start.21 = (bf16[128,2048]{1,0:T(8,128)(2,1)S(1)}, bf16[128,2048]{1,0:T(8,128)(2,1)S(1)}, u32[]{:S(2)}, u32[]{:S(2)}) collective-permute-start(bf16[128,2048]{1,0:T(8,128)(2,1)S(1)} %add_convert_fusion.6), channel_id=1, source_target_pairs={{4,8},{8,4},{5,9},{9,5},{6,10},{10,6},{7,11},{11,7},{20,24},{24,20... | collective-permute-start | bytes 1572872 | tf_op jit(solution)/shard_map/ppermute | solution.py:225
  370.2 56.5 %collective-permute-start.26 = (bf16[128,2048]{1,0:T(8,128)(2,1)S(1)}, bf16[128,2048]{1,0:T(8,128)(2,1)S(1)}, u32[]{:S(2)}, u32[]{:S(2)}) collective-permute-start(bf16[128,2048]{1,0:T(8,128)(2,1)S(1)} %get-tuple-element.44), channel_id=1, source_target_pairs={{0,4},{12,8},{1,5},{13,9},{2,6},{14,10},{3,7},{15,11},{16,20},{28,... | collective-permute-start | bytes 1572872 | tf_op jit(solution)/shard_map/ppermute | solution.py:214
  374.1 70.6 %collective-permute-start.25 = (bf16[128,2048]{1,0:T(8,128)(2,1)}, bf16[128,2048]{1,0:T(8,128)(2,1)S(1)}, u32[]{:S(2)}, u32[]{:S(2)}) collective-permute-start(bf16[128,2048]{1,0:T(8,128)(2,1)} %get-tuple-element.45), channel_id=1, source_target_pairs={{0,4},{12,8},{1,5},{13,9},{2,6},{14,10},{3,7},{15,11},{16,20},{28,... | collective-permute-start | bytes 1572872 | tf_op jit(solution)/shard_map/ppermute | solution.py:214
  391.3 36.9 %collective-permute-start.23 = (bf16[128,2048]{1,0:T(8,128)(2,1)S(1)}, bf16[128,2048]{1,0:T(8,128)(2,1)S(1)}, u32[]{:S(2)}, u32[]{:S(2)}) collective-permute-start(bf16[128,2048]{1,0:T(8,128)(2,1)S(1)} %add_convert_fusion.4), channel_id=1, source_target_pairs={{4,8},{8,4},{5,9},{9,5},{6,10},{10,6},{7,11},{11,7},{20,24},{24,20... | collective-permute-start | bytes 1572872 | tf_op jit(solution)/shard_map/ppermute | solution.py:225
  (19 other events, 311.6 us)
Sparse Core Ops, SparseCore 0:
  9.8 83.4 all-gather.2
  94.8 79.2 all-gather.4
  206.1 43.7 reduce-scatter.2
  352.6 68.9 reduce-scatter.4

commit v7 on v6

--- a/solution.py
+++ b/solution.py
@@ -321,7 +321,7 @@
         def in_turn(meta, *others):
             return after(meta.astype(jnp.int32), *latest[-1:], *others)
 
-        def multiply(step, group, *others):
+        def multiply(step, group, *others, send=True):
             lists = jnp.concatenate([kept_lists[apart] for apart in in_group[group]])
             product = cross_product(
                 in_turn(lists, *others),
@@ -330,10 +330,12 @@
                 block,
             )
             latest.append(product)
-            sent = [lax.ppermute(product, ("row", "col"), pairs) for pairs in turns]
-            products[step, group], came[step, group] = product, sum(sent[1:], sent[0])
-
-        def finish(step, group, *others):
+            products[step, group] = product
+            if send:
+                sent = [lax.ppermute(product, ("row", "col"), pairs) for pairs in turns]
+                came[step, group] = sum(sent[1:], sent[0])
+
+        def finish(step, group, *others, beside=None):
             crossed = finish_cross(
                 in_turn(places[group], *others),
                 products[step, group],
@@ -343,11 +345,15 @@
                 half,
             )
             latest.append(crossed)
-            back = [
-                lax.ppermute(crossed, ("row", "col"), [(to, source) for source, to in pairs])
-                for pairs in turns
-            ]
+            returns = [[(to, source) for source, to in pairs] for pairs in turns]
+            sent = crossed
+            if beside is not None:
+                sent = jnp.where(is_owner, crossed, products[step, beside])
+                returns = [back + pairs for back, pairs in zip(returns, turns)]
+            back = [lax.ppermute(sent, ("row", "col"), pairs) for pairs in returns]
             mine[step, group], theirs[step, group] = crossed, sum(back[1:], back[0])
+            if beside is not None:
+                came[step, beside] = theirs[step, group]
 
         meta = jnp.stack(
             [is_owner.astype(jnp.int32)]
@@ -370,8 +376,8 @@
             arrived = spread_near({0: after(cross_across, *others)})
             cross_pieces.update({half + place: arrived[place] for place in range(half)})
 
-        def spread_far_linear():
-            arrived = [spread_near({0: part}) for part in linear_across]
+        def spread_far_linear(across):
+            arrived = [spread_near({0: part}) for part in across]
             for place in range(half):
                 linear_pieces[half + place] = [part[place] for part in arrived]
 
@@ -379,19 +385,19 @@
         multiply(0, near, meta, *kept_lists, *places.values())
         spread_far_cross(latest[-1])
         multiply(0, far)
-        finish(0, near)
+        finish(0, near, *(linear_pieces[place][0] for place in range(half)))
         finish(0, far)
         multiply(1, near, linear_across[0])
-        multiply(1, far)
+        multiply(1, far, send=False)
         linear(0, near)
         summed_first = lax.psum_scatter(
             partial[0, near], "col", scatter_dimension=0, tiled=True
         )
-        finish(1, near)
+        finish(1, near, beside=far)
         finish(1, far)
-        linear_across[1] = after(linear_across[1], latest[-1])
-        spread_far_linear()
-        linear(0, far, summed_first, theirs[1, near], theirs[1, far])
+        linear_across = [after(part, latest[-1]) for part in linear_across]
+        spread_far_linear(linear_across)
+        linear(0, far, summed_first, theirs[1, far])
         begun[0] = LineSum(partial[0, far], col, n_col)
         linear(1, near)
         linear(1, far, *begun[0].middle()[:1])

time: 463 us -> 427 us (0.922)
  waiting for transfers between devices: 273 us -> 239 us
    ppermute x4 -> x3, waiting for transfers between devices: 76.8 us -> 37.1 us  [multiply(): sent = [lax.ppermute(product, ('row', 'col'), pairs) for pairs in turns]]
  transfers between devices with their start and end apart: 32 -> 31, of which waited for: 13 -> 13; matrix products, arithmetic and copies ran while one was open for 5% -> 6% of each run, Pallas kernels for 17% -> 18%
where the time goes in v7:
time: 427 us; the launch traced here: 424 us
  waiting for transfers between devices  239 us (56%)
  Pallas kernels  87.3 us (20%)
  starting transfers between devices  40.9 us (10%)
  local copies, waits for them, and re-layouts  22.3 us (5%)
  other arithmetic  17.8 us (4%)
  between operations  16.3 us (4%)
    all_gather x2, waiting for transfers between devices, on_device(): lax.all_gather(shard, 'col', axis=0, tiled=True)  77.9 us
    ppermute x6, waiting for transfers between devices, __init__(): self.begun = [lax.ppermute(self.part(i), 'col', inward) for i in (3, 2, 1)]  58 us
    ppermute x4, waiting for transfers between devices, finish(): back = [lax.ppermute(sent, ('row', 'col'), pairs) for pairs in returns]  47.3 us
    pallas_call x4, Pallas kernels, linear_product(): pl.pallas_call(functools.partial(linear_kernel, groups, parts, per_piece)...  43.1 us
    ppermute x3, waiting for transfers between devices, multiply(): sent = [lax.ppermute(product, ('row', 'col'), pairs) for pairs in turns]  37.1 us
    pallas_call x4, Pallas kernels, cross_product(): pl.pallas_call(functools.partial(cross_kernel, steps), out_shape=jax.Shap...  33.3 us
    ppermute x2, waiting for transfers between devices, end(): lax.ppermute(added(self.part(0), over_3).astype(jnp.bfloat16), 'col', [(1...  17.7 us
    ppermute x6, starting transfers between devices, __init__(): self.begun = [lax.ppermute(self.part(i), 'col', inward) for i in (3, 2, 1)]  17.4 us
  transfers between devices with their start and end apart: 31, of which 13 were waited for; matrix products, arithmetic and copies ran while one was open for 6% of the time, Pallas kernels for 18%

profile of v7, /device:TPU:0, one launch (start us, length us, event | category | flops | bytes accessed | tf_op | source)
XLA Modules:
  0.0 423.6 jit_solution(13754397838554127842)
XLA Ops:
  6.5 3.1 fusion.5
  18.7 74.5 %all-gather.3.cloned.1.call-done.samples = bf16[512,4096]{1,0:T(8,128)(2,1)} async-done(((bf16[128,4096]{1,0:T(8,128)(2,1)}), bf16[512,4096]{1,0:T(8,128)(2,1)}) %all-gather.3.cloned.1.call-update) | async-done | bytes 4194320 | tf_op jit(solution)/shard_map/all_gather | solution.py:281
  95.4 7.9 %shard_map.64.own = bf16[512,1024]{1,0:T(8,128)(2,1)S(1)} custom-call(s32[18]{0:T(128)S(1)} %pad_add_fusion.1.meta, bf16[512,4096]{1,0:T(8,128)(2,1)S(1)} %copy-done.1, bf16[4096,512]{1,0:T(8,128)(2,1)} %refs_0_.3, bf16[4096,512]{1,0:T(8,128)(2,1)} %collective-permute-done.refs_1_), custom_call_target="tpu_custom_call" | custom-call | flops 2147483648 | bytes 9437184 | tf_op jit(solution)/shard_map/pallas_call | solution.py:52
  104.8 4.7 %fusion.4 = (bf16[1024,1024]{1,0:T(8,128)(2,1)}, bf16[1024,1024]{1,0:T(8,128)(2,1)}) fusion(bf16[2048,1024]{1,0:T(8,128)(2,1)} %refs_4_.3), kind=kLoop, calls=%fused_computation.41 | loop fusion | bytes 8388608 | tf_op jit(solution)/shard_map/split | solution.py:271
  119.4 8.8 %shard_map.65.own = bf16[512,1024]{1,0:T(8,128)(2,1)S(1)} custom-call(s32[18]{0:T(128)S(1)} %pad_add_fusion.meta, bf16[512,4096]{1,0:T(8,128)(2,1)S(1)} %copy-done.2, bf16[4096,512]{1,0:T(8,128)(2,1)} %collective-permute-done.1.refs_0_, bf16[4096,512]{1,0:T(8,128)(2,1)} %collective-permute-done.2.refs_1_), custom_call_target="tpu_custom_call" | custom-call | flops 2147483648 | bytes 9437184 | tf_op jit(solution)/shard_map/pallas_call | solution.py:52
  129.5 14.4 %collective-permute-done.4.came = bf16[512,1024]{1,0:T(8,128)(2,1)S(1)} collective-permute-done((bf16[512,1024]{1,0:T(8,128)(2,1)S(1)}, bf16[512,1024]{1,0:T(8,128)(2,1)S(1)}, u32[]{:S(2)}, u32[]{:S(2)}) %collective-permute-start.4) | collective-permute-done | bytes 1048608 | tf_op jit(solution)/shard_map/ppermute | solution.py:335
  148.6 16.4 %collective-permute-done.5.came = bf16[512,1024]{1,0:T(8,128)(2,1)S(1)} collective-permute-done((bf16[512,1024]{1,0:T(8,128)(2,1)S(1)}, bf16[512,1024]{1,0:T(8,128)(2,1)S(1)}, u32[]{:S(2)}, u32[]{:S(2)}) %collective-permute-start.5) | collective-permute-done | bytes 1048608 | tf_op jit(solution)/shard_map/ppermute | solution.py:335
  170.7 3.4 all-gather.5.cloned.1.call-done.samples
  176.3 7.9 %shard_map.68.own = bf16[512,1024]{1,0:T(8,128)(2,1)S(1)} custom-call(s32[18]{0:T(128)S(1)} %pad_add_fusion.1.meta, bf16[512,4096]{1,0:T(8,128)(2,1)S(1)} %copy-done, bf16[4096,512]{1,0:T(8,128)(2,1)} %refs_0_.3, bf16[4096,512]{1,0:T(8,128)(2,1)} %collective-permute-done.refs_1_), custom_call_target="tpu_custom_call" | custom-call | flops 2147483648 | bytes 9437184 | tf_op jit(solution)/shard_map/pallas_call | solution.py:52
  185.5 8.8 %shard_map.69.own = bf16[512,1024]{1,0:T(8,128)(2,1)S(1)} custom-call(s32[18]{0:T(128)S(1)} %pad_add_fusion.meta, bf16[512,4096]{1,0:T(8,128)(2,1)S(1)} %copy-done, bf16[4096,512]{1,0:T(8,128)(2,1)} %collective-permute-done.1.refs_0_, bf16[4096,512]{1,0:T(8,128)(2,1)} %collective-permute-done.2.refs_1_), custom_call_target="tpu_custom_call" | custom-call | flops 2147483648 | bytes 9437184 | tf_op jit(solution)/shard_map/pallas_call | solution.py:52
  194.3 10.7 %shard_map.70 = bf16[512,2048]{1,0:T(8,128)(2,1)} custom-call(s32[7]{0:T(128)S(1)} %stack.57.meta, bf16[512,1024]{1,0:T(8,128)(2,1)S(1)} %shard_map.66.refs_0_, bf16[512,1024]{1,0:T(8,128)(2,1)} %shard_map.67.refs_1_, bf16[512,1024]{1,0:T(8,128)(2,1)} %collective-permute-done.7.refs_2_, bf16[512,1024]{1,0:T(8,128)(2,1)} %collective-permute-done.8.refs_3_, ...), custom_call_target="tpu_custom_call" | custom-call | flops 4294967296 | bytes 12582912 | tf_op jit(solution)/shard_map/pallas_call | solution.py:143
  205.1 6.3 %collective-permute-done.9.came = bf16[512,1024]{1,0:T(8,128)(2,1)} collective-permute-done((bf16[512,1024]{1,0:T(8,128)(2,1)S(1)}, bf16[512,1024]{1,0:T(8,128)(2,1)}, u32[]{:S(2)}, u32[]{:S(2)}) %collective-permute-start.9) | collective-permute-done | bytes 1048608 | tf_op jit(solution)/shard_map/ppermute | solution.py:335
  214.1 24.4 %collective-permute-done.10.came.refs_2_ = bf16[512,1024]{1,0:T(8,128)(2,1)S(1)} collective-permute-done((bf16[512,1024]{1,0:T(8,128)(2,1)S(1)}, bf16[512,1024]{1,0:T(8,128)(2,1)S(1)}, u32[]{:S(2)}, u32[]{:S(2)}) %collective-permute-start.10) | collective-permute-done | bytes 1048608 | tf_op jit(solution)/shard_map/ppermute | solution.py:353
  238.5 3.1 shard_map.72.refs_1_
  244.4 22.9 %collective-permute-done.11.refs_3_ = bf16[512,1024]{1,0:T(8,128)(2,1)S(1)} collective-permute-done((bf16[512,1024]{1,0:T(8,128)(2,1)}, bf16[512,1024]{1,0:T(8,128)(2,1)S(1)}, u32[]{:S(2)}, u32[]{:S(2)}) %collective-permute-start.11) | collective-permute-done | bytes 1048608 | tf_op jit(solution)/shard_map/ppermute | solution.py:353
  268.5 10.6 %shard_map.73 = bf16[512,2048]{1,0:T(8,128)(2,1)} custom-call(s32[7]{0:T(128)S(1)} %stack.57.meta, bf16[512,1024]{1,0:T(8,128)(2,1)S(1)} %copy-done.4, bf16[512,1024]{1,0:T(8,128)(2,1)} %shard_map.67.refs_1_, bf16[512,1024]{1,0:T(8,128)(2,1)} %collective-permute-done.7.refs_2_, bf16[512,1024]{1,0:T(8,128)(2,1)} %collective-permute-done.8.refs_3_, ...), custom_call_target="tpu_custom_call" | custom-call | flops 4294967296 | bytes 12582912 | tf_op jit(solution)/shard_map/pallas_call | solution.py:143
  283.0 10.8 %collective-permute-done.15 = bf16[128,2048]{1,0:T(8,128)(2,1)S(1)} collective-permute-done((bf16[128,2048]{1,0:T(8,128)(2,1)S(1)}, bf16[128,2048]{1,0:T(8,128)(2,1)S(1)}, u32[]{:S(2)}, u32[]{:S(2)}) %collective-permute-start.15) | collective-permute-done | bytes 524320 | tf_op jit(solution)/shard_map/ppermute | solution.py:214
  296.2 9.8 %collective-permute-start.19 = (bf16[128,2048]{1,0:T(8,128)(2,1)}, bf16[128,2048]{1,0:T(8,128)(2,1)}, u32[]{:S(2)}, u32[]{:S(2)}) collective-permute-start(bf16[128,2048]{1,0:T(8,128)(2,1)} %get-tuple-element.49), channel_id=1, source_target_pairs={{0,4},{12,8},{1,5},{13,9},{2,6},{14,10},{3,7},{15,11},{16,20},{28,... | collective-permute-start | bytes 1572872 | tf_op jit(solution)/shard_map/ppermute | solution.py:214
  305.9 10.8 %shard_map.74 = bf16[512,2048]{1,0:T(8,128)(2,1)} custom-call(s32[7]{0:T(128)S(1)} %stack.57.meta, bf16[512,1024]{1,0:T(8,128)(2,1)S(1)} %shard_map.71.refs_0_, bf16[512,1024]{1,0:T(8,128)(2,1)} %shard_map.72.refs_1_, bf16[512,1024]{1,0:T(8,128)(2,1)S(1)} %collective-permute-done.10.came.refs_2_, bf16[512,1024]{1,0:T(8,128)(2,1)S(1)} %collective-permute-done.11.refs_3_, ...), custom_call_target="tpu_custom_call" | custom-call | flops 4294967296 | bytes 12582912 | tf_op jit(solution)/shard_map/pallas_call | solution.py:143
  316.8 11.0 %shard_map.75 = bf16[512,2048]{1,0:T(8,128)(2,1)} custom-call(s32[7]{0:T(128)S(1)} %stack.57.meta, bf16[512,1024]{1,0:T(8,128)(2,1)S(1)} %shard_map.71.refs_0_, bf16[512,1024]{1,0:T(8,128)(2,1)} %shard_map.72.refs_1_, bf16[512,1024]{1,0:T(8,128)(2,1)S(1)} %collective-permute-done.10.came.refs_2_, bf16[512,1024]{1,0:T(8,128)(2,1)S(1)} %collective-permute-done.11.refs_3_, ...), custom_call_target="tpu_custom_call" | custom-call | flops 4294967296 | bytes 12582912 | tf_op jit(solution)/shard_map/pallas_call | solution.py:143
  338.6 17.2 %collective-permute-done.21 = bf16[128,2048]{1,0:T(8,128)(2,1)} collective-permute-done((bf16[128,2048]{1,0:T(8,128)(2,1)}, bf16[128,2048]{1,0:T(8,128)(2,1)}, u32[]{:S(2)}, u32[]{:S(2)}) %collective-permute-start.21) | collective-permute-done | bytes 524320 | tf_op jit(solution)/shard_map/ppermute | solution.py:214
  359.0 30.0 %collective-permute-done.25 = bf16[128,2048]{1,0:T(8,128)(2,1)S(1)} collective-permute-done((bf16[128,2048]{1,0:T(8,128)(2,1)S(1)}, bf16[128,2048]{1,0:T(8,128)(2,1)S(1)}, u32[]{:S(2)}, u32[]{:S(2)}) %collective-permute-start.25) | collective-permute-done | bytes 524320 | tf_op jit(solution)/shard_map/ppermute | solution.py:214
  395.2 10.5 %collective-permute-done.17 = bf16[128,2048]{1,0:T(8,128)(2,1)S(1)} collective-permute-done((bf16[128,2048]{1,0:T(8,128)(2,1)S(1)}, bf16[128,2048]{1,0:T(8,128)(2,1)S(1)}, u32[]{:S(2)}, u32[]{:S(2)}) %collective-permute-start.17) | collective-permute-done | bytes 524320 | tf_op jit(solution)/shard_map/ppermute | solution.py:238
  406.9 7.1 %collective-permute-done.23 = bf16[128,2048]{1,0:T(8,128)(2,1)S(1)} collective-permute-done((bf16[128,2048]{1,0:T(8,128)(2,1)S(1)}, bf16[128,2048]{1,0:T(8,128)(2,1)S(1)}, u32[]{:S(2)}, u32[]{:S(2)}) %collective-permute-start.23) | collective-permute-done | bytes 524320 | tf_op jit(solution)/shard_map/ppermute | solution.py:238
  (117 shorter events, 72.4 us)
Async XLA Ops:
  6.5 86.7 %all-gather.3.cloned.1.call-start = ((), (), s32[]{:S(2)}) async-start(), calls=%async_computation.2 | async-start | bytes 5242880 | tf_op jit(solution)/shard_map/all_gather | solution.py:281
  9.6 164.5 %all-gather.5.cloned.1.call-start = ((), (), s32[]{:S(2)}) async-start(), calls=%async_computation.3 | async-start | bytes 5242880 | tf_op jit(solution)/shard_map/all_gather | solution.py:281
  10.2 94.0 %collective-permute-start.1 = (bf16[4096,512]{1,0:T(8,128)(2,1)}, bf16[4096,512]{1,0:T(8,128)(2,1)}, u32[]{:S(2)}, u32[]{:S(2)}) collective-permute-start(bf16[4096,512]{1,0:T(8,128)(2,1)} %refs_0_.3), channel_id=1, source_target_pairs={{0,2},{1,3},{2,0},{3,1},{4,6},{5,7},{6,4},{7,5},{8,10},{9,11},{10,... | collective-permute-start | bytes 12582920 | tf_op jit(solution)/shard_map/ppermute | solution.py:260
  12.8 254.5 %reduce-scatter.3.cloned.1.call-start = ((), (), s32[]{:S(2)}) async-start(), calls=%async_computation.4 | async-start | bytes 2621440 | tf_op jit(solution)/shard_map/reduce_scatter | solution.py:393
  104.3 25.2 %collective-permute-start.3 = (bf16[2048,1024]{1,0:T(8,128)(2,1)}, bf16[2048,1024]{1,0:T(8,128)(2,1)}, u32[]{:S(2)}, u32[]{:S(2)}) collective-permute-start(bf16[2048,1024]{1,0:T(8,128)(2,1)} %refs_4_.3), channel_id=1, source_target_pairs={{0,1},{1,0},{2,3},{3,2},{4,5},{5,4},{6,7},{7,6},{8,9},{9,8},{10,11... | collective-permute-start | bytes 12582920 | tf_op jit(solution)/shard_map/ppermute | solution.py:260
  109.4 61.3 %collective-permute-start.6 = (bf16[1024,1024]{1,0:T(8,128)(2,1)}, bf16[1024,1024]{1,0:T(8,128)(2,1)}, u32[]{:S(2)}, u32[]{:S(2)}) collective-permute-start(bf16[1024,1024]{1,0:T(8,128)(2,1)} %get-tuple-element.44), channel_id=1, source_target_pairs={{0,2},{1,3},{2,0},{3,1},{4,6},{5,7},{6,4},{7,5},{8,10},{9,11},{10,... | collective-permute-start | bytes 6291464 | tf_op jit(solution)/shard_map/ppermute | solution.py:260
  115.9 27.9 %collective-permute-start.4 = (bf16[512,1024]{1,0:T(8,128)(2,1)S(1)}, bf16[512,1024]{1,0:T(8,128)(2,1)S(1)}, u32[]{:S(2)}, u32[]{:S(2)}) collective-permute-start(bf16[512,1024]{1,0:T(8,128)(2,1)S(1)} %shard_map.64.own), channel_id=1, source_target_pairs={{16,0},{20,4},{8,24},{12,28},{17,1},{21,5},{9,25},{13,29},{18,2},{... | collective-permute-start | bytes 3145736 | tf_op jit(solution)/shard_map/ppermute | solution.py:335
  128.1 36.9 %collective-permute-start.5 = (bf16[512,1024]{1,0:T(8,128)(2,1)S(1)}, bf16[512,1024]{1,0:T(8,128)(2,1)S(1)}, u32[]{:S(2)}, u32[]{:S(2)}) collective-permute-start(bf16[512,1024]{1,0:T(8,128)(2,1)S(1)} %shard_map.65.own), channel_id=1, source_target_pairs={{16,0},{20,4},{8,24},{12,28},{17,1},{21,5},{9,25},{13,29},{18,2},{... | collective-permute-start | bytes 3145736 | tf_op jit(solution)/shard_map/ppermute | solution.py:335
  146.1 48.2 %collective-permute-start.7 = (bf16[512,1024]{1,0:T(8,128)(2,1)S(1)}, bf16[512,1024]{1,0:T(8,128)(2,1)}, u32[]{:S(2)}, u32[]{:S(2)}) collective-permute-start(bf16[512,1024]{1,0:T(8,128)(2,1)S(1)} %shard_map.66.refs_0_), channel_id=1, source_target_pairs={{0,16},{4,20},{24,8},{28,12},{1,17},{5,21},{25,9},{29,13},{2,18},{... | collective-permute-start | bytes 3145736 | tf_op jit(solution)/shard_map/ppermute | solution.py:353
  168.0 26.3 %collective-permute-start.8 = (bf16[512,1024]{1,0:T(8,128)(2,1)}, bf16[512,1024]{1,0:T(8,128)(2,1)}, u32[]{:S(2)}, u32[]{:S(2)}) collective-permute-start(bf16[512,1024]{1,0:T(8,128)(2,1)} %shard_map.67.refs_1_), channel_id=1, source_target_pairs={{0,16},{4,20},{24,8},{28,12},{1,17},{5,21},{25,9},{29,13},{2,18},{... | collective-permute-start | bytes 3145736 | tf_op jit(solution)/shard_map/ppermute | solution.py:353
  170.5 71.2 %collective-permute-start.12 = (bf16[1024,1024]{1,0:T(8,128)(2,1)}, bf16[1024,1024]{1,0:T(8,128)(2,1)}, u32[]{:S(2)}, u32[]{:S(2)}) collective-permute-start(bf16[1024,1024]{1,0:T(8,128)(2,1)} %get-tuple-element.43), channel_id=1, source_target_pairs={{0,2},{1,3},{2,0},{3,1},{4,6},{5,7},{6,4},{7,5},{8,10},{9,11},{10,... | collective-permute-start | bytes 6291464 | tf_op jit(solution)/shard_map/ppermute | solution.py:260
  184.2 27.3 %collective-permute-start.9 = (bf16[512,1024]{1,0:T(8,128)(2,1)S(1)}, bf16[512,1024]{1,0:T(8,128)(2,1)}, u32[]{:S(2)}, u32[]{:S(2)}) collective-permute-start(bf16[512,1024]{1,0:T(8,128)(2,1)S(1)} %shard_map.68.own), channel_id=1, source_target_pairs={{16,0},{20,4},{8,24},{12,28},{17,1},{21,5},{9,25},{13,29},{18,2},{... | collective-permute-start | bytes 3145736 | tf_op jit(solution)/shard_map/ppermute | solution.py:335
  205.1 210.1 %reduce-scatter.5.cloned.1.call-start = ((), (), s32[]{:S(2)}) async-start(), calls=%async_computation.5 | async-start | bytes 2621440 | tf_op jit(solution)/shard_map/reduce_scatter | solution.py:414
  214.0 24.5 %collective-permute-start.10 = (bf16[512,1024]{1,0:T(8,128)(2,1)S(1)}, bf16[512,1024]{1,0:T(8,128)(2,1)S(1)}, u32[]{:S(2)}, u32[]{:S(2)}) collective-permute-start(bf16[512,1024]{1,0:T(8,128)(2,1)S(1)} %broadcast_select_fusion), channel_id=1, source_target_pairs={{0,16},{4,20},{24,8},{28,12},{16,0},{20,4},{8,24},{12,28},{1,17},{... | collective-permute-start | bytes 3145736 | tf_op jit(solution)/shard_map/ppermute | solution.py:353
  241.6 25.6 %collective-permute-start.14 = (bf16[1024,1024]{1,0:T(8,128)(2,1)}, bf16[1024,1024]{1,0:T(8,128)(2,1)}, u32[]{:S(2)}, u32[]{:S(2)}) collective-permute-start(bf16[1024,1024]{1,0:T(8,128)(2,1)} %collective-permute-done.12.refs_5_), channel_id=1, source_target_pairs={{0,1},{1,0},{2,3},{3,2},{4,5},{5,4},{6,7},{7,6},{8,9},{9,8},{10,11... | collective-permute-start | bytes 6291464 | tf_op jit(solution)/shard_map/ppermute | solution.py:260
  241.6 25.6 %collective-permute-start.13 = (bf16[1024,1024]{1,0:T(8,128)(2,1)}, bf16[1024,1024]{1,0:T(8,128)(2,1)}, u32[]{:S(2)}, u32[]{:S(2)}) collective-permute-start(bf16[1024,1024]{1,0:T(8,128)(2,1)} %collective-permute-done.6.refs_4_), channel_id=1, source_target_pairs={{0,1},{1,0},{2,3},{3,2},{4,5},{5,4},{6,7},{7,6},{8,9},{9,8},{10,11... | collective-permute-start | bytes 6291464 | tf_op jit(solution)/shard_map/ppermute | solution.py:260
  242.1 25.1 %collective-permute-start.11 = (bf16[512,1024]{1,0:T(8,128)(2,1)}, bf16[512,1024]{1,0:T(8,128)(2,1)S(1)}, u32[]{:S(2)}, u32[]{:S(2)}) collective-permute-start(bf16[512,1024]{1,0:T(8,128)(2,1)} %shard_map.72.refs_1_), channel_id=1, source_target_pairs={{0,16},{4,20},{24,8},{28,12},{1,17},{5,21},{25,9},{29,13},{2,18},{... | collective-permute-start | bytes 3145736 | tf_op jit(solution)/shard_map/ppermute | solution.py:353
  296.2 37.7 %collective-permute-start.19 = (bf16[128,2048]{1,0:T(8,128)(2,1)}, bf16[128,2048]{1,0:T(8,128)(2,1)}, u32[]{:S(2)}, u32[]{:S(2)}) collective-permute-start(bf16[128,2048]{1,0:T(8,128)(2,1)} %get-tuple-element.49), channel_id=1, source_target_pairs={{0,4},{12,8},{1,5},{13,9},{2,6},{14,10},{3,7},{15,11},{16,20},{28,... | collective-permute-start | bytes 1572872 | tf_op jit(solution)/shard_map/ppermute | solution.py:214
  330.3 25.5 %collective-permute-start.21 = (bf16[128,2048]{1,0:T(8,128)(2,1)}, bf16[128,2048]{1,0:T(8,128)(2,1)}, u32[]{:S(2)}, u32[]{:S(2)}) collective-permute-start(bf16[128,2048]{1,0:T(8,128)(2,1)} %get-tuple-element.45), channel_id=1, source_target_pairs={{0,4},{12,8},{1,5},{13,9},{2,6},{14,10},{3,7},{15,11},{16,20},{28,... | collective-permute-start | bytes 1572872 | tf_op jit(solution)/shard_map/ppermute | solution.py:214
  332.5 58.9 %collective-permute-start.18 = (bf16[128,2048]{1,0:T(8,128)(2,1)}, bf16[128,2048]{1,0:T(8,128)(2,1)S(1)}, u32[]{:S(2)}, u32[]{:S(2)}) collective-permute-start(bf16[128,2048]{1,0:T(8,128)(2,1)} %get-tuple-element.50), channel_id=1, source_target_pairs={{0,4},{12,8},{1,5},{13,9},{2,6},{14,10},{3,7},{15,11},{16,20},{28,... | collective-permute-start | bytes 1572872 | tf_op jit(solution)/shard_map/ppermute | solution.py:214
  335.1 60.1 %collective-permute-start.20 = (bf16[128,2048]{1,0:T(8,128)(2,1)S(1)}, bf16[128,2048]{1,0:T(8,128)(2,1)S(1)}, u32[]{:S(2)}, u32[]{:S(2)}) collective-permute-start(bf16[128,2048]{1,0:T(8,128)(2,1)S(1)} %add_convert_fusion.6), channel_id=1, source_target_pairs={{4,8},{8,4},{5,9},{9,5},{6,10},{10,6},{7,11},{11,7},{20,24},{24,20... | collective-permute-start | bytes 1572872 | tf_op jit(solution)/shard_map/ppermute | solution.py:225
  335.8 53.2 %collective-permute-start.25 = (bf16[128,2048]{1,0:T(8,128)(2,1)S(1)}, bf16[128,2048]{1,0:T(8,128)(2,1)S(1)}, u32[]{:S(2)}, u32[]{:S(2)}) collective-permute-start(bf16[128,2048]{1,0:T(8,128)(2,1)S(1)} %get-tuple-element.46), channel_id=1, source_target_pairs={{0,4},{12,8},{1,5},{13,9},{2,6},{14,10},{3,7},{15,11},{16,20},{28,... | collective-permute-start | bytes 1572872 | tf_op jit(solution)/shard_map/ppermute | solution.py:214
  337.1 69.8 %collective-permute-start.24 = (bf16[128,2048]{1,0:T(8,128)(2,1)}, bf16[128,2048]{1,0:T(8,128)(2,1)S(1)}, u32[]{:S(2)}, u32[]{:S(2)}) collective-permute-start(bf16[128,2048]{1,0:T(8,128)(2,1)} %get-tuple-element.47), channel_id=1, source_target_pairs={{0,4},{12,8},{1,5},{13,9},{2,6},{14,10},{3,7},{15,11},{16,20},{28,... | collective-permute-start | bytes 1572872 | tf_op jit(solution)/shard_map/ppermute | solution.py:214
  357.1 33.3 %collective-permute-start.22 = (bf16[128,2048]{1,0:T(8,128)(2,1)S(1)}, bf16[128,2048]{1,0:T(8,128)(2,1)S(1)}, u32[]{:S(2)}, u32[]{:S(2)}) collective-permute-start(bf16[128,2048]{1,0:T(8,128)(2,1)S(1)} %add_convert_fusion.4), channel_id=1, source_target_pairs={{4,8},{8,4},{5,9},{9,5},{6,10},{10,6},{7,11},{11,7},{20,24},{24,20... | collective-permute-start | bytes 1572872 | tf_op jit(solution)/shard_map/ppermute | solution.py:225
  (18 other events, 288.8 us)
Sparse Core Ops, SparseCore 0:
  9.8 83.4 all-gather.2
  94.8 79.2 all-gather.4
  205.2 47.9 reduce-scatter.2
  316.9 67.4 reduce-scatter.4

commit v8 on v7

--- a/solution.py
+++ b/solution.py
@@ -15,7 +15,7 @@
     return [(place, place ^ bit) for place in range(size)]
 
 
-def cross_kernel(steps, meta, samples, *refs):
+def cross_kernel(steps, first, meta, samples, *refs):
     weights, out, total = refs[:-2], refs[-2], refs[-1]
     step = lax.rem(pl.program_id(0), steps)
     piece = pl.program_id(0) // steps
@@ -26,7 +26,7 @@
 
     for place, weight in enumerate(weights):
 
-        @pl.when((piece == place) & (step < meta[place * (steps + 1)]))
+        @pl.when((piece == place) & (step < meta[(first + place) * (steps + 1)]))
         def _():
             total[...] += jnp.dot(samples[...], weight[...], preferred_element_type=jnp.float32)
 
@@ -35,13 +35,13 @@
         out[...] = total[...].astype(out.dtype)
 
 
-def cross_product(meta, samples, weights, block):
+def cross_product(meta, first, samples, weights, block):
     rows, depth = samples.shape
     columns = weights[0].shape[1]
     steps = depth // block
 
     def listed(place, step, meta):
-        return meta[place * (steps + 1) + 1 + step]
+        return meta[(first + place) * (steps + 1) + 1 + step]
 
     def weight_spec(place):
         return pl.BlockSpec(
@@ -50,7 +50,7 @@
         )
 
     return pl.pallas_call(
-        functools.partial(cross_kernel, steps),
+        functools.partial(cross_kernel, steps, first),
         out_shape=jax.ShapeDtypeStruct((rows, columns * len(weights)), jnp.bfloat16),
         grid_spec=pltpu.PrefetchScalarGridSpec(
             num_scalar_prefetch=1,
@@ -317,14 +317,16 @@
             places[group] = jnp.stack(listed)
         products, came, mine, theirs, partial = {}, {}, {}, {}, {}
         latest = []
+        lists = jnp.concatenate(kept_lists).astype(jnp.int32)
+        lists = after(lists, *parts)
 
         def in_turn(meta, *others):
             return after(meta.astype(jnp.int32), *latest[-1:], *others)
 
         def multiply(step, group, *others, send=True):
-            lists = jnp.concatenate([kept_lists[apart] for apart in in_group[group]])
             product = cross_product(
                 in_turn(lists, *others),
+                in_group[group][0],
                 gathered[step],
                 [cross_pieces[apart] for apart in in_group[group]],
                 block,
@@ -382,7 +384,7 @@
                 linear_pieces[half + place] = [part[place] for part in arrived]
 
         begun = {}
-        multiply(0, near, meta, *kept_lists, *places.values())
+        multiply(0, near)
         spread_far_cross(latest[-1])
         multiply(0, far)
         finish(0, near, *(linear_pieces[place][0] for place in range(half)))
@@ -400,8 +402,9 @@
         linear(0, far, summed_first, theirs[1, far])
         begun[0] = LineSum(partial[0, far], col, n_col)
         linear(1, near)
-        linear(1, far, *begun[0].middle()[:1])
+        linear(1, far, *begun[0].begun[:1])
         begun[1] = LineSum(partial[1, far], col, n_col)
+        begun[0].middle()
         begun[1].middle()
 
         out = jnp.zeros((shard_rows, mixed_width * n_batch), jnp.bfloat16)

time: 427 us -> 426 us (level)
  waiting for transfers between devices: 239 us -> 249 us
  other arithmetic: 17.8 us -> 11.9 us
  starting transfers between devices: 40.9 us -> 35.5 us
    ppermute x2, waiting for transfers between devices: 17.7 us -> 31.3 us  [end(): lax.ppermute(added(self.part(0), over_3).astype(jnp.bfloat16), 'col', [(1...]
    ppermute x3, waiting for transfers between devices: 37.1 us -> 26 us  [multiply(): sent = [lax.ppermute(product, ('row', 'col'), pairs) for pairs in turns]]
    ppermute x8, waiting for transfers between devices: 0.92 us -> 11.2 us  [to_batch(): return lax.ppermute(shard, 'batch', far_and_near(n_batch, bit))]
    ppermute x6, starting transfers between devices: 17.4 us -> 12.8 us  [__init__(): self.begun = [lax.ppermute(self.part(i), 'col', inward) for i in (3, 2, 1)]]
    unnamed x22 -> x24, local copies, waits for them, and re-layouts: 7.82 us -> 9.93 us
  transfers between devices with their start and end apart: 31 -> 31, of which waited for: 13 -> 13; matrix products, arithmetic and copies ran while one was open for 6% -> 5% of each run, Pallas kernels for 18% -> 18%
where the time goes in v8:
time: 426 us; the launch traced here: 424 us
  waiting for transfers between devices  249 us (58%)
  Pallas kernels  87.2 us (20%)
  starting transfers between devices  35.5 us (8%)
  local copies, waits for them, and re-layouts  24.9 us (6%)
  between operations  16.4 us (4%)
  other arithmetic  11.9 us (3%)
    all_gather x2, waiting for transfers between devices, on_device(): lax.all_gather(shard, 'col', axis=0, tiled=True)  78.3 us
    ppermute x6, waiting for transfers between devices, __init__(): self.begun = [lax.ppermute(self.part(i), 'col', inward) for i in (3, 2, 1)]  54.8 us
    ppermute x4, waiting for transfers between devices, finish(): back = [lax.ppermute(sent, ('row', 'col'), pairs) for pairs in returns]  46.8 us
    pallas_call x4, Pallas kernels, linear_product(): pl.pallas_call(functools.partial(linear_kernel, groups, parts, per_piece)...  43.3 us
    pallas_call x4, Pallas kernels, cross_product(): pl.pallas_call(functools.partial(cross_kernel, steps, first), out_shape=j...  32.2 us
    ppermute x2, waiting for transfers between devices, end(): lax.ppermute(added(self.part(0), over_3).astype(jnp.bfloat16), 'col', [(1...  31.3 us
    ppermute x3, waiting for transfers between devices, multiply(): sent = [lax.ppermute(product, ('row', 'col'), pairs) for pairs in turns]  26 us
    ppermute x6, starting transfers between devices, __init__(): self.begun = [lax.ppermute(self.part(i), 'col', inward) for i in (3, 2, 1)]  12.8 us
  transfers between devices with their start and end apart: 31, of which 13 were waited for; matrix products, arithmetic and copies ran while one was open for 5% of the time, Pallas kernels for 18%

profile of v8, /device:TPU:0, one launch (start us, length us, event | category | flops | bytes accessed | tf_op | source)
XLA Modules:
  0.0 424.4 jit_solution(8566402653470291291)
XLA Ops:
  6.5 3.1 fusion.5
  23.0 4.7 %fusion.4 = (bf16[1024,1024]{1,0:T(8,128)(2,1)}, bf16[1024,1024]{1,0:T(8,128)(2,1)}) fusion(bf16[2048,1024]{1,0:T(8,128)(2,1)} %refs_4_.3), kind=kLoop, calls=%fused_computation.39 | loop fusion | bytes 8388608 | tf_op jit(solution)/shard_map/split | solution.py:271
  27.7 65.6 %all-gather.3.cloned.1.call-done.samples = bf16[512,4096]{1,0:T(8,128)(2,1)} async-done(((bf16[128,4096]{1,0:T(8,128)(2,1)}), bf16[512,4096]{1,0:T(8,128)(2,1)}) %all-gather.3.cloned.1.call-update) | async-done | bytes 4194320 | tf_op jit(solution)/shard_map/all_gather | solution.py:281
  95.5 7.4 %shard_map.64.own = bf16[512,1024]{1,0:T(8,128)(2,1)S(1)} custom-call(s32[36]{0:T(128)S(1)} %concatenate.3.meta, bf16[512,4096]{1,0:T(8,128)(2,1)S(1)} %copy-done.1, bf16[4096,512]{1,0:T(8,128)(2,1)} %refs_0_.3, bf16[4096,512]{1,0:T(8,128)(2,1)} %collective-permute-done.refs_1_), custom_call_target="tpu_custom_call" | custom-call | flops 2147483648 | bytes 9437184 | tf_op jit(solution)/shard_map/pallas_call | solution.py:52
  107.9 9.8 %collective-permute-done.2.refs_1_ = bf16[4096,512]{1,0:T(8,128)(2,1)S(1)} collective-permute-done((bf16[4096,512]{1,0:T(8,128)(2,1)}, bf16[4096,512]{1,0:T(8,128)(2,1)S(1)}, u32[]{:S(2)}, u32[]{:S(2)}) %collective-permute-start.2) | collective-permute-done | bytes 4194336 | tf_op jit(solution)/shard_map/ppermute | solution.py:260
  119.6 8.8 %shard_map.65.own = bf16[512,1024]{1,0:T(8,128)(2,1)S(1)} custom-call(s32[36]{0:T(128)S(1)} %concatenate.3.meta, bf16[512,4096]{1,0:T(8,128)(2,1)S(1)} %copy-done.1, bf16[4096,512]{1,0:T(8,128)(2,1)} %collective-permute-done.1.refs_0_, bf16[4096,512]{1,0:T(8,128)(2,1)} %copy-done.5), custom_call_target="tpu_custom_call" | custom-call | flops 2147483648 | bytes 9437184 | tf_op jit(solution)/shard_map/pallas_call | solution.py:52
  130.0 3.4 collective-permute-done.4.came
  133.4 3.2 shard_map.66.refs_0_
  138.9 16.9 %collective-permute-done.5.came = bf16[512,1024]{1,0:T(8,128)(2,1)S(1)} collective-permute-done((bf16[512,1024]{1,0:T(8,128)(2,1)S(1)}, bf16[512,1024]{1,0:T(8,128)(2,1)S(1)}, u32[]{:S(2)}, u32[]{:S(2)}) %collective-permute-start.5) | collective-permute-done | bytes 1048608 | tf_op jit(solution)/shard_map/ppermute | solution.py:337
  161.6 12.6 %all-gather.5.cloned.1.call-done.samples = bf16[512,4096]{1,0:T(8,128)(2,1)} async-done(((bf16[128,4096]{1,0:T(8,128)(2,1)}), bf16[512,4096]{1,0:T(8,128)(2,1)}) %all-gather.5.cloned.1.call-update) | async-done | bytes 4194320 | tf_op jit(solution)/shard_map/all_gather | solution.py:281
  176.4 7.2 %shard_map.68.own = bf16[512,1024]{1,0:T(8,128)(2,1)S(1)} custom-call(s32[36]{0:T(128)S(1)} %concatenate.3.meta, bf16[512,4096]{1,0:T(8,128)(2,1)S(1)} %copy-done, bf16[4096,512]{1,0:T(8,128)(2,1)} %refs_0_.3, bf16[4096,512]{1,0:T(8,128)(2,1)} %collective-permute-done.refs_1_), custom_call_target="tpu_custom_call" | custom-call | flops 2147483648 | bytes 9437184 | tf_op jit(solution)/shard_map/pallas_call | solution.py:52
  185.0 8.8 %shard_map.69.own = bf16[512,1024]{1,0:T(8,128)(2,1)S(1)} custom-call(s32[36]{0:T(128)S(1)} %concatenate.3.meta, bf16[512,4096]{1,0:T(8,128)(2,1)S(1)} %copy-done, bf16[4096,512]{1,0:T(8,128)(2,1)} %collective-permute-done.1.refs_0_, bf16[4096,512]{1,0:T(8,128)(2,1)} %copy-done.5), custom_call_target="tpu_custom_call" | custom-call | flops 2147483648 | bytes 9437184 | tf_op jit(solution)/shard_map/pallas_call | solution.py:52
  193.8 10.9 %shard_map.70 = bf16[512,2048]{1,0:T(8,128)(2,1)} custom-call(s32[7]{0:T(128)S(1)} %stack.57.meta, bf16[512,1024]{1,0:T(8,128)(2,1)} %shard_map.66.refs_0_, bf16[512,1024]{1,0:T(8,128)(2,1)} %shard_map.67.refs_1_, bf16[512,1024]{1,0:T(8,128)(2,1)} %collective-permute-done.7.refs_2_, bf16[512,1024]{1,0:T(8,128)(2,1)} %collective-permute-done.8.refs_3_, ...), custom_call_target="tpu_custom_call" | custom-call | flops 4294967296 | bytes 12582912 | tf_op jit(solution)/shard_map/pallas_call | solution.py:143
  204.8 5.7 %collective-permute-done.9.came = bf16[512,1024]{1,0:T(8,128)(2,1)S(1)} collective-permute-done((bf16[512,1024]{1,0:T(8,128)(2,1)S(1)}, bf16[512,1024]{1,0:T(8,128)(2,1)S(1)}, u32[]{:S(2)}, u32[]{:S(2)}) %collective-permute-start.9) | collective-permute-done | bytes 1048608 | tf_op jit(solution)/shard_map/ppermute | solution.py:337
  215.4 24.0 %collective-permute-done.10.came.refs_2_ = bf16[512,1024]{1,0:T(8,128)(2,1)S(1)} collective-permute-done((bf16[512,1024]{1,0:T(8,128)(2,1)S(1)}, bf16[512,1024]{1,0:T(8,128)(2,1)S(1)}, u32[]{:S(2)}, u32[]{:S(2)}) %collective-permute-start.10) | collective-permute-done | bytes 1048608 | tf_op jit(solution)/shard_map/ppermute | solution.py:355
  245.2 22.9 %collective-permute-done.11.refs_3_ = bf16[512,1024]{1,0:T(8,128)(2,1)S(1)} collective-permute-done((bf16[512,1024]{1,0:T(8,128)(2,1)}, bf16[512,1024]{1,0:T(8,128)(2,1)S(1)}, u32[]{:S(2)}, u32[]{:S(2)}) %collective-permute-start.11) | collective-permute-done | bytes 1048608 | tf_op jit(solution)/shard_map/ppermute | solution.py:355
  268.1 10.9 %shard_map.73 = bf16[512,2048]{1,0:T(8,128)(2,1)} custom-call(s32[7]{0:T(128)S(1)} %stack.57.meta, bf16[512,1024]{1,0:T(8,128)(2,1)} %shard_map.66.refs_0_, bf16[512,1024]{1,0:T(8,128)(2,1)} %shard_map.67.refs_1_, bf16[512,1024]{1,0:T(8,128)(2,1)} %collective-permute-done.7.refs_2_, bf16[512,1024]{1,0:T(8,128)(2,1)} %collective-permute-done.8.refs_3_, ...), custom_call_target="tpu_custom_call" | custom-call | flops 4294967296 | bytes 12582912 | tf_op jit(solution)/shard_map/pallas_call | solution.py:143
  281.5 4.6 %collective-permute-start.15 = (bf16[128,2048]{1,0:T(8,128)(2,1)}, bf16[128,2048]{1,0:T(8,128)(2,1)}, u32[]{:S(2)}, u32[]{:S(2)}) collective-permute-start(bf16[128,2048]{1,0:T(8,128)(2,1)} %get-tuple-element.48), channel_id=1, source_target_pairs={{0,4},{12,8},{1,5},{13,9},{2,6},{14,10},{3,7},{15,11},{16,20},{28,... | collective-permute-start | bytes 1572872 | tf_op jit(solution)/shard_map/ppermute | solution.py:214
  290.4 10.8 %shard_map.74 = bf16[512,2048]{1,0:T(8,128)(2,1)} custom-call(s32[7]{0:T(128)S(1)} %stack.57.meta, bf16[512,1024]{1,0:T(8,128)(2,1)S(1)} %shard_map.71.refs_0_, bf16[512,1024]{1,0:T(8,128)(2,1)} %shard_map.72.refs_1_, bf16[512,1024]{1,0:T(8,128)(2,1)S(1)} %collective-permute-done.10.came.refs_2_, bf16[512,1024]{1,0:T(8,128)(2,1)S(1)} %collective-permute-done.11.refs_3_, ...), custom_call_target="tpu_custom_call" | custom-call | flops 4294967296 | bytes 12582912 | tf_op jit(solution)/shard_map/pallas_call | solution.py:143
  301.2 10.7 %shard_map.75 = bf16[512,2048]{1,0:T(8,128)(2,1)} custom-call(s32[7]{0:T(128)S(1)} %stack.57.meta, bf16[512,1024]{1,0:T(8,128)(2,1)S(1)} %shard_map.71.refs_0_, bf16[512,1024]{1,0:T(8,128)(2,1)} %shard_map.72.refs_1_, bf16[512,1024]{1,0:T(8,128)(2,1)S(1)} %collective-permute-done.10.came.refs_2_, bf16[512,1024]{1,0:T(8,128)(2,1)S(1)} %collective-permute-done.11.refs_3_, ...), custom_call_target="tpu_custom_call" | custom-call | flops 4294967296 | bytes 12582912 | tf_op jit(solution)/shard_map/pallas_call | solution.py:143
  320.9 34.9 %collective-permute-done.21 = bf16[128,2048]{1,0:T(8,128)(2,1)S(1)} collective-permute-done((bf16[128,2048]{1,0:T(8,128)(2,1)S(1)}, bf16[128,2048]{1,0:T(8,128)(2,1)S(1)}, u32[]{:S(2)}, u32[]{:S(2)}) %collective-permute-start.21) | collective-permute-done | bytes 524320 | tf_op jit(solution)/shard_map/ppermute | solution.py:214
  356.7 19.9 %collective-permute-done.25 = bf16[128,2048]{1,0:T(8,128)(2,1)S(1)} collective-permute-done((bf16[128,2048]{1,0:T(8,128)(2,1)S(1)}, bf16[128,2048]{1,0:T(8,128)(2,1)S(1)}, u32[]{:S(2)}, u32[]{:S(2)}) %collective-permute-start.25) | collective-permute-done | bytes 524320 | tf_op jit(solution)/shard_map/ppermute | solution.py:214
  381.5 27.1 %collective-permute-done.17 = bf16[128,2048]{1,0:T(8,128)(2,1)S(1)} collective-permute-done((bf16[128,2048]{1,0:T(8,128)(2,1)S(1)}, bf16[128,2048]{1,0:T(8,128)(2,1)S(1)}, u32[]{:S(2)}, u32[]{:S(2)}) %collective-permute-start.17) | collective-permute-done | bytes 524320 | tf_op jit(solution)/shard_map/ppermute | solution.py:238
  410.1 4.2 collective-permute-done.23
  (118 shorter events, 69.9 us)
Async XLA Ops:
  6.5 86.8 %all-gather.3.cloned.1.call-start = ((), (), s32[]{:S(2)}) async-start(), calls=%async_computation.2 | async-start | bytes 5242880 | tf_op jit(solution)/shard_map/all_gather | solution.py:281
  9.7 164.5 %all-gather.5.cloned.1.call-start = ((), (), s32[]{:S(2)}) async-start(), calls=%async_computation.3 | async-start | bytes 5242880 | tf_op jit(solution)/shard_map/all_gather | solution.py:281
  10.3 94.0 %collective-permute-start.1 = (bf16[4096,512]{1,0:T(8,128)(2,1)}, bf16[4096,512]{1,0:T(8,128)(2,1)}, u32[]{:S(2)}, u32[]{:S(2)}) collective-permute-start(bf16[4096,512]{1,0:T(8,128)(2,1)} %refs_0_.3), channel_id=1, source_target_pairs={{0,2},{1,3},{2,0},{3,1},{4,6},{5,7},{6,4},{7,5},{8,10},{9,11},{10,... | collective-permute-start | bytes 12582920 | tf_op jit(solution)/shard_map/ppermute | solution.py:260
  12.9 255.2 %reduce-scatter.3.cloned.1.call-start = ((), (), s32[]{:S(2)}) async-start(), calls=%async_computation.4 | async-start | bytes 2621440 | tf_op jit(solution)/shard_map/reduce_scatter | solution.py:395
  104.8 56.7 %collective-permute-start.6 = (bf16[1024,1024]{1,0:T(8,128)(2,1)}, bf16[1024,1024]{1,0:T(8,128)(2,1)}, u32[]{:S(2)}, u32[]{:S(2)}) collective-permute-start(bf16[1024,1024]{1,0:T(8,128)(2,1)} %get-tuple-element.44), channel_id=1, source_target_pairs={{0,2},{1,3},{2,0},{3,1},{4,6},{5,7},{6,4},{7,5},{8,10},{9,11},{10,... | collective-permute-start | bytes 6291464 | tf_op jit(solution)/shard_map/ppermute | solution.py:260
  106.6 26.8 %collective-permute-start.4 = (bf16[512,1024]{1,0:T(8,128)(2,1)S(1)}, bf16[512,1024]{1,0:T(8,128)(2,1)}, u32[]{:S(2)}, u32[]{:S(2)}) collective-permute-start(bf16[512,1024]{1,0:T(8,128)(2,1)S(1)} %shard_map.64.own), channel_id=1, source_target_pairs={{16,0},{20,4},{8,24},{12,28},{17,1},{21,5},{9,25},{13,29},{18,2},{... | collective-permute-start | bytes 3145736 | tf_op jit(solution)/shard_map/ppermute | solution.py:337
  128.4 27.3 %collective-permute-start.5 = (bf16[512,1024]{1,0:T(8,128)(2,1)S(1)}, bf16[512,1024]{1,0:T(8,128)(2,1)S(1)}, u32[]{:S(2)}, u32[]{:S(2)}) collective-permute-start(bf16[512,1024]{1,0:T(8,128)(2,1)S(1)} %shard_map.65.own), channel_id=1, source_target_pairs={{16,0},{20,4},{8,24},{12,28},{17,1},{21,5},{9,25},{13,29},{18,2},{... | collective-permute-start | bytes 3145736 | tf_op jit(solution)/shard_map/ppermute | solution.py:337
  136.6 57.2 %collective-permute-start.7 = (bf16[512,1024]{1,0:T(8,128)(2,1)}, bf16[512,1024]{1,0:T(8,128)(2,1)}, u32[]{:S(2)}, u32[]{:S(2)}) collective-permute-start(bf16[512,1024]{1,0:T(8,128)(2,1)} %shard_map.66.refs_0_), channel_id=1, source_target_pairs={{0,16},{4,20},{24,8},{28,12},{1,17},{5,21},{25,9},{29,13},{2,18},{... | collective-permute-start | bytes 3145736 | tf_op jit(solution)/shard_map/ppermute | solution.py:355
  158.8 34.9 %collective-permute-start.8 = (bf16[512,1024]{1,0:T(8,128)(2,1)}, bf16[512,1024]{1,0:T(8,128)(2,1)}, u32[]{:S(2)}, u32[]{:S(2)}) collective-permute-start(bf16[512,1024]{1,0:T(8,128)(2,1)} %shard_map.67.refs_1_), channel_id=1, source_target_pairs={{0,16},{4,20},{24,8},{28,12},{1,17},{5,21},{25,9},{29,13},{2,18},{... | collective-permute-start | bytes 3145736 | tf_op jit(solution)/shard_map/ppermute | solution.py:355
  161.3 81.1 %collective-permute-start.12 = (bf16[1024,1024]{1,0:T(8,128)(2,1)}, bf16[1024,1024]{1,0:T(8,128)(2,1)}, u32[]{:S(2)}, u32[]{:S(2)}) collective-permute-start(bf16[1024,1024]{1,0:T(8,128)(2,1)} %get-tuple-element.43), channel_id=1, source_target_pairs={{0,2},{1,3},{2,0},{3,1},{4,6},{5,7},{6,4},{7,5},{8,10},{9,11},{10,... | collective-permute-start | bytes 6291464 | tf_op jit(solution)/shard_map/ppermute | solution.py:260
  183.7 26.9 %collective-permute-start.9 = (bf16[512,1024]{1,0:T(8,128)(2,1)S(1)}, bf16[512,1024]{1,0:T(8,128)(2,1)S(1)}, u32[]{:S(2)}, u32[]{:S(2)}) collective-permute-start(bf16[512,1024]{1,0:T(8,128)(2,1)S(1)} %shard_map.68.own), channel_id=1, source_target_pairs={{16,0},{20,4},{8,24},{12,28},{17,1},{21,5},{9,25},{13,29},{18,2},{... | collective-permute-start | bytes 3145736 | tf_op jit(solution)/shard_map/ppermute | solution.py:337
  204.7 209.9 %reduce-scatter.5.cloned.1.call-start = ((), (), s32[]{:S(2)}) async-start(), calls=%async_computation.5 | async-start | bytes 2621440 | tf_op jit(solution)/shard_map/reduce_scatter | solution.py:417
  242.4 25.6 %collective-permute-start.14 = (bf16[1024,1024]{1,0:T(8,128)(2,1)}, bf16[1024,1024]{1,0:T(8,128)(2,1)}, u32[]{:S(2)}, u32[]{:S(2)}) collective-permute-start(bf16[1024,1024]{1,0:T(8,128)(2,1)} %collective-permute-done.12.refs_5_), channel_id=1, source_target_pairs={{0,1},{1,0},{2,3},{3,2},{4,5},{5,4},{6,7},{7,6},{8,9},{9,8},{10,11... | collective-permute-start | bytes 6291464 | tf_op jit(solution)/shard_map/ppermute | solution.py:260
  242.4 25.6 %collective-permute-start.13 = (bf16[1024,1024]{1,0:T(8,128)(2,1)}, bf16[1024,1024]{1,0:T(8,128)(2,1)}, u32[]{:S(2)}, u32[]{:S(2)}) collective-permute-start(bf16[1024,1024]{1,0:T(8,128)(2,1)} %collective-permute-done.6.refs_4_), channel_id=1, source_target_pairs={{0,1},{1,0},{2,3},{3,2},{4,5},{5,4},{6,7},{7,6},{8,9},{9,8},{10,11... | collective-permute-start | bytes 6291464 | tf_op jit(solution)/shard_map/ppermute | solution.py:260
  286.2 32.7 %collective-permute-start.19 = (bf16[128,2048]{1,0:T(8,128)(2,1)}, bf16[128,2048]{1,0:T(8,128)(2,1)}, u32[]{:S(2)}, u32[]{:S(2)}) collective-permute-start(bf16[128,2048]{1,0:T(8,128)(2,1)} %get-tuple-element.49), channel_id=1, source_target_pairs={{0,4},{12,8},{1,5},{13,9},{2,6},{14,10},{3,7},{15,11},{16,20},{28,... | collective-permute-start | bytes 1572872 | tf_op jit(solution)/shard_map/ppermute | solution.py:214
  288.3 91.6 %collective-permute-start.18 = (bf16[128,2048]{1,0:T(8,128)(2,1)}, bf16[128,2048]{1,0:T(8,128)(2,1)}, u32[]{:S(2)}, u32[]{:S(2)}) collective-permute-start(bf16[128,2048]{1,0:T(8,128)(2,1)} %get-tuple-element.50), channel_id=1, source_target_pairs={{0,4},{12,8},{1,5},{13,9},{2,6},{14,10},{3,7},{15,11},{16,20},{28,... | collective-permute-start | bytes 1572872 | tf_op jit(solution)/shard_map/ppermute | solution.py:214
  313.5 42.3 %collective-permute-start.21 = (bf16[128,2048]{1,0:T(8,128)(2,1)S(1)}, bf16[128,2048]{1,0:T(8,128)(2,1)S(1)}, u32[]{:S(2)}, u32[]{:S(2)}) collective-permute-start(bf16[128,2048]{1,0:T(8,128)(2,1)S(1)} %get-tuple-element.45), channel_id=1, source_target_pairs={{0,4},{12,8},{1,5},{13,9},{2,6},{14,10},{3,7},{15,11},{16,20},{28,... | collective-permute-start | bytes 1572872 | tf_op jit(solution)/shard_map/ppermute | solution.py:214
  314.9 61.7 %collective-permute-start.25 = (bf16[128,2048]{1,0:T(8,128)(2,1)S(1)}, bf16[128,2048]{1,0:T(8,128)(2,1)S(1)}, u32[]{:S(2)}, u32[]{:S(2)}) collective-permute-start(bf16[128,2048]{1,0:T(8,128)(2,1)S(1)} %get-tuple-element.46), channel_id=1, source_target_pairs={{0,4},{12,8},{1,5},{13,9},{2,6},{14,10},{3,7},{15,11},{16,20},{28,... | collective-permute-start | bytes 1572872 | tf_op jit(solution)/shard_map/ppermute | solution.py:214
  316.2 93.9 %collective-permute-start.24 = (bf16[128,2048]{1,0:T(8,128)(2,1)S(1)}, bf16[128,2048]{1,0:T(8,128)(2,1)S(1)}, u32[]{:S(2)}, u32[]{:S(2)}) collective-permute-start(bf16[128,2048]{1,0:T(8,128)(2,1)S(1)} %get-tuple-element.47), channel_id=1, source_target_pairs={{0,4},{12,8},{1,5},{13,9},{2,6},{14,10},{3,7},{15,11},{16,20},{28,... | collective-permute-start | bytes 1572872 | tf_op jit(solution)/shard_map/ppermute | solution.py:214
  318.9 58.5 %collective-permute-start.16 = (bf16[128,2048]{1,0:T(8,128)(2,1)S(1)}, bf16[128,2048]{1,0:T(8,128)(2,1)S(1)}, u32[]{:S(2)}, u32[]{:S(2)}) collective-permute-start(bf16[128,2048]{1,0:T(8,128)(2,1)S(1)} %add_convert_fusion.8), channel_id=1, source_target_pairs={{4,8},{8,4},{5,9},{9,5},{6,10},{10,6},{7,11},{11,7},{20,24},{24,20... | collective-permute-start | bytes 1572872 | tf_op jit(solution)/shard_map/ppermute | solution.py:225
  355.8 25.7 %collective-permute-start.20 = (bf16[128,2048]{1,0:T(8,128)(2,1)S(1)}, bf16[128,2048]{1,0:T(8,128)(2,1)S(1)}, u32[]{:S(2)}, u32[]{:S(2)}) collective-permute-start(bf16[128,2048]{1,0:T(8,128)(2,1)S(1)} %add_convert_fusion.6), channel_id=1, source_target_pairs={{4,8},{8,4},{5,9},{9,5},{6,10},{10,6},{7,11},{11,7},{20,24},{24,20... | collective-permute-start | bytes 1572872 | tf_op jit(solution)/shard_map/ppermute | solution.py:225
  377.4 32.7 %collective-permute-start.26 = (bf16[128,2048]{1,0:T(8,128)(2,1)S(1)}, bf16[128,2048]{1,0:T(8,128)(2,1)S(1)}, u32[]{:S(2)}, u32[]{:S(2)}) collective-permute-start(bf16[128,2048]{1,0:T(8,128)(2,1)S(1)} %add_convert_fusion.2), channel_id=1, source_target_pairs={{4,8},{8,4},{5,9},{9,5},{6,10},{10,6},{7,11},{11,7},{20,24},{24,20... | collective-permute-start | bytes 1572872 | tf_op jit(solution)/shard_map/ppermute | solution.py:225
  378.3 30.4 %collective-permute-start.17 = (bf16[128,2048]{1,0:T(8,128)(2,1)S(1)}, bf16[128,2048]{1,0:T(8,128)(2,1)S(1)}, u32[]{:S(2)}, u32[]{:S(2)}) collective-permute-start(bf16[128,2048]{1,0:T(8,128)(2,1)S(1)} %add_convert_fusion.7), channel_id=1, source_target_pairs={{4,0},{8,12},{5,1},{9,13},{6,2},{10,14},{7,3},{11,15},{20,16},{24,... | collective-permute-start | bytes 1572872 | tf_op jit(solution)/shard_map/ppermute | solution.py:238
  379.9 34.4 %collective-permute-start.23 = (bf16[128,2048]{1,0:T(8,128)(2,1)S(1)}, bf16[128,2048]{1,0:T(8,128)(2,1)S(1)}, u32[]{:S(2)}, u32[]{:S(2)}) collective-permute-start(bf16[128,2048]{1,0:T(8,128)(2,1)S(1)} %add_convert_fusion.3), channel_id=1, source_target_pairs={{4,0},{8,12},{5,1},{9,13},{6,2},{10,14},{7,3},{11,15},{20,16},{24,... | collective-permute-start | bytes 1572872 | tf_op jit(solution)/shard_map/ppermute | solution.py:238
  (19 other events, 304.1 us)
Sparse Core Ops, SparseCore 0:
  9.8 83.4 all-gather.2
  94.9 79.2 all-gather.4
  204.9 46.9 reduce-scatter.2
  301.3 75.7 reduce-scatter.4

commit v9 on v8

--- a/solution.py
+++ b/solution.py
@@ -399,20 +399,20 @@
         finish(1, far)
         linear_across = [after(part, latest[-1]) for part in linear_across]
         spread_far_linear(linear_across)
-        linear(0, far, summed_first, theirs[1, far])
-        begun[0] = LineSum(partial[0, far], col, n_col)
+        linear(0, far, summed_first)
+        summed_far = lax.psum_scatter(partial[0, far], "col", scatter_dimension=0, tiled=True)
         linear(1, near)
-        linear(1, far, *begun[0].begun[:1])
+        linear(1, far)
         begun[1] = LineSum(partial[1, far], col, n_col)
-        begun[0].middle()
+        begun[1].begun[:1] = [after(value, summed_far) for value in begun[1].begun[:1]]
         begun[1].middle()
 
         out = jnp.zeros((shard_rows, mixed_width * n_batch), jnp.bfloat16)
         for step, group in ((0, near), (0, far), (1, far), (1, near)):
-            if group == far:
+            if step == 0:
+                summed = summed_far if group == far else summed_first
+            elif group == far:
                 summed = begun[step].end()
-            elif step == 0:
-                summed = summed_first
             else:
                 summed = lax.psum_scatter(
                     partial[step, group], "col", scatter_dimension=0, tiled=True

time: 426 us -> 396 us (0.930)
  waiting for transfers between devices: 249 us -> 217 us
  starting transfers between devices: 35.5 us -> 40.8 us
  Pallas kernels: 87.2 us -> 82.3 us
    ppermute x2 -> x1, waiting for transfers between devices: 31.3 us -> 6.44 us  [end(): lax.ppermute(added(self.part(0), over_3).astype(jnp.bfloat16), 'col', [(1...]
    ppermute x6 -> x3, waiting for transfers between devices: 54.8 us -> 39.9 us  [__init__(): self.begun = [lax.ppermute(self.part(i), 'col', inward) for i in (3, 2, 1)]]
    reduce_scatter x1, waiting for transfers between devices: 0.01 us -> 7.55 us  [on_device(): lax.psum_scatter(partial[0, near], 'col', scatter_dimension=0, tiled=True)]
    ppermute x3, waiting for transfers between devices: 26 us -> 33.3 us  [multiply(): sent = [lax.ppermute(product, ('row', 'col'), pairs) for pairs in turns]]
    ppermute x6 -> x3, starting transfers between devices: 12.8 us -> 18.3 us  [__init__(): self.begun = [lax.ppermute(self.part(i), 'col', inward) for i in (3, 2, 1)]]
  transfers between devices with their start and end apart: 31 -> 26, of which waited for: 13 -> 13; matrix products, arithmetic and copies ran while one was open for 5% -> 6% of each run, Pallas kernels for 18% -> 18%
where the time goes in v9:
time: 396 us; the launch traced here: 395 us
  waiting for transfers between devices  217 us (55%)
  Pallas kernels  82.3 us (21%)
  starting transfers between devices  40.8 us (10%)
  local copies, waits for them, and re-layouts  25.3 us (6%)
  between operations  16.3 us (4%)
  other arithmetic  13.2 us (3%)
    all_gather x2, waiting for transfers between devices, on_device(): lax.all_gather(shard, 'col', axis=0, tiled=True)  75.7 us
    ppermute x4, waiting for transfers between devices, finish(): back = [lax.ppermute(sent, ('row', 'col'), pairs) for pairs in returns]  45.3 us
    pallas_call x4, Pallas kernels, linear_product(): pl.pallas_call(functools.partial(linear_kernel, groups, parts, per_piece)...  41.1 us
    ppermute x3, waiting for transfers between devices, __init__(): self.begun = [lax.ppermute(self.part(i), 'col', inward) for i in (3, 2, 1)]  39.9 us
    ppermute x3, waiting for transfers between devices, multiply(): sent = [lax.ppermute(product, ('row', 'col'), pairs) for pairs in turns]  33.3 us
    pallas_call x4, Pallas kernels, cross_product(): pl.pallas_call(functools.partial(cross_kernel, steps, first), out_shape=j...  30.4 us
    ppermute x3, starting transfers between devices, __init__(): self.begun = [lax.ppermute(self.part(i), 'col', inward) for i in (3, 2, 1)]  18.3 us
    pallas_call x4, Pallas kernels, finish_cross(): pl.pallas_call(finish_kernel, out_shape=jax.ShapeDtypeStruct(own.shape, j...  10.9 us
  transfers between devices with their start and end apart: 26, of which 13 were waited for; matrix products, arithmetic and copies ran while one was open for 6% of the time, Pallas kernels for 18%

profile of v9, /device:TPU:0, one launch (start us, length us, event | category | flops | bytes accessed | tf_op | source)
XLA Modules:
  0.0 395.2 jit_solution(3605708869185968323)
XLA Ops:
  23.1 4.7 %fusion.4 = (bf16[1024,1024]{1,0:T(8,128)(2,1)}, bf16[1024,1024]{1,0:T(8,128)(2,1)}) fusion(bf16[2048,1024]{1,0:T(8,128)(2,1)} %refs_4_.3), kind=kLoop, calls=%fused_computation.33 | loop fusion | bytes 8388608 | tf_op jit(solution)/shard_map/split | solution.py:271
  27.8 65.5 %all-gather.3.cloned.1.call-done.samples = bf16[512,4096]{1,0:T(8,128)(2,1)} async-done(((bf16[128,4096]{1,0:T(8,128)(2,1)}), bf16[512,4096]{1,0:T(8,128)(2,1)}) %all-gather.3.cloned.1.call-update) | async-done | bytes 4194320 | tf_op jit(solution)/shard_map/all_gather | solution.py:281
  95.4 8.8 %shard_map.64.own = bf16[512,1024]{1,0:T(8,128)(2,1)S(1)} custom-call(s32[36]{0:T(128)S(1)} %concatenate.3.meta, bf16[512,4096]{1,0:T(8,128)(2,1)S(1)} %copy-done.1, bf16[4096,512]{1,0:T(8,128)(2,1)} %refs_0_.3, bf16[4096,512]{1,0:T(8,128)(2,1)} %collective-permute-done.refs_1_), custom_call_target="tpu_custom_call" | custom-call | flops 2147483648 | bytes 9437184 | tf_op jit(solution)/shard_map/pallas_call | solution.py:52
  107.8 9.1 %collective-permute-done.2.refs_1_ = bf16[4096,512]{1,0:T(8,128)(2,1)S(1)} collective-permute-done((bf16[4096,512]{1,0:T(8,128)(2,1)}, bf16[4096,512]{1,0:T(8,128)(2,1)S(1)}, u32[]{:S(2)}, u32[]{:S(2)}) %collective-permute-start.2) | collective-permute-done | bytes 4194336 | tf_op jit(solution)/shard_map/ppermute | solution.py:260
  118.9 6.5 %shard_map.65.own = bf16[512,1024]{1,0:T(8,128)(2,1)S(1)} custom-call(s32[36]{0:T(128)S(1)} %concatenate.3.meta, bf16[512,4096]{1,0:T(8,128)(2,1)S(1)} %copy-done.1, bf16[4096,512]{1,0:T(8,128)(2,1)} %collective-permute-done.1.refs_0_, bf16[4096,512]{1,0:T(8,128)(2,1)} %copy-done.7), custom_call_target="tpu_custom_call" | custom-call | flops 2147483648 | bytes 9437184 | tf_op jit(solution)/shard_map/pallas_call | solution.py:52
  126.9 8.3 %collective-permute-done.4.came = bf16[512,1024]{1,0:T(8,128)(2,1)} collective-permute-done((bf16[512,1024]{1,0:T(8,128)(2,1)S(1)}, bf16[512,1024]{1,0:T(8,128)(2,1)}, u32[]{:S(2)}, u32[]{:S(2)}) %collective-permute-start.4) | collective-permute-done | bytes 1048608 | tf_op jit(solution)/shard_map/ppermute | solution.py:337
  140.7 17.0 %collective-permute-done.5.came = bf16[512,1024]{1,0:T(8,128)(2,1)S(1)} collective-permute-done((bf16[512,1024]{1,0:T(8,128)(2,1)S(1)}, bf16[512,1024]{1,0:T(8,128)(2,1)S(1)}, u32[]{:S(2)}, u32[]{:S(2)}) %collective-permute-start.5) | collective-permute-done | bytes 1048608 | tf_op jit(solution)/shard_map/ppermute | solution.py:337
  163.9 10.3 %all-gather.5.cloned.1.call-done.samples = bf16[512,4096]{1,0:T(8,128)(2,1)} async-done(((bf16[128,4096]{1,0:T(8,128)(2,1)}), bf16[512,4096]{1,0:T(8,128)(2,1)}) %all-gather.5.cloned.1.call-update) | async-done | bytes 4194320 | tf_op jit(solution)/shard_map/all_gather | solution.py:281
  176.3 8.7 %shard_map.68.own = bf16[512,1024]{1,0:T(8,128)(2,1)S(1)} custom-call(s32[36]{0:T(128)S(1)} %concatenate.3.meta, bf16[512,4096]{1,0:T(8,128)(2,1)S(1)} %copy-done, bf16[4096,512]{1,0:T(8,128)(2,1)} %refs_0_.3, bf16[4096,512]{1,0:T(8,128)(2,1)} %collective-permute-done.refs_1_), custom_call_target="tpu_custom_call" | custom-call | flops 2147483648 | bytes 9437184 | tf_op jit(solution)/shard_map/pallas_call | solution.py:52
  186.4 6.5 %shard_map.69.own = bf16[512,1024]{1,0:T(8,128)(2,1)S(1)} custom-call(s32[36]{0:T(128)S(1)} %concatenate.3.meta, bf16[512,4096]{1,0:T(8,128)(2,1)S(1)} %copy-done, bf16[4096,512]{1,0:T(8,128)(2,1)} %collective-permute-done.1.refs_0_, bf16[4096,512]{1,0:T(8,128)(2,1)} %copy-done.7), custom_call_target="tpu_custom_call" | custom-call | flops 2147483648 | bytes 9437184 | tf_op jit(solution)/shard_map/pallas_call | solution.py:52
  192.8 10.9 %shard_map.70 = bf16[512,2048]{1,0:T(8,128)(2,1)} custom-call(s32[7]{0:T(128)S(1)} %stack.57.meta, bf16[512,1024]{1,0:T(8,128)(2,1)} %shard_map.66.refs_0_, bf16[512,1024]{1,0:T(8,128)(2,1)} %shard_map.67.refs_1_, bf16[512,1024]{1,0:T(8,128)(2,1)} %collective-permute-done.7.refs_2_, bf16[512,1024]{1,0:T(8,128)(2,1)} %collective-permute-done.8.refs_3_, ...), custom_call_target="tpu_custom_call" | custom-call | flops 4294967296 | bytes 12582912 | tf_op jit(solution)/shard_map/pallas_call | solution.py:143
  203.9 8.0 %collective-permute-done.9.came = bf16[512,1024]{1,0:T(8,128)(2,1)S(1)} collective-permute-done((bf16[512,1024]{1,0:T(8,128)(2,1)S(1)}, bf16[512,1024]{1,0:T(8,128)(2,1)S(1)}, u32[]{:S(2)}, u32[]{:S(2)}) %collective-permute-start.9) | collective-permute-done | bytes 1048608 | tf_op jit(solution)/shard_map/ppermute | solution.py:337
  216.6 24.0 %collective-permute-done.10.came.refs_2_ = bf16[512,1024]{1,0:T(8,128)(2,1)S(1)} collective-permute-done((bf16[512,1024]{1,0:T(8,128)(2,1)S(1)}, bf16[512,1024]{1,0:T(8,128)(2,1)S(1)}, u32[]{:S(2)}, u32[]{:S(2)}) %collective-permute-start.10) | collective-permute-done | bytes 1048608 | tf_op jit(solution)/shard_map/ppermute | solution.py:355
  244.5 7.5 %reduce-scatter.4.cloned.1.call-done = bf16[128,2048]{1,0:T(8,128)(2,1)} async-done(((bf16[512,2048]{1,0:T(8,128)(2,1)}), bf16[128,2048]{1,0:T(8,128)(2,1)}) %reduce-scatter.4.cloned.1.call-update) | async-done | bytes 524304 | tf_op jit(solution)/shard_map/reduce_scatter | solution.py:395
  252.1 10.8 %shard_map.73 = bf16[512,2048]{1,0:T(8,128)(2,1)} custom-call(s32[7]{0:T(128)S(1)} %stack.57.meta, bf16[512,1024]{1,0:T(8,128)(2,1)} %shard_map.66.refs_0_, bf16[512,1024]{1,0:T(8,128)(2,1)} %shard_map.67.refs_1_, bf16[512,1024]{1,0:T(8,128)(2,1)} %collective-permute-done.7.refs_2_, bf16[512,1024]{1,0:T(8,128)(2,1)} %collective-permute-done.8.refs_3_, ...), custom_call_target="tpu_custom_call" | custom-call | flops 4294967296 | bytes 12582912 | tf_op jit(solution)/shard_map/pallas_call | solution.py:143
  264.2 4.4 %collective-permute-start.14 = (bf16[512,1024]{1,0:T(8,128)(2,1)S(1)}, bf16[512,1024]{1,0:T(8,128)(2,1)}, u32[]{:S(2)}, u32[]{:S(2)}) collective-permute-start(bf16[512,1024]{1,0:T(8,128)(2,1)S(1)} %copy-done.3), channel_id=1, source_target_pairs={{0,16},{4,20},{24,8},{28,12},{1,17},{5,21},{25,9},{29,13},{2,18},{... | collective-permute-start | bytes 3145736 | tf_op jit(solution)/shard_map/ppermute | solution.py:355
  268.5 21.2 %collective-permute-done.14.refs_3_ = bf16[512,1024]{1,0:T(8,128)(2,1)} collective-permute-done((bf16[512,1024]{1,0:T(8,128)(2,1)S(1)}, bf16[512,1024]{1,0:T(8,128)(2,1)}, u32[]{:S(2)}, u32[]{:S(2)}) %collective-permute-start.14) | collective-permute-done | bytes 1048608 | tf_op jit(solution)/shard_map/ppermute | solution.py:355
  289.8 9.7 %shard_map.74 = bf16[512,2048]{1,0:T(8,128)(2,1)} custom-call(s32[7]{0:T(128)S(1)} %stack.57.meta, bf16[512,1024]{1,0:T(8,128)(2,1)S(1)} %shard_map.71.refs_0_, bf16[512,1024]{1,0:T(8,128)(2,1)S(1)} %copy-done.3, bf16[512,1024]{1,0:T(8,128)(2,1)S(1)} %collective-permute-done.10.came.refs_2_, bf16[512,1024]{1,0:T(8,128)(2,1)} %collective-permute-done.14.refs_3_, ...), custom_call_target="tpu_custom_call" | custom-call | flops 4294967296 | bytes 12582912 | tf_op jit(solution)/shard_map/pallas_call | solution.py:143
  299.5 9.6 %shard_map.75 = bf16[512,2048]{1,0:T(8,128)(2,1)} custom-call(s32[7]{0:T(128)S(1)} %stack.57.meta, bf16[512,1024]{1,0:T(8,128)(2,1)S(1)} %shard_map.71.refs_0_, bf16[512,1024]{1,0:T(8,128)(2,1)S(1)} %copy-done.3, bf16[512,1024]{1,0:T(8,128)(2,1)S(1)} %collective-permute-done.10.came.refs_2_, bf16[512,1024]{1,0:T(8,128)(2,1)} %collective-permute-done.14.refs_3_, ...), custom_call_target="tpu_custom_call" | custom-call | flops 4294967296 | bytes 12582912 | tf_op jit(solution)/shard_map/pallas_call | solution.py:143
  315.7 20.5 %collective-permute-done.15 = bf16[128,2048]{1,0:T(8,128)(2,1)} collective-permute-done((bf16[128,2048]{1,0:T(8,128)(2,1)S(1)}, bf16[128,2048]{1,0:T(8,128)(2,1)}, u32[]{:S(2)}, u32[]{:S(2)}) %collective-permute-start.15) | collective-permute-done | bytes 524320 | tf_op jit(solution)/shard_map/ppermute | solution.py:214
  338.9 14.0 %collective-permute-start.18 = (bf16[128,2048]{1,0:T(8,128)(2,1)}, bf16[128,2048]{1,0:T(8,128)(2,1)S(1)}, u32[]{:S(2)}, u32[]{:S(2)}) collective-permute-start(bf16[128,2048]{1,0:T(8,128)(2,1)} %get-tuple-element.49), channel_id=1, source_target_pairs={{0,4},{12,8},{1,5},{13,9},{2,6},{14,10},{3,7},{15,11},{16,20},{28,... | collective-permute-start | bytes 1572872 | tf_op jit(solution)/shard_map/ppermute | solution.py:214
  352.9 5.6 %collective-permute-done.19 = bf16[128,2048]{1,0:T(8,128)(2,1)} collective-permute-done((bf16[128,2048]{1,0:T(8,128)(2,1)S(1)}, bf16[128,2048]{1,0:T(8,128)(2,1)}, u32[]{:S(2)}, u32[]{:S(2)}) %collective-permute-start.19) | collective-permute-done | bytes 524320 | tf_op jit(solution)/shard_map/ppermute | solution.py:214
  365.3 13.8 %collective-permute-done.18 = bf16[128,2048]{1,0:T(8,128)(2,1)S(1)} collective-permute-done((bf16[128,2048]{1,0:T(8,128)(2,1)}, bf16[128,2048]{1,0:T(8,128)(2,1)S(1)}, u32[]{:S(2)}, u32[]{:S(2)}) %collective-permute-start.18) | collective-permute-done | bytes 524320 | tf_op jit(solution)/shard_map/ppermute | solution.py:214
  379.2 6.4 %collective-permute-done.17 = bf16[128,2048]{1,0:T(8,128)(2,1)S(1)} collective-permute-done((bf16[128,2048]{1,0:T(8,128)(2,1)S(1)}, bf16[128,2048]{1,0:T(8,128)(2,1)S(1)}, u32[]{:S(2)}, u32[]{:S(2)}) %collective-permute-start.17) | collective-permute-done | bytes 524320 | tf_op jit(solution)/shard_map/ppermute | solution.py:238
  (105 shorter events, 67.2 us)
Async XLA Ops:
  6.5 86.7 %all-gather.3.cloned.1.call-start = ((), (), s32[]{:S(2)}) async-start(), calls=%async_computation.3 | async-start | bytes 5242880 | tf_op jit(solution)/shard_map/all_gather | solution.py:281
  9.6 164.5 %all-gather.5.cloned.1.call-start = ((), (), s32[]{:S(2)}) async-start(), calls=%async_computation.4 | async-start | bytes 5242880 | tf_op jit(solution)/shard_map/all_gather | solution.py:281
  9.7 18.1 %collective-permute-start = (bf16[4096,512]{1,0:T(8,128)(2,1)}, bf16[4096,512]{1,0:T(8,128)(2,1)}, u32[]{:S(2)}, u32[]{:S(2)}) collective-permute-start(bf16[4096,512]{1,0:T(8,128)(2,1)} %refs_0_.3), channel_id=1, source_target_pairs={{0,1},{1,0},{2,3},{3,2},{4,5},{5,4},{6,7},{7,6},{8,9},{9,8},{10,11... | collective-permute-start | bytes 12582920 | tf_op jit(solution)/shard_map/ppermute | solution.py:260
  10.2 94.0 %collective-permute-start.1 = (bf16[4096,512]{1,0:T(8,128)(2,1)}, bf16[4096,512]{1,0:T(8,128)(2,1)}, u32[]{:S(2)}, u32[]{:S(2)}) collective-permute-start(bf16[4096,512]{1,0:T(8,128)(2,1)} %refs_0_.3), channel_id=1, source_target_pairs={{0,2},{1,3},{2,0},{3,1},{4,6},{5,7},{6,4},{7,5},{8,10},{9,11},{10,... | collective-permute-start | bytes 12582920 | tf_op jit(solution)/shard_map/ppermute | solution.py:260
  12.8 239.3 %reduce-scatter.4.cloned.1.call-start = ((), (), s32[]{:S(2)}) async-start(), calls=%async_computation.5 | async-start | bytes 2621440 | tf_op jit(solution)/shard_map/reduce_scatter | solution.py:395
  104.3 12.6 %collective-permute-start.2 = (bf16[4096,512]{1,0:T(8,128)(2,1)}, bf16[4096,512]{1,0:T(8,128)(2,1)S(1)}, u32[]{:S(2)}, u32[]{:S(2)}) collective-permute-start(bf16[4096,512]{1,0:T(8,128)(2,1)} %collective-permute-done.1.refs_0_), channel_id=1, source_target_pairs={{0,1},{1,0},{2,3},{3,2},{4,5},{5,4},{6,7},{7,6},{8,9},{9,8},{10,11... | collective-permute-start | bytes 12582920 | tf_op jit(solution)/shard_map/ppermute | solution.py:260
  104.3 22.5 %collective-permute-start.3 = (bf16[2048,1024]{1,0:T(8,128)(2,1)}, bf16[2048,1024]{1,0:T(8,128)(2,1)}, u32[]{:S(2)}, u32[]{:S(2)}) collective-permute-start(bf16[2048,1024]{1,0:T(8,128)(2,1)} %refs_4_.3), channel_id=1, source_target_pairs={{0,1},{1,0},{2,3},{3,2},{4,5},{5,4},{6,7},{7,6},{8,9},{9,8},{10,11... | collective-permute-start | bytes 12582920 | tf_op jit(solution)/shard_map/ppermute | solution.py:260
  104.8 59.1 %collective-permute-start.6 = (bf16[1024,1024]{1,0:T(8,128)(2,1)}, bf16[1024,1024]{1,0:T(8,128)(2,1)}, u32[]{:S(2)}, u32[]{:S(2)}) collective-permute-start(bf16[1024,1024]{1,0:T(8,128)(2,1)} %get-tuple-element.46), channel_id=1, source_target_pairs={{0,2},{1,3},{2,0},{3,1},{4,6},{5,7},{6,4},{7,5},{8,10},{9,11},{10,... | collective-permute-start | bytes 6291464 | tf_op jit(solution)/shard_map/ppermute | solution.py:260
  106.5 28.7 %collective-permute-start.4 = (bf16[512,1024]{1,0:T(8,128)(2,1)S(1)}, bf16[512,1024]{1,0:T(8,128)(2,1)}, u32[]{:S(2)}, u32[]{:S(2)}) collective-permute-start(bf16[512,1024]{1,0:T(8,128)(2,1)S(1)} %shard_map.64.own), channel_id=1, source_target_pairs={{16,0},{20,4},{8,24},{12,28},{17,1},{21,5},{9,25},{13,29},{18,2},{... | collective-permute-start | bytes 3145736 | tf_op jit(solution)/shard_map/ppermute | solution.py:337
  125.4 32.4 %collective-permute-start.5 = (bf16[512,1024]{1,0:T(8,128)(2,1)S(1)}, bf16[512,1024]{1,0:T(8,128)(2,1)S(1)}, u32[]{:S(2)}, u32[]{:S(2)}) collective-permute-start(bf16[512,1024]{1,0:T(8,128)(2,1)S(1)} %shard_map.65.own), channel_id=1, source_target_pairs={{16,0},{20,4},{8,24},{12,28},{17,1},{21,5},{9,25},{13,29},{18,2},{... | collective-permute-start | bytes 3145736 | tf_op jit(solution)/shard_map/ppermute | solution.py:337
  138.4 54.4 %collective-permute-start.7 = (bf16[512,1024]{1,0:T(8,128)(2,1)}, bf16[512,1024]{1,0:T(8,128)(2,1)}, u32[]{:S(2)}, u32[]{:S(2)}) collective-permute-start(bf16[512,1024]{1,0:T(8,128)(2,1)} %shard_map.66.refs_0_), channel_id=1, source_target_pairs={{0,16},{4,20},{24,8},{28,12},{1,17},{5,21},{25,9},{29,13},{2,18},{... | collective-permute-start | bytes 3145736 | tf_op jit(solution)/shard_map/ppermute | solution.py:355
  160.8 32.1 %collective-permute-start.8 = (bf16[512,1024]{1,0:T(8,128)(2,1)}, bf16[512,1024]{1,0:T(8,128)(2,1)}, u32[]{:S(2)}, u32[]{:S(2)}) collective-permute-start(bf16[512,1024]{1,0:T(8,128)(2,1)} %shard_map.67.refs_1_), channel_id=1, source_target_pairs={{0,16},{4,20},{24,8},{28,12},{1,17},{5,21},{25,9},{29,13},{2,18},{... | collective-permute-start | bytes 3145736 | tf_op jit(solution)/shard_map/ppermute | solution.py:355
  163.2 80.8 %collective-permute-start.11 = (bf16[1024,1024]{1,0:T(8,128)(2,1)}, bf16[1024,1024]{1,0:T(8,128)(2,1)}, u32[]{:S(2)}, u32[]{:S(2)}) collective-permute-start(bf16[1024,1024]{1,0:T(8,128)(2,1)} %get-tuple-element.45), channel_id=1, source_target_pairs={{0,2},{1,3},{2,0},{3,1},{4,6},{5,7},{6,4},{7,5},{8,10},{9,11},{10,... | collective-permute-start | bytes 6291464 | tf_op jit(solution)/shard_map/ppermute | solution.py:260
  185.1 26.7 %collective-permute-start.9 = (bf16[512,1024]{1,0:T(8,128)(2,1)S(1)}, bf16[512,1024]{1,0:T(8,128)(2,1)S(1)}, u32[]{:S(2)}, u32[]{:S(2)}) collective-permute-start(bf16[512,1024]{1,0:T(8,128)(2,1)S(1)} %shard_map.68.own), channel_id=1, source_target_pairs={{16,0},{20,4},{8,24},{12,28},{17,1},{21,5},{9,25},{13,29},{18,2},{... | collective-permute-start | bytes 3145736 | tf_op jit(solution)/shard_map/ppermute | solution.py:337
  203.8 132.4 %reduce-scatter.6.cloned.1.call-start = ((), (), s32[]{:S(2)}) async-start(), calls=%async_computation.6 | async-start | bytes 2621440 | tf_op jit(solution)/shard_map/reduce_scatter | solution.py:403
  216.5 24.1 %collective-permute-start.10 = (bf16[512,1024]{1,0:T(8,128)(2,1)S(1)}, bf16[512,1024]{1,0:T(8,128)(2,1)S(1)}, u32[]{:S(2)}, u32[]{:S(2)}) collective-permute-start(bf16[512,1024]{1,0:T(8,128)(2,1)S(1)} %broadcast_select_fusion), channel_id=1, source_target_pairs={{0,16},{4,20},{24,8},{28,12},{16,0},{20,4},{8,24},{12,28},{1,17},{... | collective-permute-start | bytes 3145736 | tf_op jit(solution)/shard_map/ppermute | solution.py:355
  263.0 123.8 %reduce-scatter.8.cloned.1.call-start = ((), (), s32[]{:S(2)}) async-start(), calls=%async_computation.7 | async-start | bytes 2621440 | tf_op jit(solution)/shard_map/reduce_scatter | solution.py:417
  264.2 25.6 %collective-permute-start.14 = (bf16[512,1024]{1,0:T(8,128)(2,1)S(1)}, bf16[512,1024]{1,0:T(8,128)(2,1)}, u32[]{:S(2)}, u32[]{:S(2)}) collective-permute-start(bf16[512,1024]{1,0:T(8,128)(2,1)S(1)} %copy-done.3), channel_id=1, source_target_pairs={{0,16},{4,20},{24,8},{28,12},{1,17},{5,21},{25,9},{29,13},{2,18},{... | collective-permute-start | bytes 3145736 | tf_op jit(solution)/shard_map/ppermute | solution.py:355
  311.4 24.8 %collective-permute-start.15 = (bf16[128,2048]{1,0:T(8,128)(2,1)S(1)}, bf16[128,2048]{1,0:T(8,128)(2,1)}, u32[]{:S(2)}, u32[]{:S(2)}) collective-permute-start(bf16[128,2048]{1,0:T(8,128)(2,1)S(1)} %get-tuple-element.47), channel_id=1, source_target_pairs={{0,4},{12,8},{1,5},{13,9},{2,6},{14,10},{3,7},{15,11},{16,20},{28,... | collective-permute-start | bytes 1572872 | tf_op jit(solution)/shard_map/ppermute | solution.py:214
  313.7 44.8 %collective-permute-start.19 = (bf16[128,2048]{1,0:T(8,128)(2,1)S(1)}, bf16[128,2048]{1,0:T(8,128)(2,1)}, u32[]{:S(2)}, u32[]{:S(2)}) collective-permute-start(bf16[128,2048]{1,0:T(8,128)(2,1)S(1)} %get-tuple-element.48), channel_id=1, source_target_pairs={{0,4},{12,8},{1,5},{13,9},{2,6},{14,10},{3,7},{15,11},{16,20},{28,... | collective-permute-start | bytes 1572872 | tf_op jit(solution)/shard_map/ppermute | solution.py:214
  338.2 22.4 %collective-permute-start.16 = (bf16[128,2048]{1,0:T(8,128)(2,1)}, bf16[128,2048]{1,0:T(8,128)(2,1)S(1)}, u32[]{:S(2)}, u32[]{:S(2)}) collective-permute-start(bf16[128,2048]{1,0:T(8,128)(2,1)} %add_convert_fusion.4), channel_id=1, source_target_pairs={{4,8},{8,4},{5,9},{9,5},{6,10},{10,6},{7,11},{11,7},{20,24},{24,20... | collective-permute-start | bytes 1572872 | tf_op jit(solution)/shard_map/ppermute | solution.py:225
  338.9 40.3 %collective-permute-start.18 = (bf16[128,2048]{1,0:T(8,128)(2,1)}, bf16[128,2048]{1,0:T(8,128)(2,1)S(1)}, u32[]{:S(2)}, u32[]{:S(2)}) collective-permute-start(bf16[128,2048]{1,0:T(8,128)(2,1)} %get-tuple-element.49), channel_id=1, source_target_pairs={{0,4},{12,8},{1,5},{13,9},{2,6},{14,10},{3,7},{15,11},{16,20},{28,... | collective-permute-start | bytes 1572872 | tf_op jit(solution)/shard_map/ppermute | solution.py:214
  359.7 19.5 %collective-permute-start.20 = (bf16[128,2048]{1,0:T(8,128)(2,1)S(1)}, bf16[128,2048]{1,0:T(8,128)(2,1)S(1)}, u32[]{:S(2)}, u32[]{:S(2)}) collective-permute-start(bf16[128,2048]{1,0:T(8,128)(2,1)S(1)} %add_convert_fusion.2), channel_id=1, source_target_pairs={{4,8},{8,4},{5,9},{9,5},{6,10},{10,6},{7,11},{11,7},{20,24},{24,20... | collective-permute-start | bytes 1572872 | tf_op jit(solution)/shard_map/ppermute | solution.py:225
  360.7 24.9 %collective-permute-start.17 = (bf16[128,2048]{1,0:T(8,128)(2,1)S(1)}, bf16[128,2048]{1,0:T(8,128)(2,1)S(1)}, u32[]{:S(2)}, u32[]{:S(2)}) collective-permute-start(bf16[128,2048]{1,0:T(8,128)(2,1)S(1)} %add_convert_fusion.3), channel_id=1, source_target_pairs={{4,0},{8,12},{5,1},{9,13},{6,2},{10,14},{7,3},{11,15},{20,16},{24,... | collective-permute-start | bytes 1572872 | tf_op jit(solution)/shard_map/ppermute | solution.py:238
  (14 other events, 145.5 us)
Sparse Core Ops, SparseCore 0:
  9.8 83.4 all-gather.2
  94.8 79.2 all-gather.4
  203.9 48.0 reduce-scatter.3
  263.1 43.8 reduce-scatter.5
  309.1 71.4 reduce-scatter.7

commit v10 on v9

--- a/solution.py
+++ b/solution.py
@@ -401,10 +401,10 @@
         spread_far_linear(linear_across)
         linear(0, far, summed_first)
         summed_far = lax.psum_scatter(partial[0, far], "col", scatter_dimension=0, tiled=True)
-        linear(1, near)
         linear(1, far)
         begun[1] = LineSum(partial[1, far], col, n_col)
-        begun[1].begun[:1] = [after(value, summed_far) for value in begun[1].begun[:1]]
+        linear(1, near)
+        begun[1].begun[:1] = [after(value, summed_far, partial[1, near]) for value in begun[1].begun[:1]]
         begun[1].middle()
 
         out = jnp.zeros((shard_rows, mixed_width * n_batch), jnp.bfloat16)

time: 396 us -> 393 us (level)
  waiting for transfers between devices: 217 us -> 209 us
  Pallas kernels: 82.3 us -> 89.9 us
    ppermute x3, waiting for transfers between devices: 33.3 us -> 25.2 us  [multiply(): sent = [lax.ppermute(product, ('row', 'col'), pairs) for pairs in turns]]
    pallas_call x4, Pallas kernels: 30.4 us -> 37.9 us  [cross_product(): pl.pallas_call(functools.partial(cross_kernel, steps, first), out_shape=j...]
    ppermute x1, waiting for transfers between devices: 6.44 us -> 1.47 us  [end(): lax.ppermute(added(self.part(0), over_3).astype(jnp.bfloat16), 'col', [(1...]
  transfers between devices with their start and end apart: 26 -> 26, of which waited for: 13 -> 15; matrix products, arithmetic and copies ran while one was open for 6% -> 5% of each run, Pallas kernels for 18% -> 20%
where the time goes in v10:
time: 393 us; the launch traced here: 391 us
  waiting for transfers between devices  209 us (53%)
  Pallas kernels  89.9 us (23%)
  starting transfers between devices  37.4 us (10%)
  local copies, waits for them, and re-layouts  25.5 us (6%)
  between operations  16.3 us (4%)
  other arithmetic  13.2 us (3%)
    all_gather x2, waiting for transfers between devices, on_device(): lax.all_gather(shard, 'col', axis=0, tiled=True)  76.2 us
    ppermute x4, waiting for transfers between devices, finish(): back = [lax.ppermute(sent, ('row', 'col'), pairs) for pairs in returns]  46.4 us
    ppermute x3, waiting for transfers between devices, __init__(): self.begun = [lax.ppermute(self.part(i), 'col', inward) for i in (3, 2, 1)]  41.2 us
    pallas_call x4, Pallas kernels, linear_product(): pl.pallas_call(functools.partial(linear_kernel, groups, parts, per_piece)...  41.1 us
    pallas_call x4, Pallas kernels, cross_product(): pl.pallas_call(functools.partial(cross_kernel, steps, first), out_shape=j...  37.9 us
    ppermute x3, waiting for transfers between devices, multiply(): sent = [lax.ppermute(product, ('row', 'col'), pairs) for pairs in turns]  25.2 us
    ppermute x3, starting transfers between devices, __init__(): self.begun = [lax.ppermute(self.part(i), 'col', inward) for i in (3, 2, 1)]  15.5 us
    unnamed x24, local copies, waits for them, and re-layouts  12.5 us
  transfers between devices with their start and end apart: 26, of which 15 were waited for; matrix products, arithmetic and copies ran while one was open for 5% of the time, Pallas kernels for 20%

profile of v10, /device:TPU:0, one launch (start us, length us, event | category | flops | bytes accessed | tf_op | source)
XLA Modules:
  0.0 391.3 jit_solution(17450218200165196113)
XLA Ops:
  23.1 4.7 %fusion.4 = (bf16[1024,1024]{1,0:T(8,128)(2,1)}, bf16[1024,1024]{1,0:T(8,128)(2,1)}) fusion(bf16[2048,1024]{1,0:T(8,128)(2,1)} %refs_4_.3), kind=kLoop, calls=%fused_computation.33 | loop fusion | bytes 8388608 | tf_op jit(solution)/shard_map/split | solution.py:271
  27.8 65.5 %all-gather.3.cloned.1.call-done.samples = bf16[512,4096]{1,0:T(8,128)(2,1)} async-done(((bf16[128,4096]{1,0:T(8,128)(2,1)}), bf16[512,4096]{1,0:T(8,128)(2,1)}) %all-gather.3.cloned.1.call-update) | async-done | bytes 4194320 | tf_op jit(solution)/shard_map/all_gather | solution.py:281
  95.5 8.8 %shard_map.64.own = bf16[512,1024]{1,0:T(8,128)(2,1)S(1)} custom-call(s32[36]{0:T(128)S(1)} %concatenate.3.meta, bf16[512,4096]{1,0:T(8,128)(2,1)S(1)} %copy-done.1, bf16[4096,512]{1,0:T(8,128)(2,1)} %refs_0_.3, bf16[4096,512]{1,0:T(8,128)(2,1)} %collective-permute-done.refs_1_), custom_call_target="tpu_custom_call" | custom-call | flops 2147483648 | bytes 9437184 | tf_op jit(solution)/shard_map/pallas_call | solution.py:52
  109.2 7.8 %collective-permute-done.2.refs_1_ = bf16[4096,512]{1,0:T(8,128)(2,1)S(1)} collective-permute-done((bf16[4096,512]{1,0:T(8,128)(2,1)}, bf16[4096,512]{1,0:T(8,128)(2,1)S(1)}, u32[]{:S(2)}, u32[]{:S(2)}) %collective-permute-start.2) | collective-permute-done | bytes 4194336 | tf_op jit(solution)/shard_map/ppermute | solution.py:260
  119.1 10.2 %shard_map.65.own = bf16[512,1024]{1,0:T(8,128)(2,1)S(1)} custom-call(s32[36]{0:T(128)S(1)} %concatenate.3.meta, bf16[512,4096]{1,0:T(8,128)(2,1)S(1)} %copy-done.1, bf16[4096,512]{1,0:T(8,128)(2,1)} %collective-permute-done.1.refs_0_, bf16[4096,512]{1,0:T(8,128)(2,1)} %copy-done.7), custom_call_target="tpu_custom_call" | custom-call | flops 2147483648 | bytes 9437184 | tf_op jit(solution)/shard_map/pallas_call | solution.py:52
  130.8 3.9 collective-permute-done.4.came
  134.7 3.2 shard_map.66.refs_0_
  140.3 17.1 %collective-permute-done.5.came = bf16[512,1024]{1,0:T(8,128)(2,1)S(1)} collective-permute-done((bf16[512,1024]{1,0:T(8,128)(2,1)S(1)}, bf16[512,1024]{1,0:T(8,128)(2,1)S(1)}, u32[]{:S(2)}, u32[]{:S(2)}) %collective-permute-start.5) | collective-permute-done | bytes 1048608 | tf_op jit(solution)/shard_map/ppermute | solution.py:337
  163.5 10.7 %all-gather.5.cloned.1.call-done.samples = bf16[512,4096]{1,0:T(8,128)(2,1)} async-done(((bf16[128,4096]{1,0:T(8,128)(2,1)}), bf16[512,4096]{1,0:T(8,128)(2,1)}) %all-gather.5.cloned.1.call-update) | async-done | bytes 4194320 | tf_op jit(solution)/shard_map/all_gather | solution.py:281
  176.4 8.7 %shard_map.68.own = bf16[512,1024]{1,0:T(8,128)(2,1)S(1)} custom-call(s32[36]{0:T(128)S(1)} %concatenate.3.meta, bf16[512,4096]{1,0:T(8,128)(2,1)S(1)} %copy-done, bf16[4096,512]{1,0:T(8,128)(2,1)} %refs_0_.3, bf16[4096,512]{1,0:T(8,128)(2,1)} %collective-permute-done.refs_1_), custom_call_target="tpu_custom_call" | custom-call | flops 2147483648 | bytes 9437184 | tf_op jit(solution)/shard_map/pallas_call | solution.py:52
  186.4 10.2 %shard_map.69.own = bf16[512,1024]{1,0:T(8,128)(2,1)S(1)} custom-call(s32[36]{0:T(128)S(1)} %concatenate.3.meta, bf16[512,4096]{1,0:T(8,128)(2,1)S(1)} %copy-done, bf16[4096,512]{1,0:T(8,128)(2,1)} %collective-permute-done.1.refs_0_, bf16[4096,512]{1,0:T(8,128)(2,1)} %copy-done.7), custom_call_target="tpu_custom_call" | custom-call | flops 2147483648 | bytes 9437184 | tf_op jit(solution)/shard_map/pallas_call | solution.py:52
  196.6 10.9 %shard_map.70 = bf16[512,2048]{1,0:T(8,128)(2,1)} custom-call(s32[7]{0:T(128)S(1)} %stack.57.meta, bf16[512,1024]{1,0:T(8,128)(2,1)} %shard_map.66.refs_0_, bf16[512,1024]{1,0:T(8,128)(2,1)} %shard_map.67.refs_1_, bf16[512,1024]{1,0:T(8,128)(2,1)} %collective-permute-done.7.refs_2_, bf16[512,1024]{1,0:T(8,128)(2,1)} %collective-permute-done.8.refs_3_, ...), custom_call_target="tpu_custom_call" | custom-call | flops 4294967296 | bytes 12582912 | tf_op jit(solution)/shard_map/pallas_call | solution.py:143
  207.7 4.3 %collective-permute-done.9.came = bf16[512,1024]{1,0:T(8,128)(2,1)S(1)} collective-permute-done((bf16[512,1024]{1,0:T(8,128)(2,1)S(1)}, bf16[512,1024]{1,0:T(8,128)(2,1)S(1)}, u32[]{:S(2)}, u32[]{:S(2)}) %collective-permute-start.9) | collective-permute-done | bytes 1048608 | tf_op jit(solution)/shard_map/ppermute | solution.py:337
  216.7 24.1 %collective-permute-done.10.came.refs_2_ = bf16[512,1024]{1,0:T(8,128)(2,1)S(1)} collective-permute-done((bf16[512,1024]{1,0:T(8,128)(2,1)S(1)}, bf16[512,1024]{1,0:T(8,128)(2,1)S(1)}, u32[]{:S(2)}, u32[]{:S(2)}) %collective-permute-start.10) | collective-permute-done | bytes 1048608 | tf_op jit(solution)/shard_map/ppermute | solution.py:355
  244.7 6.0 %reduce-scatter.4.cloned.1.call-done = bf16[128,2048]{1,0:T(8,128)(2,1)} async-done(((bf16[512,2048]{1,0:T(8,128)(2,1)}), bf16[128,2048]{1,0:T(8,128)(2,1)}) %reduce-scatter.4.cloned.1.call-update) | async-done | bytes 524304 | tf_op jit(solution)/shard_map/reduce_scatter | solution.py:395
  251.6 10.8 %shard_map.73 = bf16[512,2048]{1,0:T(8,128)(2,1)} custom-call(s32[7]{0:T(128)S(1)} %stack.57.meta, bf16[512,1024]{1,0:T(8,128)(2,1)} %shard_map.66.refs_0_, bf16[512,1024]{1,0:T(8,128)(2,1)} %shard_map.67.refs_1_, bf16[512,1024]{1,0:T(8,128)(2,1)} %collective-permute-done.7.refs_2_, bf16[512,1024]{1,0:T(8,128)(2,1)} %collective-permute-done.8.refs_3_, ...), custom_call_target="tpu_custom_call" | custom-call | flops 4294967296 | bytes 12582912 | tf_op jit(solution)/shard_map/pallas_call | solution.py:143
  266.3 22.3 %collective-permute-done.14.refs_3_ = bf16[512,1024]{1,0:T(8,128)(2,1)S(1)} collective-permute-done((bf16[512,1024]{1,0:T(8,128)(2,1)S(1)}, bf16[512,1024]{1,0:T(8,128)(2,1)S(1)}, u32[]{:S(2)}, u32[]{:S(2)}) %collective-permute-start.14) | collective-permute-done | bytes 1048608 | tf_op jit(solution)/shard_map/ppermute | solution.py:355
  288.6 9.6 %shard_map.74 = bf16[512,2048]{1,0:T(8,128)(2,1)} custom-call(s32[7]{0:T(128)S(1)} %stack.57.meta, bf16[512,1024]{1,0:T(8,128)(2,1)S(1)} %shard_map.71.refs_0_, bf16[512,1024]{1,0:T(8,128)(2,1)S(1)} %copy-done.3, bf16[512,1024]{1,0:T(8,128)(2,1)S(1)} %collective-permute-done.10.came.refs_2_, bf16[512,1024]{1,0:T(8,128)(2,1)S(1)} %collective-permute-done.14.refs_3_, ...), custom_call_target="tpu_custom_call" | custom-call | flops 4294967296 | bytes 12582912 | tf_op jit(solution)/shard_map/pallas_call | solution.py:143
  298.2 9.7 %shard_map.75 = bf16[512,2048]{1,0:T(8,128)(2,1)} custom-call(s32[7]{0:T(128)S(1)} %stack.57.meta, bf16[512,1024]{1,0:T(8,128)(2,1)S(1)} %shard_map.71.refs_0_, bf16[512,1024]{1,0:T(8,128)(2,1)S(1)} %copy-done.3, bf16[512,1024]{1,0:T(8,128)(2,1)S(1)} %collective-permute-done.10.came.refs_2_, bf16[512,1024]{1,0:T(8,128)(2,1)S(1)} %collective-permute-done.14.refs_3_, ...), custom_call_target="tpu_custom_call" | custom-call | flops 4294967296 | bytes 12582912 | tf_op jit(solution)/shard_map/pallas_call | solution.py:143
  314.7 18.7 %collective-permute-done.15 = bf16[128,2048]{1,0:T(8,128)(2,1)} collective-permute-done((bf16[128,2048]{1,0:T(8,128)(2,1)S(1)}, bf16[128,2048]{1,0:T(8,128)(2,1)}, u32[]{:S(2)}, u32[]{:S(2)}) %collective-permute-start.15) | collective-permute-done | bytes 524320 | tf_op jit(solution)/shard_map/ppermute | solution.py:214
  336.1 11.2 %collective-permute-start.18 = (bf16[128,2048]{1,0:T(8,128)(2,1)}, bf16[128,2048]{1,0:T(8,128)(2,1)S(1)}, u32[]{:S(2)}, u32[]{:S(2)}) collective-permute-start(bf16[128,2048]{1,0:T(8,128)(2,1)} %get-tuple-element.49), channel_id=1, source_target_pairs={{0,4},{12,8},{1,5},{13,9},{2,6},{14,10},{3,7},{15,11},{16,20},{28,... | collective-permute-start | bytes 1572872 | tf_op jit(solution)/shard_map/ppermute | solution.py:214
  347.4 8.5 %collective-permute-done.19 = bf16[128,2048]{1,0:T(8,128)(2,1)} collective-permute-done((bf16[128,2048]{1,0:T(8,128)(2,1)S(1)}, bf16[128,2048]{1,0:T(8,128)(2,1)}, u32[]{:S(2)}, u32[]{:S(2)}) %collective-permute-start.19) | collective-permute-done | bytes 524320 | tf_op jit(solution)/shard_map/ppermute | solution.py:214
  362.7 13.9 %collective-permute-done.18 = bf16[128,2048]{1,0:T(8,128)(2,1)S(1)} collective-permute-done((bf16[128,2048]{1,0:T(8,128)(2,1)}, bf16[128,2048]{1,0:T(8,128)(2,1)S(1)}, u32[]{:S(2)}, u32[]{:S(2)}) %collective-permute-start.18) | collective-permute-done | bytes 524320 | tf_op jit(solution)/shard_map/ppermute | solution.py:214
  379.3 3.6 reduce-scatter.8.cloned.1.call-done
  (105 shorter events, 70.5 us)
Async XLA Ops:
  6.5 86.8 %all-gather.3.cloned.1.call-start = ((), (), s32[]{:S(2)}) async-start(), calls=%async_computation.3 | async-start | bytes 5242880 | tf_op jit(solution)/shard_map/all_gather | solution.py:281
  9.7 164.5 %all-gather.5.cloned.1.call-start = ((), (), s32[]{:S(2)}) async-start(), calls=%async_computation.4 | async-start | bytes 5242880 | tf_op jit(solution)/shard_map/all_gather | solution.py:281
  9.7 18.0 %collective-permute-start = (bf16[4096,512]{1,0:T(8,128)(2,1)}, bf16[4096,512]{1,0:T(8,128)(2,1)}, u32[]{:S(2)}, u32[]{:S(2)}) collective-permute-start(bf16[4096,512]{1,0:T(8,128)(2,1)} %refs_0_.3), channel_id=1, source_target_pairs={{0,1},{1,0},{2,3},{3,2},{4,5},{5,4},{6,7},{7,6},{8,9},{9,8},{10,11... | collective-permute-start | bytes 12582920 | tf_op jit(solution)/shard_map/ppermute | solution.py:260
  10.3 94.1 %collective-permute-start.1 = (bf16[4096,512]{1,0:T(8,128)(2,1)}, bf16[4096,512]{1,0:T(8,128)(2,1)}, u32[]{:S(2)}, u32[]{:S(2)}) collective-permute-start(bf16[4096,512]{1,0:T(8,128)(2,1)} %refs_0_.3), channel_id=1, source_target_pairs={{0,2},{1,3},{2,0},{3,1},{4,6},{5,7},{6,4},{7,5},{8,10},{9,11},{10,... | collective-permute-start | bytes 12582920 | tf_op jit(solution)/shard_map/ppermute | solution.py:260
  12.9 237.8 %reduce-scatter.4.cloned.1.call-start = ((), (), s32[]{:S(2)}) async-start(), calls=%async_computation.5 | async-start | bytes 2621440 | tf_op jit(solution)/shard_map/reduce_scatter | solution.py:395
  104.3 12.6 %collective-permute-start.2 = (bf16[4096,512]{1,0:T(8,128)(2,1)}, bf16[4096,512]{1,0:T(8,128)(2,1)S(1)}, u32[]{:S(2)}, u32[]{:S(2)}) collective-permute-start(bf16[4096,512]{1,0:T(8,128)(2,1)} %collective-permute-done.1.refs_0_), channel_id=1, source_target_pairs={{0,1},{1,0},{2,3},{3,2},{4,5},{5,4},{6,7},{7,6},{8,9},{9,8},{10,11... | collective-permute-start | bytes 12582920 | tf_op jit(solution)/shard_map/ppermute | solution.py:260
  104.4 26.4 %collective-permute-start.3 = (bf16[2048,1024]{1,0:T(8,128)(2,1)}, bf16[2048,1024]{1,0:T(8,128)(2,1)}, u32[]{:S(2)}, u32[]{:S(2)}) collective-permute-start(bf16[2048,1024]{1,0:T(8,128)(2,1)} %refs_4_.3), channel_id=1, source_target_pairs={{0,1},{1,0},{2,3},{3,2},{4,5},{5,4},{6,7},{7,6},{8,9},{9,8},{10,11... | collective-permute-start | bytes 12582920 | tf_op jit(solution)/shard_map/ppermute | solution.py:260
  104.9 58.6 %collective-permute-start.6 = (bf16[1024,1024]{1,0:T(8,128)(2,1)}, bf16[1024,1024]{1,0:T(8,128)(2,1)}, u32[]{:S(2)}, u32[]{:S(2)}) collective-permute-start(bf16[1024,1024]{1,0:T(8,128)(2,1)} %get-tuple-element.46), channel_id=1, source_target_pairs={{0,2},{1,3},{2,0},{3,1},{4,6},{5,7},{6,4},{7,5},{8,10},{9,11},{10,... | collective-permute-start | bytes 6291464 | tf_op jit(solution)/shard_map/ppermute | solution.py:260
  107.9 26.9 %collective-permute-start.4 = (bf16[512,1024]{1,0:T(8,128)(2,1)S(1)}, bf16[512,1024]{1,0:T(8,128)(2,1)}, u32[]{:S(2)}, u32[]{:S(2)}) collective-permute-start(bf16[512,1024]{1,0:T(8,128)(2,1)S(1)} %shard_map.64.own), channel_id=1, source_target_pairs={{16,0},{20,4},{8,24},{12,28},{17,1},{21,5},{9,25},{13,29},{18,2},{... | collective-permute-start | bytes 3145736 | tf_op jit(solution)/shard_map/ppermute | solution.py:337
  129.3 28.0 %collective-permute-start.5 = (bf16[512,1024]{1,0:T(8,128)(2,1)S(1)}, bf16[512,1024]{1,0:T(8,128)(2,1)S(1)}, u32[]{:S(2)}, u32[]{:S(2)}) collective-permute-start(bf16[512,1024]{1,0:T(8,128)(2,1)S(1)} %shard_map.65.own), channel_id=1, source_target_pairs={{16,0},{20,4},{8,24},{12,28},{17,1},{21,5},{9,25},{13,29},{18,2},{... | collective-permute-start | bytes 3145736 | tf_op jit(solution)/shard_map/ppermute | solution.py:337
  138.0 58.7 %collective-permute-start.7 = (bf16[512,1024]{1,0:T(8,128)(2,1)}, bf16[512,1024]{1,0:T(8,128)(2,1)}, u32[]{:S(2)}, u32[]{:S(2)}) collective-permute-start(bf16[512,1024]{1,0:T(8,128)(2,1)} %shard_map.66.refs_0_), channel_id=1, source_target_pairs={{0,16},{4,20},{24,8},{28,12},{1,17},{5,21},{25,9},{29,13},{2,18},{... | collective-permute-start | bytes 3145736 | tf_op jit(solution)/shard_map/ppermute | solution.py:355
  160.4 36.3 %collective-permute-start.8 = (bf16[512,1024]{1,0:T(8,128)(2,1)}, bf16[512,1024]{1,0:T(8,128)(2,1)}, u32[]{:S(2)}, u32[]{:S(2)}) collective-permute-start(bf16[512,1024]{1,0:T(8,128)(2,1)} %shard_map.67.refs_1_), channel_id=1, source_target_pairs={{0,16},{4,20},{24,8},{28,12},{1,17},{5,21},{25,9},{29,13},{2,18},{... | collective-permute-start | bytes 3145736 | tf_op jit(solution)/shard_map/ppermute | solution.py:355
  162.8 81.3 %collective-permute-start.11 = (bf16[1024,1024]{1,0:T(8,128)(2,1)}, bf16[1024,1024]{1,0:T(8,128)(2,1)}, u32[]{:S(2)}, u32[]{:S(2)}) collective-permute-start(bf16[1024,1024]{1,0:T(8,128)(2,1)} %get-tuple-element.45), channel_id=1, source_target_pairs={{0,2},{1,3},{2,0},{3,1},{4,6},{5,7},{6,4},{7,5},{8,10},{9,11},{10,... | collective-permute-start | bytes 6291464 | tf_op jit(solution)/shard_map/ppermute | solution.py:260
  185.1 26.8 %collective-permute-start.9 = (bf16[512,1024]{1,0:T(8,128)(2,1)S(1)}, bf16[512,1024]{1,0:T(8,128)(2,1)S(1)}, u32[]{:S(2)}, u32[]{:S(2)}) collective-permute-start(bf16[512,1024]{1,0:T(8,128)(2,1)S(1)} %shard_map.68.own), channel_id=1, source_target_pairs={{16,0},{20,4},{8,24},{12,28},{17,1},{21,5},{9,25},{13,29},{18,2},{... | collective-permute-start | bytes 3145736 | tf_op jit(solution)/shard_map/ppermute | solution.py:337
  207.6 125.8 %reduce-scatter.6.cloned.1.call-start = ((), (), s32[]{:S(2)}) async-start(), calls=%async_computation.6 | async-start | bytes 2621440 | tf_op jit(solution)/shard_map/reduce_scatter | solution.py:403
  216.6 24.2 %collective-permute-start.10 = (bf16[512,1024]{1,0:T(8,128)(2,1)S(1)}, bf16[512,1024]{1,0:T(8,128)(2,1)S(1)}, u32[]{:S(2)}, u32[]{:S(2)}) collective-permute-start(bf16[512,1024]{1,0:T(8,128)(2,1)S(1)} %broadcast_select_fusion), channel_id=1, source_target_pairs={{0,16},{4,20},{24,8},{28,12},{16,0},{20,4},{8,24},{12,28},{1,17},{... | collective-permute-start | bytes 3145736 | tf_op jit(solution)/shard_map/ppermute | solution.py:355
  262.5 120.3 %reduce-scatter.8.cloned.1.call-start = ((), (), s32[]{:S(2)}) async-start(), calls=%async_computation.7 | async-start | bytes 2621440 | tf_op jit(solution)/shard_map/reduce_scatter | solution.py:417
  263.7 24.9 %collective-permute-start.14 = (bf16[512,1024]{1,0:T(8,128)(2,1)S(1)}, bf16[512,1024]{1,0:T(8,128)(2,1)S(1)}, u32[]{:S(2)}, u32[]{:S(2)}) collective-permute-start(bf16[512,1024]{1,0:T(8,128)(2,1)S(1)} %copy-done.3), channel_id=1, source_target_pairs={{0,16},{4,20},{24,8},{28,12},{1,17},{5,21},{25,9},{29,13},{2,18},{... | collective-permute-start | bytes 3145736 | tf_op jit(solution)/shard_map/ppermute | solution.py:355
  310.4 23.0 %collective-permute-start.15 = (bf16[128,2048]{1,0:T(8,128)(2,1)S(1)}, bf16[128,2048]{1,0:T(8,128)(2,1)}, u32[]{:S(2)}, u32[]{:S(2)}) collective-permute-start(bf16[128,2048]{1,0:T(8,128)(2,1)S(1)} %get-tuple-element.47), channel_id=1, source_target_pairs={{0,4},{12,8},{1,5},{13,9},{2,6},{14,10},{3,7},{15,11},{16,20},{28,... | collective-permute-start | bytes 1572872 | tf_op jit(solution)/shard_map/ppermute | solution.py:214
  312.6 43.3 %collective-permute-start.19 = (bf16[128,2048]{1,0:T(8,128)(2,1)S(1)}, bf16[128,2048]{1,0:T(8,128)(2,1)}, u32[]{:S(2)}, u32[]{:S(2)}) collective-permute-start(bf16[128,2048]{1,0:T(8,128)(2,1)S(1)} %get-tuple-element.48), channel_id=1, source_target_pairs={{0,4},{12,8},{1,5},{13,9},{2,6},{14,10},{3,7},{15,11},{16,20},{28,... | collective-permute-start | bytes 1572872 | tf_op jit(solution)/shard_map/ppermute | solution.py:214
  335.4 22.5 %collective-permute-start.16 = (bf16[128,2048]{1,0:T(8,128)(2,1)}, bf16[128,2048]{1,0:T(8,128)(2,1)S(1)}, u32[]{:S(2)}, u32[]{:S(2)}) collective-permute-start(bf16[128,2048]{1,0:T(8,128)(2,1)} %add_convert_fusion.4), channel_id=1, source_target_pairs={{4,8},{8,4},{5,9},{9,5},{6,10},{10,6},{7,11},{11,7},{20,24},{24,20... | collective-permute-start | bytes 1572872 | tf_op jit(solution)/shard_map/ppermute | solution.py:225
  336.1 40.5 %collective-permute-start.18 = (bf16[128,2048]{1,0:T(8,128)(2,1)}, bf16[128,2048]{1,0:T(8,128)(2,1)S(1)}, u32[]{:S(2)}, u32[]{:S(2)}) collective-permute-start(bf16[128,2048]{1,0:T(8,128)(2,1)} %get-tuple-element.49), channel_id=1, source_target_pairs={{0,4},{12,8},{1,5},{13,9},{2,6},{14,10},{3,7},{15,11},{16,20},{28,... | collective-permute-start | bytes 1572872 | tf_op jit(solution)/shard_map/ppermute | solution.py:214
  357.1 19.6 %collective-permute-start.20 = (bf16[128,2048]{1,0:T(8,128)(2,1)S(1)}, bf16[128,2048]{1,0:T(8,128)(2,1)S(1)}, u32[]{:S(2)}, u32[]{:S(2)}) collective-permute-start(bf16[128,2048]{1,0:T(8,128)(2,1)S(1)} %add_convert_fusion.2), channel_id=1, source_target_pairs={{4,8},{8,4},{5,9},{9,5},{6,10},{10,6},{7,11},{11,7},{20,24},{24,20... | collective-permute-start | bytes 1572872 | tf_op jit(solution)/shard_map/ppermute | solution.py:225
  358.1 20.0 %collective-permute-start.17 = (bf16[128,2048]{1,0:T(8,128)(2,1)S(1)}, bf16[128,2048]{1,0:T(8,128)(2,1)S(1)}, u32[]{:S(2)}, u32[]{:S(2)}) collective-permute-start(bf16[128,2048]{1,0:T(8,128)(2,1)S(1)} %add_convert_fusion.3), channel_id=1, source_target_pairs={{4,0},{8,12},{5,1},{9,13},{6,2},{10,14},{7,3},{11,15},{20,16},{24,... | collective-permute-start | bytes 1572872 | tf_op jit(solution)/shard_map/ppermute | solution.py:238
  (14 other events, 92.2 us)
Sparse Core Ops, SparseCore 0:
  9.8 83.4 all-gather.2
  94.9 79.2 all-gather.4
  207.7 42.8 reduce-scatter.3
  262.6 43.5 reduce-scatter.5
  308.4 74.4 reduce-scatter.7
